TPU v7x, 32 devices: a whole 2x2x4 slice. The times are simulated.
32 devices in a mesh: ctx: 16 (over z, y, core), wa: 2 (over x).
Axes of the slice: x: 2, y: 2, z: 4, core: 2. Of those that a mesh axis runs over, the one named last changes fastest.
Arguments:
- tokens: bfloat16 [4, 4096, 768], P('wa', 'ctx'), may hold values from -6 to 6
- teacher: bfloat16 [4, 4096, 768], P('wa', 'ctx'), may hold values from -12 to 12
- lengths: int32 [4], P('wa'), may hold values from 1024 to 4096, as said below
- block_order: int32 [32], replicated, may hold values from 0 to 31, each once
- query_weight: bfloat16 [768, 768], P('wa'), may hold values from -0.21875 to 0.21875
- query_bias: bfloat16 [768], P('wa'), may hold values from -1.796875 to 1.796875
- key_weight: bfloat16 [768, 768], P('wa'), may hold values from -0.21875 to 0.21875
- value_weight: bfloat16 [768, 768], P('wa'), may hold values from -0.21875 to 0.21875
- value_bias: bfloat16 [768], P('wa'), may hold values from -0.059814453 to 0.059814453
- out_weight: bfloat16 [768, 768], P('wa'), may hold values from -12 to 12
- out_bias: bfloat16 [768], P('wa'), may hold values from -1.796875 to 1.796875
- gain_one: bfloat16 [768], P('wa'), may hold values from 0.5 to 1.5
- shift_one: bfloat16 [768], P('wa'), may hold values from -1.796875 to 1.796875
- inner_weight: bfloat16 [768, 3072], P('wa'), may hold values from -0.21875 to 0.21875
- inner_bias: bfloat16 [3072], P('wa'), may hold values from -1.796875 to 1.796875
- outer_weight: bfloat16 [3072, 768], P('wa'), may hold values from -0.109375 to 0.109375
- outer_bias: bfloat16 [768], P('wa'), may hold values from -1.796875 to 1.796875
- gain_two: bfloat16 [768], P('wa'), may hold values from 0.5 to 1.5
- shift_two: bfloat16 [768], P('wa'), may hold values from -1.796875 to 1.796875
Outputs:
- output: bfloat16 [4, 4096, 768], P('wa', 'ctx')
- tokens_grad: float32 [4, 4096, 768], P('wa', 'ctx')
- query_weight_grad: float32 [768, 768], P('wa')
- query_bias_grad: float32 [768], P('wa')
- key_weight_grad: float32 [768, 768], P('wa')
- value_weight_grad: float32 [768, 768], P('wa')
- value_bias_grad: float32 [768], P('wa')
- out_weight_grad: float32 [768, 768], P('wa')
- out_bias_grad: float32 [768], P('wa')
- gain_one_grad: float32 [768], P('wa')
- shift_one_grad: float32 [768], P('wa')
- inner_weight_grad: float32 [768, 3072], P('wa')
- inner_bias_grad: float32 [3072], P('wa')
- outer_weight_grad: float32 [3072, 768], P('wa')
- outer_bias_grad: float32 [768], P('wa')
- gain_two_grad: float32 [768], P('wa')
- shift_two_grad: float32 [768], P('wa')
- loss: float32 [], replicated
Inputs may be any that keep to these rules, and one draw needn't show every extreme that they name: `lengths`: one sequence of every draw fills all 4096 slots. `block_order`: every block number appears once.
All inputs are finite; a program needn't handle non-finite values.
Results may differ from a plain program's by a relative error of at most 0.017.
Values may be sent and summed in bfloat16 or wider, within the bound.
A program may use at most 384 MiB of HBM per device.

v0:
```python
import jax
import jax.numpy as jnp
from jax import lax
from jax.sharding import PartitionSpec as P

DH = 64


def project(left, right):
    return jnp.dot(left, right, preferred_element_type=jnp.float32)


def transposed(left, right):
    return lax.dot_general(
        left, right, (((0,), (0,)), ((), ())), preferred_element_type=jnp.float32
    )


def against(left, right):
    return lax.dot_general(
        left, right, (((1,), (1,)), ((), ())), preferred_element_type=jnp.float32
    )


def normalize(values):
    average = jnp.mean(values, -1, keepdims=True)
    centered = values - average
    spread = jnp.mean(centered * centered, -1, keepdims=True)
    inverse = lax.rsqrt(spread + 1e-06)
    return (centered * inverse, inverse)


def norm_back(upstream, normed, inverse):
    return inverse * (
        upstream
        - jnp.mean(upstream, -1, keepdims=True)
        - normed * jnp.mean(upstream * normed, -1, keepdims=True)
    )


def slot_usable(order, lengths, first_row, slot_total, block_len):
    slot_ids = first_row + jnp.arange(slot_total, dtype=jnp.int32)
    block_ids = slot_ids // block_len
    table = jnp.arange(order.shape[0], dtype=jnp.int32)
    dealt = jnp.sum(jnp.where(block_ids[:, None] == table[None, :], order[None, :], 0), axis=1)
    positions = dealt * block_len + slot_ids % block_len
    return positions[None, :] < lengths[:, None]


def each_shard(step, state_now, shard_part, shard_rows):
    pieces_count = shard_part[0].shape[1] // shard_rows
    stacked = tuple(
        (
            jnp.moveaxis(
                member.reshape(member.shape[0], pieces_count, shard_rows, member.shape[2]), 1, 0
            )
            for member in shard_part
        )
    )

    def advance(state_inner, indexed):
        position, members = indexed
        return (step(state_inner, members, position * shard_rows), None)

    result, _ = lax.scan(advance, state_now, (jnp.arange(pieces_count, dtype=jnp.int32), stacked))
    return result


def shards(
    tokens,
    teacher,
    lengths,
    block_order,
    query_weight,
    query_bias,
    key_weight,
    value_weight,
    value_bias,
    out_weight,
    out_bias,
    gain_one,
    shift_one,
    inner_weight,
    inner_bias,
    outer_weight,
    outer_bias,
    gain_two,
    shift_two,
):
    (
        full_query,
        full_key,
        full_value,
        full_out,
        full_inner,
        full_outer,
        bias_query,
        bias_value,
        bias_out,
        gain_first,
        shift_first,
        bias_inner,
        bias_outer,
        gain_second,
        shift_second,
    ) = (
        lax.all_gather(query_weight, "wa", axis=0, tiled=True),
        lax.all_gather(key_weight, "wa", axis=0, tiled=True),
        lax.all_gather(value_weight, "wa", axis=0, tiled=True),
        lax.all_gather(out_weight, "wa", axis=0, tiled=True),
        lax.all_gather(inner_weight, "wa", axis=0, tiled=True),
        lax.all_gather(outer_weight, "wa", axis=0, tiled=True),
        lax.all_gather(query_bias, "wa", axis=0, tiled=True),
        lax.all_gather(value_bias, "wa", axis=0, tiled=True),
        lax.all_gather(out_bias, "wa", axis=0, tiled=True),
        lax.all_gather(gain_one, "wa", axis=0, tiled=True),
        lax.all_gather(shift_one, "wa", axis=0, tiled=True),
        lax.all_gather(inner_bias, "wa", axis=0, tiled=True),
        lax.all_gather(outer_bias, "wa", axis=0, tiled=True),
        lax.all_gather(gain_two, "wa", axis=0, tiled=True),
        lax.all_gather(shift_two, "wa", axis=0, tiled=True),
    )
    seq_count, slot_count, width = tokens.shape
    head_count = width // DH
    scaling = DH ** (-0.5)
    block_len = slot_count // 2
    shaped = (seq_count, slot_count, width)
    heads_shape = (seq_count, slot_count, head_count, DH)
    flat_rows = tokens.reshape(-1, width)
    queries = (project(flat_rows, full_query) + bias_query.astype(jnp.float32)).astype(jnp.bfloat16)
    keys_own = project(flat_rows, full_key).astype(jnp.bfloat16)
    values_own = (project(flat_rows, full_value) + bias_value.astype(jnp.float32)).astype(
        jnp.bfloat16
    )
    query_heads = queries.reshape(heads_shape)
    key_heads_own = keys_own.reshape(heads_shape)
    value_heads_own = values_own.reshape(heads_shape)
    own_start = lax.axis_index("ctx") * slot_count
    own_usable = slot_usable(block_order, lengths, own_start, slot_count, block_len)

    def scores_for(query_part, key_part, usable):
        logits = (
            jnp.einsum("sqhd,skhd->shqk", query_part, key_part, preferred_element_type=jnp.float32)
            * scaling
        )
        return jnp.where(usable[:, None, None, :], logits, -1e30)

    def forward_step(state_now, shard_part, first_row):
        running, totals, gathered_sum = state_now
        key_part, value_part = shard_part
        key_count = key_part.shape[1]
        scores = scores_for(
            query_heads,
            key_part.reshape(seq_count, key_count, head_count, DH),
            slot_usable(block_order, lengths, first_row, key_count, block_len),
        )
        updated = jnp.maximum(running, jnp.max(scores, -1))
        fading = jnp.exp(running - updated)
        weights = jnp.exp(scores - updated[..., None])
        totals = totals * fading + jnp.sum(weights, -1)
        mixed = jnp.einsum(
            "shqk,skhd->sqhd",
            weights.astype(jnp.bfloat16),
            value_part.reshape(seq_count, key_count, head_count, DH),
            preferred_element_type=jnp.float32,
        )
        gathered_sum = gathered_sum * jnp.swapaxes(fading, 1, 2)[..., None] + mixed
        return (updated, totals, gathered_sum)

    stat_zeros = jnp.zeros((seq_count, head_count, slot_count), jnp.float32)
    head_zeros = jnp.zeros(heads_shape, jnp.float32)
    running, totals, gathered_sum = each_shard(
        forward_step,
        (stat_zeros - 1e29, stat_zeros, head_zeros),
        (
            lax.all_gather(keys_own.reshape(shaped), "ctx", axis=1, tiled=True),
            lax.all_gather(values_own.reshape(shaped), "ctx", axis=1, tiled=True),
        ),
        slot_count,
    )
    logsum = running + jnp.log(totals)
    attended = (gathered_sum / jnp.swapaxes(totals, 1, 2)[..., None]).reshape(-1, width)
    attended_low = attended.astype(jnp.bfloat16)
    gain_first_f = gain_first.astype(jnp.float32)
    gain_second_f = gain_second.astype(jnp.float32)
    first = (
        flat_rows.astype(jnp.float32)
        + project(attended_low, full_out)
        + bias_out.astype(jnp.float32)
    )
    normed_one, inverse_one = normalize(first)
    hidden_in = normed_one * gain_first_f + shift_first.astype(jnp.float32)
    hidden_low = hidden_in.astype(jnp.bfloat16)
    inner_act = project(hidden_low, full_inner) + bias_inner.astype(jnp.float32)
    activated = jax.nn.gelu(inner_act, approximate=False).astype(jnp.bfloat16)
    second = hidden_in + project(activated, full_outer) + bias_outer.astype(jnp.float32)
    normed_two, inverse_two = normalize(second)
    final_rows = normed_two * gain_second_f + shift_second.astype(jnp.float32)
    row_mask = own_usable.reshape(-1).astype(jnp.float32)
    residue = (final_rows - teacher.reshape(-1, width).astype(jnp.float32)) * row_mask[:, None]
    loss_total, count_total = lax.psum(
        (0.5 * jnp.sum(residue * residue), jnp.sum(row_mask)), ("ctx", "wa")
    )
    loss = 2.0 * loss_total / (count_total * width)
    gain_two_grad = jnp.sum(residue * normed_two, 0)
    shift_two_grad = jnp.sum(residue, 0)
    second_grad = norm_back(residue * gain_second_f, normed_two, inverse_two)
    outer_low = second_grad.astype(jnp.bfloat16)
    outer_bias_grad = jnp.sum(outer_low.astype(jnp.float32), 0)
    outer_weight_grad = transposed(activated, outer_low)
    _, gelu_pull = jax.vjp(lambda inner_in: jax.nn.gelu(inner_in, approximate=False), inner_act)
    (inner_float,) = gelu_pull(against(outer_low, full_outer))
    inner_low = inner_float.astype(jnp.bfloat16)
    inner_bias_grad = jnp.sum(inner_low.astype(jnp.float32), 0)
    inner_weight_grad = transposed(hidden_low, inner_low)
    hidden_grad = second_grad + against(inner_low, full_inner)
    gain_one_grad = jnp.sum(hidden_grad * normed_one, 0)
    shift_one_grad = jnp.sum(hidden_grad, 0)
    first_grad = norm_back(hidden_grad * gain_first_f, normed_one, inverse_one)
    branch_low = first_grad.astype(jnp.bfloat16)
    out_bias_grad = jnp.sum(branch_low.astype(jnp.float32), 0)
    out_weight_grad = transposed(attended_low, branch_low)
    attended_grad = against(branch_low, full_out).astype(jnp.bfloat16)
    grad_heads = attended_grad.reshape(heads_shape)
    row_delta = jnp.sum((attended_grad.astype(jnp.float32) * attended).reshape(heads_shape), -1)
    delta_heads = jnp.swapaxes(row_delta, 1, 2)

    def query_step(state_now, shard_part, first_row):
        key_part, value_part = shard_part
        key_count = key_part.shape[1]
        key_heads = key_part.reshape(seq_count, key_count, head_count, DH)
        value_heads = value_part.reshape(seq_count, key_count, head_count, DH)
        scores = scores_for(
            query_heads,
            key_heads,
            slot_usable(block_order, lengths, first_row, key_count, block_len),
        )
        probability = jnp.exp(scores - logsum[..., None])
        prob_grad = jnp.einsum(
            "sqhd,skhd->shqk", grad_heads, value_heads, preferred_element_type=jnp.float32
        )
        score_grad = (probability * (prob_grad - delta_heads[..., None])).astype(jnp.bfloat16)
        return (
            state_now
            + jnp.einsum(
                "shqk,skhd->sqhd", score_grad, key_heads, preferred_element_type=jnp.float32
            )
            * scaling
        )

    query_grad = each_shard(
        query_step,
        head_zeros,
        (
            lax.all_gather(keys_own.reshape(shaped), "ctx", axis=1, tiled=True),
            lax.all_gather(values_own.reshape(shaped), "ctx", axis=1, tiled=True),
        ),
        slot_count,
    )
    query_low = query_grad.reshape(-1, width).astype(jnp.bfloat16)
    all_logsum, all_delta = (
        lax.all_gather(
            jnp.swapaxes(logsum, 1, 2).astype(jnp.bfloat16), "ctx", axis=1, tiled=True
        ).astype(jnp.float32),
        lax.all_gather(row_delta.astype(jnp.bfloat16), "ctx", axis=1, tiled=True).astype(
            row_delta.dtype
        ),
    )

    def key_step(state_now, shard_part, first_row):
        key_acc, value_acc = state_now
        query_part, grad_part = shard_part
        query_count = query_part.shape[1]
        part_heads = query_part.reshape(seq_count, query_count, head_count, DH)
        grad_part_heads = grad_part.reshape(seq_count, query_count, head_count, DH)
        logsum_part = jnp.swapaxes(
            lax.dynamic_slice_in_dim(all_logsum, first_row, query_count, 1), 1, 2
        )
        delta_part = jnp.swapaxes(
            lax.dynamic_slice_in_dim(all_delta, first_row, query_count, 1), 1, 2
        )
        scores = scores_for(part_heads, key_heads_own, own_usable)
        probability = jnp.exp(scores - logsum_part[..., None])
        value_acc = value_acc + jnp.einsum(
            "shqk,sqhd->skhd",
            probability.astype(jnp.bfloat16),
            grad_part_heads,
            preferred_element_type=jnp.float32,
        )
        prob_grad = jnp.einsum(
            "sqhd,skhd->shqk", grad_part_heads, value_heads_own, preferred_element_type=jnp.float32
        )
        score_grad = (probability * (prob_grad - delta_part[..., None])).astype(jnp.bfloat16)
        key_acc = (
            key_acc
            + jnp.einsum(
                "shqk,sqhd->skhd", score_grad, part_heads, preferred_element_type=jnp.float32
            )
            * scaling
        )
        return (key_acc, value_acc)

    key_grad, value_grad = each_shard(
        key_step,
        (head_zeros, head_zeros),
        (
            lax.all_gather(queries.reshape(shaped), "ctx", axis=1, tiled=True),
            lax.all_gather(attended_grad.reshape(shaped), "ctx", axis=1, tiled=True),
        ),
        slot_count,
    )
    key_low = key_grad.reshape(-1, width).astype(jnp.bfloat16)
    value_low = value_grad.reshape(-1, width).astype(jnp.bfloat16)
    query_weight_grad = transposed(flat_rows, query_low)
    query_bias_grad = jnp.sum(query_low.astype(jnp.float32), 0)
    key_weight_grad = transposed(flat_rows, key_low)
    value_weight_grad = transposed(flat_rows, value_low)
    value_bias_grad = jnp.sum(value_low.astype(jnp.float32), 0)
    tokens_grad = (
        first_grad
        + against(query_low, full_query)
        + against(key_low, full_key)
        + against(value_low, full_value)
    )
    (
        query_weight_grad,
        query_bias_grad,
        key_weight_grad,
        value_weight_grad,
        value_bias_grad,
        out_weight_grad,
        out_bias_grad,
        gain_one_grad,
        shift_one_grad,
        inner_weight_grad,
        inner_bias_grad,
        outer_weight_grad,
        outer_bias_grad,
        gain_two_grad,
        shift_two_grad,
    ) = lax.psum(
        (
            query_weight_grad,
            query_bias_grad,
            key_weight_grad,
            value_weight_grad,
            value_bias_grad,
            out_weight_grad,
            out_bias_grad,
            gain_one_grad,
            shift_one_grad,
            inner_weight_grad,
            inner_bias_grad,
            outer_weight_grad,
            outer_bias_grad,
            gain_two_grad,
            shift_two_grad,
        ),
        "ctx",
    )
    (
        query_weight_grad,
        query_bias_grad,
        key_weight_grad,
        value_weight_grad,
        value_bias_grad,
        out_weight_grad,
        out_bias_grad,
        gain_one_grad,
        shift_one_grad,
        inner_weight_grad,
        inner_bias_grad,
        outer_weight_grad,
        outer_bias_grad,
        gain_two_grad,
        shift_two_grad,
    ) = (
        lax.psum_scatter(
            query_weight_grad.astype(jnp.bfloat16), "wa", scatter_dimension=0, tiled=True
        ).astype(jnp.float32),
        lax.psum_scatter(
            query_bias_grad.astype(jnp.bfloat16), "wa", scatter_dimension=0, tiled=True
        ).astype(jnp.float32),
        lax.psum_scatter(
            key_weight_grad.astype(jnp.bfloat16), "wa", scatter_dimension=0, tiled=True
        ).astype(jnp.float32),
        lax.psum_scatter(
            value_weight_grad.astype(jnp.bfloat16), "wa", scatter_dimension=0, tiled=True
        ).astype(jnp.float32),
        lax.psum_scatter(
            value_bias_grad.astype(jnp.bfloat16), "wa", scatter_dimension=0, tiled=True
        ).astype(jnp.float32),
        lax.psum_scatter(
            out_weight_grad.astype(jnp.bfloat16), "wa", scatter_dimension=0, tiled=True
        ).astype(jnp.float32),
        lax.psum_scatter(
            out_bias_grad.astype(jnp.bfloat16), "wa", scatter_dimension=0, tiled=True
        ).astype(jnp.float32),
        lax.psum_scatter(
            gain_one_grad.astype(jnp.bfloat16), "wa", scatter_dimension=0, tiled=True
        ).astype(jnp.float32),
        lax.psum_scatter(
            shift_one_grad.astype(jnp.bfloat16), "wa", scatter_dimension=0, tiled=True
        ).astype(jnp.float32),
        lax.psum_scatter(
            inner_weight_grad.astype(jnp.bfloat16), "wa", scatter_dimension=0, tiled=True
        ).astype(jnp.float32),
        lax.psum_scatter(
            inner_bias_grad.astype(jnp.bfloat16), "wa", scatter_dimension=0, tiled=True
        ).astype(jnp.float32),
        lax.psum_scatter(
            outer_weight_grad.astype(jnp.bfloat16), "wa", scatter_dimension=0, tiled=True
        ).astype(jnp.float32),
        lax.psum_scatter(
            outer_bias_grad.astype(jnp.bfloat16), "wa", scatter_dimension=0, tiled=True
        ).astype(jnp.float32),
        lax.psum_scatter(
            gain_two_grad.astype(jnp.bfloat16), "wa", scatter_dimension=0, tiled=True
        ).astype(jnp.float32),
        lax.psum_scatter(
            shift_two_grad.astype(jnp.bfloat16), "wa", scatter_dimension=0, tiled=True
        ).astype(jnp.float32),
    )
    return (
        final_rows.astype(jnp.bfloat16).reshape(shaped),
        tokens_grad.reshape(shaped),
        query_weight_grad,
        query_bias_grad,
        key_weight_grad,
        value_weight_grad,
        value_bias_grad,
        out_weight_grad,
        out_bias_grad,
        gain_one_grad,
        shift_one_grad,
        inner_weight_grad,
        inner_bias_grad,
        outer_weight_grad,
        outer_bias_grad,
        gain_two_grad,
        shift_two_grad,
        loss,
    )


def solution(mesh):
    placed = (
        P("wa", "ctx", None),
        P("wa", "ctx", None),
        P("wa"),
        P(),
        P("wa", None),
        P("wa"),
        P("wa", None),
        P("wa", None),
        P("wa"),
        P("wa", None),
        P("wa"),
        P("wa"),
        P("wa"),
        P("wa", None),
        P("wa"),
        P("wa", None),
        P("wa"),
        P("wa"),
        P("wa"),
    )
    return jax.shard_map(
        shards,
        mesh=mesh,
        in_specs=placed,
        out_specs=(
            P("wa", "ctx", None),
            P("wa", "ctx", None),
            P("wa", None),
            P("wa"),
            P("wa", None),
            P("wa", None),
            P("wa"),
            P("wa", None),
            P("wa"),
            P("wa"),
            P("wa"),
            P("wa", None),
            P("wa"),
            P("wa", None),
            P("wa"),
            P("wa"),
            P("wa"),
            P(),
        ),
        check_vma=False,
    )
```

profile of v0, /device:TPU:0, one launch (start us, length us, event | category | flops | bytes accessed | tf_op | source)
XLA Modules:
  0.0 2056.2 jit_solution(13002974719565323747)
XLA Ops:
  14.8 20.3 all-gather.26.cloned.1.call-done
  38.1 21.3 %all-gather.20.cloned.1.call-done = bf16[768,768]{1,0:T(8,128)(2,1)} async-done(((bf16[384,768]{1,0:T(8,128)(2,1)}), bf16[768,768]{1,0:T(8,128)(2,1)}) %all-gather.20.cloned.1.call-update) | async-done | bytes 1179664 | tf_op jit(solution)/shard_map/all_gather | solution.py:108
  116.9 70.6 %all-gather.28.cloned.1.call-done = bf16[2,4096,768]{2,1,0:T(8,128)(2,1)} async-done(((bf16[2,256,768]{2,1,0:T(8,128)(2,1)}), bf16[2,4096,768]{2,1,0:T(8,128)(2,1)}) %all-gather.28.cloned.1.call-update) | async-done | bytes 12582928 | tf_op jit(solution)/shard_map/all_gather | solution.py:177
  187.5 16.7 copy.101
  204.2 85.0 %all-gather.22.cloned.1.call-done = bf16[2,4096,768]{2,1,0:T(8,128)(2,1)} async-done(((bf16[2,256,768]{2,1,0:T(8,128)(2,1)}), bf16[2,4096,768]{2,1,0:T(8,128)(2,1)}) %all-gather.22.cloned.1.call-update) | async-done | bytes 12582928 | tf_op jit(solution)/shard_map/all_gather | solution.py:176
  289.2 16.7 copy.99
  305.9 212.8 %while.43 = (s32[]{:T(128)}, f32[2,12,256]{2,1,0:T(8,128)S(1)}, f32[2,12,256]{2,1,0:T(8,128)S(1)}, f32[2,256,12,64]{1,3,2,0:T(8,128)S(1)}, s32[16]{0:T(128)S(1)}...) while((s32[]{:T(128)}, f32[2,12,256]{2,1,0:T(8,128)S(1)}, ...), condition=%wide.region_4.5_spmd.clone, body=%wide.region_0.0_spmd.clone.sunk | while | flops 421203712 | bytes 53092688 | solution.py:65
  525.8 21.1 %multiply_convert_fusion.8 = (bf16[512,3072]{1,0:T(8,128)(2,1)}, f32[512,3072]{1,0:T(8,128)}, f32[512,3072]{1,0:T(8,128)}) fusion(f32[3072]{0:T(1024)S(1)} %bitcast.253, bf16[768,3072]{1,0:T(8,128)(2,1)} %all-gather.32.cloned.1.call-done, f32[512,768]{1,0:T(8,128)} %copy-done.10, f32[768]{0:T(1024)S(1)} %reshape.419, f32[768]{0:T(1024)S(1)} %reshape.418, ...), kind=kOutput, calls=%fused_computation.83 | convolution fusion | flops 2521694208 | bytes 22042624 | tf_op jit(solution)/shard_map/dot_general | solution.py:10
  564.1 20.4 convert_reduce_fusion
  584.6 7.4 fusion.68
  610.6 224.3 %while.44 = (s32[]{:T(128)}, f32[2,256,12,64]{1,3,2,0:T(8,128)}, bf16[16,2,256,768]{2,3,1,0:T(8,128)(2,1)}, s32[16]{0:T(128)S(1)}, s32[32]{0:T(128)S(1)}, /*inde...) while((s32[]{:T(128)}, f32[2,256,12,64]{1,3,2,0:T(8,128)}, ...), condition=%wide.region_17.18_spmd.clone, body=%wide.region_15.17_spmd.clone.sunk | while | flops 614629120 | bytes 22863164 | solution.py:65
  617.2 7.6 bitcast_add_fusion.9
  631.3 7.4 bitcast_add_fusion.9
  645.3 7.4 bitcast_add_fusion.9
  659.3 7.5 bitcast_add_fusion.9
  673.3 7.4 bitcast_add_fusion.9
  687.3 7.9 bitcast_add_fusion.9
  701.7 7.6 bitcast_add_fusion.9
  715.9 7.4 bitcast_add_fusion.9
  729.8 7.4 bitcast_add_fusion.9
  743.8 7.4 bitcast_add_fusion.9
  757.7 7.4 bitcast_add_fusion.9
  771.7 7.4 bitcast_add_fusion.9
  785.6 7.4 bitcast_add_fusion.9
  799.6 7.4 bitcast_add_fusion.9
  813.5 7.4 bitcast_add_fusion.9
  827.5 7.4 bitcast_add_fusion.9
  839.8 20.7 %all_gather.85 = bf16[2,4096,12]{1,0,2:T(2,128)(2,1)S(1)} all-gather(bf16[2,256,12]{1,0,2:T(2,128)(2,1)S(1)} %convert_element_type.279), channel_id=1, replica_groups=mesh['ctx'=16,'wa'=2] {'ctx'}, dimensions={1}, use_global_device_ids=true | all-gather | bytes 208896 | tf_op jit(solution)/shard_map/all_gather | solution.py:265
  861.4 18.1 all_gather.83
  880.3 339.0 %while.45 = (s32[]{:T(128)}, f32[2,256,12,64]{1,3,2,0:T(8,128)}, f32[2,256,12,64]{1,3,2,0:T(8,128)}, bf16[16,2,256,768]{3,2,0,1:T(8,128)(2,1)}, bf16[2,256,12,64...) while((s32[]{:T(128)}, f32[2,256,12,64]{1,3,2,0:T(8,128)}, ...), condition=%wide.region_19.20_spmd.clone, body=%wide.region_18.19_spmd.clone.sunk | while | flops 823001600 | bytes 39545608 | solution.py:65
  915.1 7.0 bitcast_add_fusion.10
  936.3 7.0 bitcast_add_fusion.10
  957.5 7.0 bitcast_add_fusion.10
  978.8 7.0 bitcast_add_fusion.10
  1000.0 7.0 bitcast_add_fusion.10
  1021.2 7.0 bitcast_add_fusion.10
  1042.4 7.0 bitcast_add_fusion.10
  1063.7 7.0 bitcast_add_fusion.10
  1106.1 7.0 bitcast_add_fusion.10
  1127.4 7.0 bitcast_add_fusion.10
  1169.8 7.0 bitcast_add_fusion.10
  1191.0 7.0 bitcast_add_fusion.10
  1227.8 580.2 %all-reduce.13 = (bf16[768,768]{0,1:T(8,128)(2,1)}, bf16[768,768]{0,1:T(8,128)(2,1)}, bf16[768,768]{0,1:T(8,128)(2,1)}, bf16[768]{0:T(1024)(128)(2,1)S(1)}, bf16...) all-reduce(f32[768,768]{0,1:T(8,128)S(1)} %copy-done.4, ...), channel_id=1, replica_groups=mesh['ctx'=16,'wa'=2] {'ctx'}, use_global_device_ids=true, to_apply=%region_20.21 | all-reduce | flops 7087104 | bytes 42522624 | tf_op jit(solution)/shard_map/psum | solution.py:341
  1819.0 52.2 %all-reduce.9 = (f32[]{:T(128)}, f32[]{:T(128)}) all-reduce(f32[]{:T(128)S(6)} %mul.295, f32[]{:T(128)} %fusion.56), channel_id=1, replica_groups=mesh['ctx'=16,'wa'=2] {'ctx','wa'}, use_global_device_ids=true, to_apply=%region_60.61 | all-reduce | flops 2 | bytes 16 | tf_op jit(solution)/shard_map/psum | solution.py:201
  1875.9 9.5 all-reduce.11
  1904.9 14.0 reduce-scatter.13.cloned.1.call-done
  1921.0 60.6 %reduce-scatter.15.cloned.1.call-done = bf16[384,3072]{1,0:T(8,128)(2,1)} async-done(((bf16[768,3072]{1,0:T(8,128)(2,1)}), bf16[384,3072]{1,0:T(8,128)(2,1)}) %reduce-scatter.15.cloned.1.call-update) | async-done | bytes 2359312 | tf_op jit(solution)/shard_map/reduce_scatter | solution.py:405
  1986.0 57.9 %reduce-scatter.17.cloned.1.call-done = bf16[1536,768]{1,0:T(8,128)(2,1)} async-done(((bf16[3072,768]{1,0:T(8,128)(2,1)}), bf16[1536,768]{1,0:T(8,128)(2,1)}) %reduce-scatter.17.cloned.1.call-update) | async-done | bytes 2359312 | tf_op jit(solution)/shard_map/reduce_scatter | solution.py:411
  (781 shorter events, 706.6 us)
Async XLA Ops:
  7.2 27.9 %copy-start.6 = (bf16[2,256,768]{2,1,0:T(8,128)(2,1)S(1)}, bf16[2,256,768]{2,1,0:T(8,128)(2,1)}, u32[]{:S(2)}) copy-start(bf16[2,256,768]{2,1,0:T(8,128)(2,1)} %param.25) | copy-start | bytes 2359300
  7.2 27.9 %all-gather.26.cloned.1.call-start = ((), (), s32[]{:S(2)}) async-start(), calls=%async_computation.9 | async-start | bytes 1769472 | tf_op jit(solution)/shard_map/all_gather | solution.py:109
  7.9 51.5 %all-gather.20.cloned.1.call-start = ((), (), s32[]{:S(2)}) async-start(), calls=%async_computation.6 | async-start | bytes 1769472 | tf_op jit(solution)/shard_map/all_gather | solution.py:108
  8.7 94.8 %all-gather.24.cloned.1.call-start = ((), (), s32[]{:S(2)}) async-start(), calls=%async_computation.8 | async-start | bytes 1769472 | tf_op jit(solution)/shard_map/all_gather | solution.py:107
  9.4 178.1 %all-gather.28.cloned.1.call-start = ((), (), s32[]{:S(2)}) async-start(), calls=%async_computation.10 | async-start | bytes 13369344 | tf_op jit(solution)/shard_map/all_gather | solution.py:177
  38.1 251.2 %all-gather.22.cloned.1.call-start = ((), (), s32[]{:S(2)}) async-start(), calls=%async_computation.7 | async-start | bytes 13369344 | tf_op jit(solution)/shard_map/all_gather | solution.py:176
  62.4 459.4 %all-gather.30.cloned.1.call-start = ((), (), s32[]{:S(2)}) async-start(), calls=%async_computation.11 | async-start | bytes 1769472 | tf_op jit(solution)/shard_map/all_gather | solution.py:110
  63.0 462.8 %all-gather.32.cloned.1.call-start = ((), (), s32[]{:S(2)}) async-start(), calls=%async_computation.12 | async-start | bytes 7077888 | tf_op jit(solution)/shard_map/all_gather | solution.py:111
  63.8 9.7 copy-start.35
  63.8 14.1 copy-start.36
  63.8 18.5 copy-start.31
  63.8 22.9 %copy-start.37 = (bf16[384]{0:T(512)(128)(2,1)S(1)}, bf16[384]{0:T(512)(128)(2,1)}, u32[]{:S(2)}) copy-start(bf16[384]{0:T(512)(128)(2,1)} %param.41) | copy-start | bytes 2308
  63.8 27.3 %copy-start.30 = (s32[32]{0:T(128)S(1)}, s32[32]{0:T(128)}, u32[]{:S(2)}) copy-start(s32[32]{0:T(128)} %param.28) | copy-start | bytes 388
  63.8 27.4 %copy-start.27 = (s32[2]{0:T(128)S(1)}, s32[2]{0:T(128)}, u32[]{:S(2)}) copy-start(s32[2]{0:T(128)} %param.27) | copy-start | bytes 28
  63.8 27.5 %copy-start.38 = (bf16[384]{0:T(512)(128)(2,1)S(1)}, bf16[384]{0:T(512)(128)(2,1)}, u32[]{:S(2)}) copy-start(bf16[384]{0:T(512)(128)(2,1)} %param.42) | copy-start | bytes 2308
  63.8 31.8 %copy-start.39 = (bf16[384]{0:T(512)(128)(2,1)S(1)}, bf16[384]{0:T(512)(128)(2,1)}, u32[]{:S(2)}) copy-start(bf16[384]{0:T(512)(128)(2,1)} %param.43) | copy-start | bytes 2308
  63.9 36.2 %copy-start.14 = (bf16[512,768]{1,0:T(8,128)(2,1)S(1)}, bf16[512,768]{1,0:T(8,128)(2,1)}, u32[]{:S(2)}) copy-start(bf16[512,768]{1,0:T(8,128)(2,1)} %add_convert_fusion.1) | copy-start | bytes 2359300
  63.9 483.0 %all-gather.34.cloned.1.call-start = ((), (), s32[]{:S(2)}) async-start(), calls=%async_computation.13 | async-start | bytes 7077888 | tf_op jit(solution)/shard_map/all_gather | solution.py:112
  64.6 815.7 %all-gather.36.cloned.1.call-start = ((), (), s32[]{:S(2)}) async-start(), calls=%async_computation.14 | async-start | bytes 13369344 | tf_op jit(solution)/shard_map/all_gather | solution.py:307
  91.2 12.3 copy-start.28
  116.6 763.7 %all-gather.38.cloned.1.call-start = ((), (), s32[]{:S(2)}) async-start(), calls=%async_computation.15 | async-start | bytes 13369344 | tf_op jit(solution)/shard_map/all_gather | solution.py:308
  485.1 5.6 copy-start
  557.2 6.9 slice-start.2
  559.1 32.9 %slice-start = ((s8[4718592]{0:T(1024)(128)(4,1)}), s8[4194304]{0:T(1024)(128)(4,1)S(1)}, s32[]{:S(2)}) async-start(s8[4718592]{0:T(1024)(128)(4,1)} %bitcast.256), calls=%async_computation.22 | async-start | bytes 8388608
  564.1 20.5 copy-start.11
  564.1 27.9 %slice-start.1 = ((s8[4718592]{0:T(1024)(128)(4,1)}), s8[524288]{0:T(1024)(128)(4,1)S(1)}, s32[]{:S(2)}) async-start(s8[4718592]{0:T(1024)(128)(4,1)} %bitcast.256), calls=%async_computation.23 | async-start | bytes 1048576
  584.6 7.4 copy-start.41
  600.8 8.2 copy-start.5
  610.6 1286.3 %reduce-scatter.19.cloned.1.call-start = ((), (), s32[]{:S(2)}) async-start(), calls=%async_computation.19 | async-start | bytes 1769472
  839.7 40.6 %copy-start.1 = (bf16[2,256,12,64]{1,3,2,0:T(8,128)(2,1)S(1)}, bf16[2,256,12,64]{1,3,2,0:T(8,128)(2,1)}, u32[]{:S(2)}) copy-start(bf16[2,256,12,64]{1,3,2,0:T(8,128)(2,1)} %copy.115) | copy-start | bytes 2359300
  839.7 40.6 %copy-start.29 = (s32[256]{0:T(256)S(1)}, s32[256]{0:T(256)}, u32[]{:S(2)}) copy-start(s32[256]{0:T(256)} %copy-done.28) | copy-start | bytes 3076
  909.5 5.6 copy-start.26
  951.9 5.6 copy-start.26
  973.2 5.6 copy-start.26
  994.4 5.6 copy-start.26
  1015.6 5.6 copy-start.26
  1036.8 5.6 copy-start.26
  1058.1 5.6 copy-start.26
  1079.3 5.6 copy-start.26
  1100.5 5.6 copy-start.26
  1121.8 5.6 copy-start.26
  1810.6 88.9 %reduce-scatter.21.cloned.1.call-start = ((), (), s32[]{:S(2)}) async-start(), calls=%async_computation.20 | async-start | bytes 1769472
  1812.1 90.0 %reduce-scatter.23.cloned.1.call-start = ((), (), s32[]{:S(2)}) async-start(), calls=%async_computation.21 | async-start | bytes 1769472
  1813.7 105.2 %reduce-scatter.13.cloned.1.call-start = ((), (), s32[]{:S(2)}) async-start(), calls=%async_computation.16 | async-start | bytes 1769472 | tf_op jit(solution)/shard_map/reduce_scatter | solution.py:393
  1814.2 167.4 %reduce-scatter.15.cloned.1.call-start = ((), (), s32[]{:S(2)}) async-start(), calls=%async_computation.17 | async-start | bytes 7077888 | tf_op jit(solution)/shard_map/reduce_scatter | solution.py:405
  1814.8 229.1 %reduce-scatter.17.cloned.1.call-start = ((), (), s32[]{:S(2)}) async-start(), calls=%async_computation.18 | async-start | bytes 7077888 | tf_op jit(solution)/shard_map/reduce_scatter | solution.py:411
  1815.1 57.4 %copy-start.17 = (bf16[96,8,2,256]{3,1,2,0:T(8,128)(2,1)S(1)}, bf16[96,8,2,256]{3,1,2,0:T(8,128)(2,1)}, u32[]{:S(2)}) copy-start(bf16[96,8,2,256]{3,1,2,0:T(8,128)(2,1)} %copy-done.16) | copy-start | bytes 2359300
  1872.5 18.7 copy-start.19
  (44 other events, 157.2 us)
Sparse Core Ops, SparseCore 0:
  9.6 25.4 all-gather.25
  36.6 22.7 all-gather.19
  61.0 22.9 all-gather.23
  86.7 100.7 all-gather.27
  190.2 98.9 all-gather.21
  290.6 20.9 all-gather.29
  313.1 62.6 all-gather.31
  377.4 62.6 all-gather.33
  442.9 100.7 all-gather.35
  610.7 100.3 all-gather.37
  1810.7 34.0 reduce-scatter.18
  1847.6 22.1 reduce-scatter.20
  1872.6 22.4 reduce-scatter.22
  1897.3 21.4 reduce-scatter.12
  1921.6 59.9 reduce-scatter.14
  1983.9 59.9 reduce-scatter.16
where the time goes:
time: 2070 us; the launch traced here: 2060 us
  blocking collectives  721 us (35%)
  matrix products  674 us (33%)
  waiting for transfers between devices  335 us (16%)
  local copies, waits for them, and re-layouts  213 us (10%)
  other arithmetic  59.3 us (3%)
  loops' own time  33.3 us (2%)
    psum x1, blocking collectives, shards(): lax.psum((query_weight_grad, query_bias_grad, key_weight_grad, value_weig...  580 us
    dot_general x48, matrix products, scores_for(): jnp.einsum('sqhd,skhd->shqk', query_part, key_part, preferred_element_typ...  184 us
    dot_general x16, matrix products, query_step(): jnp.einsum('shqk,skhd->sqhd', score_grad, key_heads, preferred_element_ty...  119 us
    dot_general x16, matrix products, key_step(): jnp.einsum('shqk,sqhd->skhd', score_grad, part_heads, preferred_element_t...  112 us
    dynamic_slice x128, local copies, waits for them, and re-layouts, each_shard(): lax.scan(advance, state_now, (jnp.arange(pieces_count, dtype=jnp.int32),...  108 us
    dot_general x16, matrix products, key_step(): jnp.einsum('shqk,sqhd->skhd', probability.astype(jnp.bfloat16), grad_part...  89 us
    all_gather x1, waiting for transfers between devices, shards(): lax.all_gather(keys_own.reshape(shaped), 'ctx', axis=1, tiled=True)  85 us
    dot_general x16, matrix products, forward_step(): jnp.einsum('shqk,skhd->sqhd', weights.astype(jnp.bfloat16), value_part.re...  75.8 us
  transfers between devices with their start and end apart: 16, of which 7 were waited for; matrix products, arithmetic and copies ran while one was open for 29% of the time, Pallas kernels for 0%

commit v1 on v0

v1 whole, which is shorter than its diff:
```python
import functools
import math

import jax
import jax.numpy as jnp
from jax import lax
from jax.experimental import pallas as pl
from jax.experimental.pallas import tpu as pltpu
from jax.sharding import PartitionSpec as P

DH = 64
BLK = 128
GROUPS = 4
LN2 = math.log(2.0)
NT = (((1,), (1,)), ((), ()))
NN = (((1,), (0,)), ((), ()))
TN = (((0,), (0,)), ((), ()))
F32 = jnp.float32
BF16 = jnp.bfloat16
VMEM = pl.BlockSpec(memory_space=pltpu.VMEM)
SMEM = pl.BlockSpec(memory_space=pltpu.SMEM)
ANY = pl.BlockSpec(memory_space=pl.ANY)
ROOM = pltpu.CompilerParams(vmem_limit_bytes=58 * 2**20)


def dot(left, right, dims=NN):
    return lax.dot_general(left, right, dims, preferred_element_type=F32)


def cost(us):
    return pl.CostEstimate(flops=int(us * 1.15e9), bytes_accessed=1 << 20, transcendentals=0)


def weight_copies(full, own, first, second, sems, base):
    x, c = lax.axis_index("wa"), lax.rem(lax.axis_index("ctx"), 2)
    half = own.shape[0]
    quarter = half // 2
    other = (1 - x) * half
    places = (
        (own, x * half, half),
        (first, other + c * quarter, quarter),
        (second, other + (1 - c) * quarter, quarter),
    )
    return [
        pltpu.make_async_copy(
            src, full.at[pl.ds(pl.multiple_of(start, quarter), size)], sems.at[base + i]
        )
        for i, (src, start, size) in enumerate(places)
    ]


def project_kernel(tok, vec, wq, wk, wv, first, second, *rest):
    seqs, rows, width = tok.shape
    outs, (full, sems) = rest[: 2 * seqs], rest[2 * seqs :]
    quarter = wq.shape[0] // 2
    copies = []
    for i, own in enumerate((wq, wk, wv)):
        part = pl.ds(i * quarter, quarter)
        copies.append(
            weight_copies(full.at[i], own, first.at[part], second.at[part], sems, 3 * i)
        )
    for group in copies:
        for copy in group:
            copy.start()
    flat = tok[...].reshape(seqs * rows, width)
    per = width // GROUPS
    heads = per // DH
    for copy in copies[1]:
        copy.wait()
    keys = dot(flat, full[1]).astype(BF16)
    for copy in copies[2]:
        copy.wait()
    values = (dot(flat, full[2]) + vec[1:2, :]).astype(BF16)
    for s in range(seqs):
        rs = slice(s * rows, (s + 1) * rows)
        for g in range(GROUPS):
            for h in range(heads):
                cols = slice(g * per + h * DH, g * per + (h + 1) * DH)
                outs[2 * s + 1][g, :, h * 128 : (h + 1) * 128] = jnp.concatenate(
                    [keys[rs, cols], values[rs, cols]], 1
                )
    for copy in copies[0]:
        copy.wait()
    queries = ((dot(flat, full[0]) + vec[0:1, :]) * (DH**-0.5 / LN2)).astype(BF16)
    for s in range(seqs):
        rs = slice(s * rows, (s + 1) * rows)
        for g in range(GROUPS):
            outs[2 * s][g] = queries[rs, g * per : (g + 1) * per]


def project(tok, vec, wq, wk, wv, first, second):
    seqs, rows, width = tok.shape
    per = width // GROUPS
    shapes = [
        jax.ShapeDtypeStruct((GROUPS, rows, n), BF16) for _ in range(seqs) for n in (per, 2 * per)
    ]
    return pl.pallas_call(
        project_kernel,
        out_shape=shapes,
        in_specs=[VMEM, VMEM] + [ANY] * 5,
        out_specs=[VMEM] * len(shapes),
        scratch_shapes=[pltpu.VMEM((3, width, width), BF16), pltpu.SemaphoreType.DMA((9,))],
        compiler_params=ROOM,
        cost_estimate=cost(5),
        name="project",
    )(tok, vec, wq, wk, wv, first, second)


def load_pieces(pieces, kv, sems):
    per = pieces[0].shape[0]
    copies = [
        pltpu.make_async_copy(piece, kv.at[pl.ds(i * per, per)], sems.at[i])
        for i, piece in enumerate(pieces)
    ]
    for copy in copies:
        copy.start()
    for copy in copies:
        copy.wait()


def forward_kernel(wide, narrow, count, sc, q_ref, *rest):
    pieces, (o_ref, lse_ref, kv_ref, qa, acc, sums, sems) = rest[:count], rest[count:]
    blocks = q_ref.shape[0]
    heads = q_ref.shape[2] // DH
    rows = blocks * BLK
    length = sc[0]
    load_pieces(pieces, kv_ref, sems)

    def gather(h, start, n):
        return jnp.concatenate(
            [kv_ref[sc[8 + blocks + start + i], :, h * 128 : (h + 1) * 128] for i in range(n)], 0
        )

    whole = length // (wide * BLK)
    tail = whole * wide
    tails = (length - tail * BLK + narrow * BLK - 1) // (narrow * BLK)
    for h in range(heads):
        hs = slice(h * DH, (h + 1) * DH)
        own = jnp.concatenate([q_ref[b, :, hs] for b in range(blocks)], 0)
        qa[...] = jnp.concatenate([own, jnp.zeros_like(own)], 1)
        acc[...] = jnp.zeros_like(acc)
        sums[...] = jnp.zeros_like(sums)

        def step(start, n, masked, h=h):
            kv = gather(h, start, n)
            scores = dot(qa[...], kv, NT)
            if masked:
                place = lax.broadcasted_iota(jnp.int32, scores.shape, 1) + start * BLK
                scores = jnp.where(place < length, scores, -1e30)
            p = jnp.exp2(scores)
            sums[...] += sum(p[:, i * 128 : (i + 1) * 128] for i in range(n))
            acc[...] += dot(p.astype(BF16), kv)

        def wide_step(j, _, step=step):
            step(j * wide, wide, False)
            return 0

        def narrow_step(j, _, step=step):
            step(tail + j * narrow, narrow, True)
            return 0

        lax.fori_loop(0, whole, wide_step, 0)
        lax.fori_loop(0, tails, narrow_step, 0)
        total = jnp.sum(sums[...], 1, keepdims=True)
        across = jnp.transpose(jnp.broadcast_to(total, (rows, 128)))[:8]
        good = (jnp.min(across) > 2.0**-80) & (jnp.max(across) < 2.0**100)

        @pl.when(good)
        def _(h=h, hs=hs, total=total, across=across):
            lse_ref[h] = jnp.log2(across)
            o_ref[:, hs] = (acc[:, DH:] * (1.0 / total)).astype(BF16)

        @pl.when(jnp.logical_not(good))
        def _(h=h, hs=hs):
            key_blocks = (length + BLK - 1) // BLK

            def rows_step(t, _):
                part = pl.ds(pl.multiple_of(t * BLK, BLK), BLK)
                q = qa[part, :]

                def scores_of(j):
                    kv = gather(h, j, 1)
                    scores = dot(q, kv, NT)
                    place = lax.broadcasted_iota(jnp.int32, scores.shape, 1) + j * BLK
                    return kv, jnp.where(place < length, scores, -1e30)

                largest = lax.fori_loop(
                    0,
                    key_blocks,
                    lambda j, m: jnp.maximum(m, jnp.max(scores_of(j)[1], 1, keepdims=True)),
                    jnp.full((BLK, 1), -1e30, F32),
                )
                acc[part, :] = jnp.zeros((BLK, 128), F32)
                sums[part, :] = jnp.zeros((BLK, 128), F32)

                def add(j, _):
                    kv, scores = scores_of(j)
                    p = jnp.exp2(scores - largest)
                    sums[part, :] += p
                    acc[part, :] += dot(p.astype(BF16), kv)
                    return 0

                lax.fori_loop(0, key_blocks, add, 0)
                row_total = jnp.sum(sums[part, :], 1, keepdims=True)
                lse = largest + jnp.log2(row_total)
                lse_ref[h, :, part] = jnp.transpose(jnp.broadcast_to(lse, (BLK, 128)))[:8]
                o_ref[part, hs] = (acc[part, :][:, DH:] * (1.0 / row_total)).astype(BF16)
                return 0

            lax.fori_loop(0, rows // BLK, rows_step, 0)


def attend(sc, q, pieces):
    blocks, _, per = q.shape
    rows, heads = blocks * BLK, per // DH
    key_blocks = len(pieces) * pieces[0].shape[0]
    return pl.pallas_call(
        functools.partial(forward_kernel, 8, 2, len(pieces)),
        out_shape=(
            jax.ShapeDtypeStruct((rows, per), BF16),
            jax.ShapeDtypeStruct((heads, 8, rows), F32),
        ),
        in_specs=[SMEM, VMEM] + [ANY] * len(pieces),
        out_specs=(VMEM, VMEM),
        scratch_shapes=[
            pltpu.VMEM((key_blocks, BLK, 2 * per), BF16),
            pltpu.VMEM((rows, 128), BF16),
            pltpu.VMEM((rows, 128), F32),
            pltpu.VMEM((rows, 128), F32),
            pltpu.SemaphoreType.DMA((len(pieces),)),
        ],
        compiler_params=ROOM,
        cost_estimate=cost(20),
        name="attend",
    )(sc, q, *pieces)


def backward_kernel(qn, kn, count, sc, q_ref, do_ref, o_ref, lse_ref, *rest):
    pieces, dq_ref, outs = rest[:count], rest[count], rest[count + 1 : 2 * count + 1]
    kv_ref, both, dkv, dq, lse_row, delta_row, sems = rest[2 * count + 1 :]
    blocks = q_ref.shape[0]
    heads = q_ref.shape[2] // DH
    key_blocks = kv_ref.shape[0]
    tile = qn * BLK
    length, used = sc[0], sc[1]
    whole = length // (kn * BLK)
    parts = (length + kn * BLK - 1) // (kn * BLK)
    tiles = (used + qn - 1) // qn
    ones = jnp.ones((8, DH), BF16)
    load_pieces(pieces, kv_ref, sems)
    for h in range(heads):
        hs = slice(h * DH, (h + 1) * DH)

        def clear(i, _):
            dkv[pl.ds(pl.multiple_of(i * 1024, 1024), 1024), :] = jnp.zeros((1024, 128), F32)
            return 0

        lax.fori_loop(0, key_blocks // 8, clear, 0)
        dq[...] = jnp.zeros_like(dq)

        def prepare(t, _, h=h, hs=hs):
            base = pl.multiple_of(t * (2 * tile), 2 * tile)
            start = pl.multiple_of(t * tile, tile)
            places = [sc[8 + t * qn + i] for i in range(qn)]
            q = jnp.concatenate([q_ref[s, :, hs] for s in places], 0)
            do = jnp.concatenate([do_ref[s, :, hs] for s in places], 0)
            o = jnp.concatenate([o_ref[s, :, hs] for s in places], 0)
            zero = jnp.zeros_like(q)
            both[pl.ds(base, tile), :] = jnp.concatenate([q, zero], 1)
            both[pl.ds(base + tile, tile), :] = jnp.concatenate([zero, do], 1)
            product = do.astype(F32) * o.astype(F32)
            high = product.astype(BF16)
            rest_of = (product - high.astype(F32)).astype(BF16)
            delta_row[:, pl.ds(start, tile)] = dot(ones, high, NT) + dot(ones, rest_of, NT)
            lse_row[:, pl.ds(start, tile)] = jnp.concatenate(
                [lse_ref[h, :, pl.ds(pl.multiple_of(s * BLK, BLK), BLK)] for s in places], 1
            )
            return 0

        lax.fori_loop(0, tiles, prepare, 0)

        def rows_step(t, _, h=h):
            base = pl.multiple_of(t * (2 * tile), 2 * tile)
            span = pl.ds(pl.multiple_of(t * tile, tile), tile)

            def step(j, masked):
                places = [sc[8 + blocks + j * kn + i] for i in range(kn)]
                kv = jnp.concatenate([kv_ref[s, :, h * 128 : (h + 1) * 128] for s in places], 0)
                b = both[pl.ds(base, 2 * tile), :]
                found = dot(kv, b, NT)
                p = jnp.exp2(found[:, :tile] - lse_row[:1, span])
                if masked:
                    place = lax.broadcasted_iota(jnp.int32, p.shape, 0) + j * (kn * BLK)
                    p = jnp.where(place < length, p, 0.0)
                ds = (p * (found[:, tile:] - delta_row[:1, span])).astype(BF16)
                grads = dot(jnp.concatenate([ds, p.astype(BF16)], 1), b)
                for i, s in enumerate(places):
                    dkv[pl.ds(pl.multiple_of(s * BLK, BLK), BLK), :] += grads[
                        i * BLK : (i + 1) * BLK
                    ]
                dq[span, :] += dot(ds, kv, TN)

            def whole_step(j, _):
                step(j, False)
                return 0

            lax.fori_loop(0, whole, whole_step, 0)

            @pl.when(parts > whole)
            def _():
                step(whole, True)

            return 0

        lax.fori_loop(0, tiles, rows_step, 0)
        for i in range(blocks):
            dq_ref[sc[8 + i], :, hs] = (
                dq[i * BLK : (i + 1) * BLK, :DH] * DH**-0.5
            ).astype(BF16)
        level = jnp.where(lax.broadcasted_iota(jnp.int32, (1, 128), 1) < DH, LN2, 1.0)
        per_piece = key_blocks // count
        for n, out in enumerate(outs):
            for i in range(per_piece):
                b = n * per_piece + i
                out[i, :, h * 128 : (h + 1) * 128] = (
                    dkv[b * BLK : (b + 1) * BLK, :] * level
                ).astype(BF16)


def attend_back(sc, q, do, o, lse, pieces):
    blocks, _, per = q.shape
    rows = blocks * BLK
    key_blocks = len(pieces) * pieces[0].shape[0]
    return pl.pallas_call(
        functools.partial(backward_kernel, 4, 4, len(pieces)),
        out_shape=[jax.ShapeDtypeStruct(q.shape, BF16)]
        + [jax.ShapeDtypeStruct(p.shape, BF16) for p in pieces],
        in_specs=[SMEM] + [VMEM] * 4 + [ANY] * len(pieces),
        out_specs=[VMEM] * (1 + len(pieces)),
        scratch_shapes=[
            pltpu.VMEM((key_blocks, BLK, 2 * per), BF16),
            pltpu.VMEM((2 * rows, 128), BF16),
            pltpu.VMEM((key_blocks * BLK, 128), F32),
            pltpu.VMEM((rows, 128), F32),
            pltpu.VMEM((8, rows), F32),
            pltpu.VMEM((8, rows), F32),
            pltpu.SemaphoreType.DMA((len(pieces),)),
        ],
        compiler_params=ROOM,
        cost_estimate=cost(45),
        name="attend_back",
    )(sc, q, do, o, lse, *pieces)


def norm(values):
    centered = values - jnp.mean(values, -1, keepdims=True)
    inverse = lax.rsqrt(jnp.mean(centered * centered, -1, keepdims=True) + 1e-6)
    return centered * inverse, inverse


def norm_back(upstream, normed, inverse):
    return inverse * (
        upstream
        - jnp.mean(upstream, -1, keepdims=True)
        - normed * jnp.mean(upstream * normed, -1, keepdims=True)
    )


def normal_parts(x):
    z = jnp.abs(x) * (0.5**0.5)
    bell = jnp.exp(-0.5 * x * x)
    t = 1.0 / (1.0 + 0.3275911 * z)
    poly = t * (
        0.254829592
        + t * (-0.284496736 + t * (1.421413741 + t * (-1.453152027 + t * 1.061405429)))
    )
    upper = 0.5 * poly * bell
    return jnp.where(x >= 0, 1.0 - upper, upper), bell * (2.0 * math.pi) ** -0.5


def dense_kernel(sc, att4, tok, teach, vec, wide_vec, *rest):
    weights, rest = rest[:9], rest[9:]
    outs, (wo, wi, wu, slope, sems) = rest[:11], rest[11:]
    out, fg, ag, att_o, br_o, hl_o, il_o, act_o, ol_o, sums, wide_sums = outs
    rows, width = tok.shape
    hidden = wi.shape[1]
    tile = 512
    copies = [
        weight_copies(full, *weights[3 * i : 3 * i + 3], sems, 3 * i)
        for i, full in enumerate((wo, wi, wu))
    ]
    for group in copies:
        for copy in group:
            copy.start()
    per = att4.shape[2]
    att = jnp.concatenate([att4[g] for g in range(GROUPS)], 1)
    att_o[...] = att
    row = lax.broadcasted_iota(jnp.int32, (rows, 1), 0)
    mask = jnp.where(
        row < BLK, jnp.where(row < sc[0], 1.0, 0.0), jnp.where(row - BLK < sc[1], 1.0, 0.0)
    )
    out_bias, gain_one, shift_one = vec[0:1, :], vec[1:2, :], vec[2:3, :]
    outer_bias, gain_two, shift_two = vec[3:4, :], vec[4:5, :], vec[5:6, :]
    for copy in copies[0]:
        copy.wait()
    first = tok[...].astype(F32) + dot(att, wo[...]) + out_bias
    normed_one, inverse_one = norm(first)
    hidden_in = normed_one * gain_one + shift_one
    hl = hidden_in.astype(BF16)
    hl_o[...] = hl
    for copy in copies[1] + copies[2]:
        copy.wait()
    second = hidden_in + outer_bias
    for n in range(hidden // tile):
        cols = slice(n * tile, (n + 1) * tile)
        inner = dot(hl, wi[:, cols]) + wide_vec[0:1, cols]
        below, density = normal_parts(inner)
        act = (inner * below).astype(BF16)
        act_o[:, cols] = act
        slope[:, cols] = below + inner * density
        second += dot(act, wu[cols, :])
    normed_two, inverse_two = norm(second)
    final = normed_two * gain_two + shift_two
    out[...] = final.astype(BF16)
    residue = (final - teach[...].astype(F32)) * mask
    add = functools.partial(jnp.sum, axis=0, keepdims=True)
    second_grad = norm_back(residue * gain_two, normed_two, inverse_two)
    ol = second_grad.astype(BF16)
    ol_o[...] = ol
    hidden_grad = second_grad
    for n in range(hidden // tile):
        cols = slice(n * tile, (n + 1) * tile)
        il = (dot(ol, wu[cols, :], NT) * slope[:, cols]).astype(BF16)
        il_o[:, cols] = il
        wide_sums[0:1, cols] = add(il.astype(F32))
        hidden_grad += dot(il, wi[:, cols], NT)
    first_grad = norm_back(hidden_grad * gain_one, normed_one, inverse_one)
    fg[...] = first_grad
    br = first_grad.astype(BF16)
    br_o[...] = br
    att_grad = dot(br, wo[...], NT).astype(BF16)
    for g in range(GROUPS):
        ag[g] = att_grad[:, g * per : (g + 1) * per]
    sums[0:1, :] = add(residue * normed_two)
    sums[1:2, :] = add(residue)
    sums[2:3, :] = add(ol.astype(F32))
    sums[3:4, :] = add(hidden_grad * normed_one)
    sums[4:5, :] = add(hidden_grad)
    sums[5:6, :] = add(br.astype(F32))
    sums[6:7, :] = add(residue * residue)
    sums[7:8, :] = jnp.zeros((1, width), F32)


def dense(sc, att4, tok, teach, vec, wide_vec, weights):
    rows, width = tok.shape
    hidden = wide_vec.shape[1]
    narrow = jax.ShapeDtypeStruct((rows, width), BF16)
    wide = jax.ShapeDtypeStruct((rows, hidden), BF16)
    return pl.pallas_call(
        dense_kernel,
        out_shape=[
            narrow,
            jax.ShapeDtypeStruct((rows, width), F32),
            jax.ShapeDtypeStruct(att4.shape, BF16),
            narrow,
            narrow,
            narrow,
            wide,
            wide,
            narrow,
            jax.ShapeDtypeStruct((8, width), F32),
            jax.ShapeDtypeStruct((1, hidden), F32),
        ],
        in_specs=[SMEM] + [VMEM] * 5 + [ANY] * 9,
        out_specs=[VMEM] * 11,
        scratch_shapes=[
            pltpu.VMEM((width, width), BF16),
            pltpu.VMEM((width, hidden), BF16),
            pltpu.VMEM((hidden, width), BF16),
            pltpu.VMEM((rows, hidden), F32),
            pltpu.SemaphoreType.DMA((9,)),
        ],
        compiler_params=ROOM,
        cost_estimate=cost(15),
        name="dense",
    )(sc, att4, tok, teach, vec, wide_vec, *weights)


def dense_grads_kernel(seqs, *refs):
    ins, (g_out, g_inner, g_outer) = refs[: 6 * seqs], refs[6 * seqs :]
    att, br, hl, il, act, ol = (
        jnp.concatenate([ins[6 * s + i][...] for s in range(seqs)], 0) for i in range(6)
    )
    for target, left, right in ((g_out, att, br), (g_inner, hl, il), (g_outer, act, ol)):
        rows = target.shape[1]
        for n in range(4):
            piece = left[:, n * rows : (n + 1) * rows]
            for t in range(right.shape[1] // 768):
                cols = slice(t * 768, (t + 1) * 768)
                target[n, :, cols] = dot(piece, right[:, cols], TN).astype(BF16)


def dense_grads(saved):
    seqs = len(saved)
    width, hidden = saved[0][0].shape[1], saved[0][3].shape[1]
    return pl.pallas_call(
        functools.partial(dense_grads_kernel, seqs),
        out_shape=[
            jax.ShapeDtypeStruct((4, width // 4, width), BF16),
            jax.ShapeDtypeStruct((4, width // 4, hidden), BF16),
            jax.ShapeDtypeStruct((4, hidden // 4, width), BF16),
        ],
        in_specs=[VMEM] * (6 * seqs),
        out_specs=[VMEM] * 3,
        compiler_params=ROOM,
        cost_estimate=cost(10),
        name="dense_grads",
    )(*[member for group in saved for member in group])


def project_grads_kernel(seqs, tok, *refs):
    fgs, refs = refs[:seqs], refs[seqs:]
    dqs, refs = refs[:seqs], refs[seqs:]
    dkvs, refs = refs[:seqs], refs[seqs:]
    wq, wk, wv, first, second, tg, grads, sums, full, sems = refs
    rows, width = tok.shape[1:]
    per = width // GROUPS
    heads = per // DH
    quarter = wq.shape[0] // 2
    copies = []
    for i, own in enumerate((wq, wk, wv)):
        part = pl.ds(i * quarter, quarter)
        copies += weight_copies(full.at[i], own, first.at[part], second.at[part], sems, 3 * i)
    for copy in copies:
        copy.start()
    dq = jnp.concatenate(
        [jnp.concatenate([dqs[s][g] for g in range(GROUPS)], 1) for s in range(seqs)], 0
    )
    pair = [
        jnp.concatenate([dkvs[s][g] for g in range(GROUPS)], 1) for s in range(seqs)
    ]
    pair = jnp.concatenate(pair, 0)
    halves = [
        jnp.concatenate(
            [
                pair[:, n * 128 + part * DH : n * 128 + (part + 1) * DH]
                for n in range(GROUPS * heads)
            ],
            1,
        )
        for part in (0, 1)
    ]
    flat = tok[...].reshape(seqs * rows, width)
    for copy in copies:
        copy.wait()
    total = jnp.concatenate([fgs[s][...] for s in range(seqs)], 0)
    for i, grad in enumerate((dq, *halves)):
        total += dot(grad, full[i], NT)
        found = dot(flat, grad, TN).astype(BF16)
        for n in range(4):
            grads[n, i * quarter : (i + 1) * quarter, :] = found[n * quarter : (n + 1) * quarter]
    tg[...] = total.reshape(seqs, rows, width)
    sums[0:1, :] = jnp.sum(dq.astype(F32), 0, keepdims=True)
    sums[1:2, :] = jnp.sum(halves[1].astype(F32), 0, keepdims=True)
    sums[2:8, :] = jnp.zeros((6, width), F32)


def project_grads(tok, fgs, dqs, dkvs, wq, wk, wv, first, second):
    seqs, rows, width = tok.shape
    return pl.pallas_call(
        functools.partial(project_grads_kernel, seqs),
        out_shape=[
            jax.ShapeDtypeStruct(tok.shape, F32),
            jax.ShapeDtypeStruct((4, 3 * (width // 4), width), BF16),
            jax.ShapeDtypeStruct((8, width), F32),
        ],
        in_specs=[VMEM] * (1 + 3 * seqs) + [ANY] * 5,
        out_specs=[VMEM] * 3,
        scratch_shapes=[pltpu.VMEM((3, width, width), BF16), pltpu.SemaphoreType.DMA((9,))],
        compiler_params=ROOM,
        cost_estimate=cost(10),
        name="project_grads",
    )(tok, *fgs, *dqs, *dkvs, wq, wk, wv, first, second)


def pick(table, index):
    places = jnp.arange(table.shape[0], dtype=jnp.int32)
    return jnp.sum(jnp.where(index[..., None] == places, table, 0), -1)


def shards(
    size,
    tokens,
    teacher,
    lengths,
    block_order,
    query_weight,
    query_bias,
    key_weight,
    value_weight,
    value_bias,
    out_weight,
    out_bias,
    gain_one,
    shift_one,
    inner_weight,
    inner_bias,
    outer_weight,
    outer_bias,
    gain_two,
    shift_two,
):
    seqs, rows, width = tokens.shape
    per_plane = size // GROUPS
    blocks_each = rows // BLK
    ctx, x = lax.axis_index("ctx"), lax.axis_index("wa")
    c, place = lax.rem(ctx, 2), lax.rem(ctx, per_plane)
    masks = [1 << b for b in reversed(range(per_plane.bit_length() - 1))]
    offsets = [0]
    for m in masks:
        offsets += [o ^ m for o in offsets]

    def across(value):
        return lax.ppermute(value, "wa", [(0, 1), (1, 0)])

    def flip(value, m):
        return lax.ppermute(value, "ctx", [(i, i ^ m) for i in range(size)])

    lines = [[g * per_plane + r for g in range(GROUPS)] for r in range(per_plane)]

    def turn(value):
        return lax.all_to_all(value, "ctx", 0, 0, axis_index_groups=lines)

    vectors = (
        query_bias,
        value_bias,
        out_bias,
        gain_one,
        shift_one,
        outer_bias,
        gain_two,
        shift_two,
        inner_bias,
    )
    own_vec = jnp.concatenate(vectors)[None]
    other_vec = across(own_vec)
    pair = jnp.where(
        x == 0, jnp.stack([own_vec, other_vec]), jnp.stack([other_vec, own_vec])
    ).astype(F32)
    half = width // 2
    narrow = pair[:, 0, : 8 * half].reshape(2, 8, half).swapaxes(0, 1).reshape(8, width)
    wide_vec = pair[:, 0, 8 * half :].reshape(1, -1)

    def quarter(weight):
        n = weight.shape[0] // 2
        return lax.dynamic_slice_in_dim(weight, c * n, n, 0)

    first_qkv = across(
        jnp.concatenate([quarter(w) for w in (query_weight, key_weight, value_weight)], 0)
    )
    second_qkv = flip(first_qkv, 1)
    dense_weights = []
    last = first_qkv
    for weight in (out_weight, inner_weight, outer_weight):
        piece, last = lax.optimization_barrier((quarter(weight), last))
        last = across(piece)
        dense_weights += [weight, last, flip(last, 1)]

    count = block_order.shape[0]
    ids = jnp.arange(count, dtype=jnp.int32)
    owner = ids // blocks_each
    index_of = jnp.array([offsets.index(o) for o in range(per_plane)], jnp.int32)
    piece_of = pick(index_of, (owner % per_plane) ^ place)
    spot = (piece_of * GROUPS + owner // per_plane) * blocks_each + ids % blocks_each
    key_order = jnp.sum(jnp.where(block_order[None, :] == ids[:, None], spot[None, :], 0), 1)
    near = jnp.arange(GROUPS * blocks_each, dtype=jnp.int32)
    near_ids = (near // blocks_each * per_plane + place) * blocks_each + near % blocks_each
    near_pos = pick(block_order, near_ids)
    rank = jnp.sum((near_pos[None, :] < near_pos[:, None]).astype(jnp.int32), 1)
    query_order = jnp.sum(jnp.where(rank[None, :] == near[:, None], near[None, :], 0), 1)
    own_pos = pick(block_order, ctx * blocks_each + jnp.arange(blocks_each, dtype=jnp.int32))
    scalars, row_counts = [], []
    for s in range(seqs):
        used = jnp.sum((near_pos * BLK < lengths[s]).astype(jnp.int32))
        head = jnp.concatenate([lengths[s][None], used[None], jnp.zeros((6,), jnp.int32)])
        scalars.append(jnp.concatenate([head, query_order, key_order]))
        row_counts.append(jnp.clip(lengths[s] - own_pos * BLK, 0, BLK))

    projected = project(
        tokens, narrow, query_weight, key_weight, value_weight, first_qkv, second_qkv
    )
    queries, pieces = [], []
    for s in range(seqs):
        kv = turn(projected[2 * s + 1])
        queries.append(turn(projected[2 * s]).reshape(-1, BLK, width // GROUPS))
        held = [kv.reshape(-1, BLK, kv.shape[2])]
        for m in masks:
            held += [flip(piece, m) for piece in held]
        pieces.append(held)

    attended, lses, dense_out = [], [], []
    for s in range(seqs):
        o, lse = attend(scalars[s], queries[s], pieces[s])
        attended.append(o.reshape(queries[s].shape))
        lses.append(lse)
    for s in range(seqs):
        o4 = turn(attended[s].reshape(GROUPS, rows, -1))
        dense_out.append(
            dense(
                row_counts[s], o4, tokens[s], teacher[s], narrow[2:], wide_vec, dense_weights
            )
        )
    saved = [d[3:9] for d in dense_out]
    heads_grad = [turn(d[2]).reshape(queries[s].shape) for s, d in enumerate(dense_out)]
    g_dense = dense_grads(saved)

    dqs, dkvs = [], []
    for s in range(seqs):
        found = attend_back(
            scalars[s], queries[s], heads_grad[s], attended[s], lses[s], pieces[s]
        )
        dqs.append(turn(found[0].reshape(GROUPS, rows, -1)))
        held = list(found[1:])
        for m in reversed(masks):
            n = len(held) // 2
            held = [
                (mine.astype(F32) + flip(theirs, m).astype(F32)).astype(BF16)
                for mine, theirs in zip(held[:n], held[n:])
            ]
        dkvs.append(turn(held[0].reshape(GROUPS, rows, -1)))
    tokens_grad, g_qkv, sums_qkv = project_grads(
        tokens,
        [d[1] for d in dense_out],
        dqs,
        dkvs,
        query_weight,
        key_weight,
        value_weight,
        first_qkv,
        second_qkv,
    )

    cores = [[i for i in range(size) if i % 2 == k] for k in range(2)]

    def reduced(grad):
        four = grad.reshape(2, 2, *grad.shape[1:])
        keep = lax.dynamic_index_in_dim(four, c, 1, False)
        send = lax.dynamic_index_in_dim(four, 1 - c, 1, False)
        keep = (keep.astype(F32) + flip(send, 1).astype(F32)).astype(BF16)
        mine = lax.dynamic_index_in_dim(keep, x, 0, False)
        theirs = across(lax.dynamic_index_in_dim(keep, 1 - x, 0, False))
        mine = (mine.astype(F32) + theirs.astype(F32)).astype(BF16)
        mine = lax.psum(mine, "ctx", axis_index_groups=cores)
        sibling = flip(mine, 1)
        return jnp.where(c == 0, jnp.stack([mine, sibling]), jnp.stack([sibling, mine]))

    out_grad, inner_grad, outer_grad = (
        reduced(g).reshape(-1, g.shape[2]).astype(F32) for g in g_dense
    )
    qkv = reduced(g_qkv).reshape(2, 3, width // 4, width).astype(F32)
    query_grad, key_grad, value_grad = (qkv[:, i].reshape(half, width) for i in range(3))

    sums = sum(d[9] for d in dense_out)
    wide_sums = sum(d[10] for d in dense_out)
    loss_part = jnp.sum(sums[6])
    valid = sum(jnp.sum(r) for r in row_counts).astype(F32)
    small = jnp.concatenate(
        [sums[:6].reshape(-1), sums_qkv[:2].reshape(-1), wide_sums[0], jnp.stack([loss_part, valid])]
    )
    small = lax.psum(small, ("ctx", "wa"))

    def vector(start, length):
        return lax.dynamic_slice_in_dim(small, start + x * (length // 2), length // 2, 0)

    end = 8 * width
    hidden = wide_vec.shape[1]
    loss = small[end + hidden] / (small[end + hidden + 1] * width)
    return (
        jnp.stack([d[0] for d in dense_out]),
        tokens_grad,
        query_grad,
        vector(6 * width, width),
        key_grad,
        value_grad,
        vector(7 * width, width),
        out_grad,
        vector(5 * width, width),
        vector(3 * width, width),
        vector(4 * width, width),
        inner_grad,
        vector(end, hidden),
        outer_grad,
        vector(2 * width, width),
        vector(0, width),
        vector(width, width),
        loss,
    )


def solution(mesh):
    row, split, both = P("wa"), P("wa", None), P("wa", "ctx", None)
    placed = (both, both, row, P(), split, row, split, split, row, split, row, row, row)
    placed += (split, row, split, row, row, row)
    return jax.shard_map(
        functools.partial(shards, mesh.shape["ctx"]),
        mesh=mesh,
        in_specs=placed,
        out_specs=(
            both,
            both,
            split,
            row,
            split,
            split,
            row,
            split,
            row,
            row,
            row,
            split,
            row,
            split,
            row,
            row,
            row,
            P(),
        ),
        check_vma=False,
    )
```

time: 2070 us -> 724 us (0.35)
  blocking collectives: 721 us -> 40.3 us
  matrix products: 674 us -> 0 us
  Pallas kernels: 0 us -> 157 us
  local copies, waits for them, and re-layouts: 213 us -> 67 us
  starting transfers between devices: 1.1 us -> 121 us
  waiting for transfers between devices: 335 us -> 261 us
  loops' own time: 33.3 us -> 0 us
    dot_general x130 -> x0, matrix products: 674 us -> none  [the longest x48 184 us: scores_for(): jnp.einsum('sqhd,skhd->shqk', query_part, key_part, preferred_element_typ...]
    psum x2 -> x1, blocking collectives: 632 us -> 40.3 us  [shards(): small = lax.psum(small, ('ctx', 'wa'))]
    all_gather x10 -> x0, waiting for transfers between devices: 197 us -> none  [the longest x1 85 us: shards(): lax.all_gather(keys_own.reshape(shaped), 'ctx', axis=1, tiled=True)]
    pallas_call x0 -> x9, Pallas kernels: none -> 157 us  [the longest x2 61 us: attend_back(): pl.pallas_call(functools.partial(backward_kernel, 4, 4, len(pieces)), out...]
    psum x0 -> x1, waiting for transfers between devices: none -> 139 us  [reduced(): mine = lax.psum(mine, 'ctx', axis_index_groups=cores)]
    reduce_scatter x3 -> x0, waiting for transfers between devices: 132 us -> none  [the longest x1 60.6 us: shards(): lax.psum_scatter(inner_weight_grad.astype(jnp.bfloat16), 'wa', scatter_di...]
    dynamic_slice x144 -> x7, local copies, waits for them, and re-layouts: 120 us -> 7.82 us  [the longest x5 4.91 us: quarter(): return lax.dynamic_slice_in_dim(weight, c * n, n, 0)]
    ppermute x0 -> x33, waiting for transfers between devices: none -> 90.6 us  [the longest x9 83.7 us: across(): return lax.ppermute(value, 'wa', [(0, 1), (1, 0)])]
  transfers between devices with their start and end apart: 16 -> 46, of which waited for: 7 -> 15; matrix products, arithmetic and copies ran while one was open for 29% -> 14% of each run, Pallas kernels for 0% -> 21%
where the time goes in v1:
time: 724 us; the launch traced here: 711 us
  waiting for transfers between devices  261 us (36%)
  Pallas kernels  157 us (22%)
  starting transfers between devices  121 us (17%)
  local copies, waits for them, and re-layouts  67 us (9%)
  other arithmetic  44.9 us (6%)
  blocking collectives  40.3 us (6%)
  between operations  19.1 us (3%)
    psum x1, waiting for transfers between devices, reduced(): mine = lax.psum(mine, 'ctx', axis_index_groups=cores)  139 us
    ppermute x9, waiting for transfers between devices, across(): return lax.ppermute(value, 'wa', [(0, 1), (1, 0)])  83.7 us
    pallas_call x2, Pallas kernels, attend_back(): pl.pallas_call(functools.partial(backward_kernel, 4, 4, len(pieces)), out...  61 us
    all_to_all x12, starting transfers between devices, turn(): return lax.all_to_all(value, 'ctx', 0, 0, axis_index_groups=lines)  55.7 us
    ppermute x9, starting transfers between devices, across(): return lax.ppermute(value, 'wa', [(0, 1), (1, 0)])  44.2 us
    psum x1, blocking collectives, shards(): small = lax.psum(small, ('ctx', 'wa'))  40.3 us
    pallas_call x2, Pallas kernels, attend(): pl.pallas_call(functools.partial(forward_kernel, 8, 2, len(pieces)), out_...  33.9 us
    pallas_call x2, Pallas kernels, dense(): pl.pallas_call(dense_kernel, out_shape=[narrow, jax.ShapeDtypeStruct((row...  33.6 us
  transfers between devices with their start and end apart: 46, of which 15 were waited for; matrix products, arithmetic and copies ran while one was open for 14% of the time, Pallas kernels for 21%

profile of v1, /device:TPU:0, one launch (start us, length us, event | category | flops | bytes accessed | tf_op | source)
XLA Modules:
  0.0 711.3 jit_solution(11049474918110684657)
XLA Ops:
  9.5 3.0 collective-permute-start.1
  12.5 19.6 %collective-permute-done.1.first.refs_9_ = bf16[576,768]{1,0:T(8,128)(2,1)S(1)} collective-permute-done((bf16[576,768]{1,0:T(8,128)(2,1)S(1)}, bf16[576,768]{1,0:T(8,128)(2,1)S(1)}, u32[]{:S(2)}, u32[]{:S(2)}) %collective-permute-start.1) | collective-permute-done | bytes 884768 | tf_op jit(solution)/shard_map/ppermute | solution.py:624
  39.4 6.6 project.1
  46.1 5.3 all-to-all-start.4
  55.3 5.1 collective-permute-done.6.rest_1_
  61.9 9.2 %all-to-all-done.4 = bf16[4,256,384]{2,1,0:T(8,128)(2,1)} async-done(((bf16[4,256,384]{2,1,0:T(8,128)(2,1)}), bf16[4,256,384]{2,1,0:T(8,128)(2,1)}, u32[]{:S(2)}, u32[]{:S(2)}) %all-to-all-start.4) | async-done | bytes 786464 | tf_op jit(solution)/shard_map/all_to_all | solution.py:632
  71.0 4.2 all-to-all-start.1
  76.8 2.5 fusion.20
  83.9 2.7 collective-permute-done.8.rest_4_
  88.0 6.9 all-to-all-done.1
  94.9 3.5 all-to-all-start
  109.5 3.6 all-to-all-start.3
  115.4 9.9 %all-to-all-done.3 = bf16[4,256,192]{1,2,0:T(8,128)(2,1)S(1)} async-done(((bf16[4,256,192]{1,2,0:T(8,128)(2,1)}), bf16[4,256,192]{1,2,0:T(8,128)(2,1)S(1)}, u32[]{:S(2)}, u32[]{:S(2)}) %all-to-all-start.3) | async-done | bytes 393248 | tf_op jit(solution)/shard_map/all_to_all | solution.py:632
  127.7 14.9 %attend.3 = (bf16[1024,192]{1,0:T(8,128)(2,1)}, f32[3,8,1024]{2,1,0:T(8,128)}) custom-call(s32[48]{0:T(128)} %concatenate.36.sc, bf16[8,128,192]{2,1,0:T(8,128)(2,1)} %bitcast.134, bf16[8,128,384]{2,1,0:T(8,128)(2,1)} %bitcast.15.rest_0_, bf16[8,128,384]{2,1,0:T(8,128)(2,1)} %collective-permute-done.12.rest_1_, ...), custom_call_target="tpu_custom_call" | custom-call | flops 23000000512 | bytes 1048576 | tf_op jit(solution)/shard_map/attend/pallas_call | solution.py:217
  144.6 3.5 all-to-all-start.5
  148.1 19.0 %attend.2 = (bf16[1024,192]{1,0:T(8,128)(2,1)}, f32[3,8,1024]{2,1,0:T(8,128)}) custom-call(s32[48]{0:T(128)} %concatenate.33.sc, bf16[8,128,192]{2,1,0:T(8,128)(2,1)} %bitcast.132, bf16[8,128,384]{2,1,0:T(8,128)(2,1)} %bitcast.6.rest_0_, bf16[8,128,384]{2,1,0:T(8,128)(2,1)} %copy-done.37, bf16[8,128,384]{2,1,0:T(8,128)(2,1)} %collective-permute-done.4.rest_2_, ...), custom_call_target="tpu_custom_call" | custom-call | flops 23000000512 | bytes 1048576 | tf_op jit(solution)/shard_map/attend/pallas_call | solution.py:217
  169.1 5.3 all-to-all-start.2
  176.9 16.8 %dense.3 = (bf16[256,768]{1,0:T(8,128)(2,1)}, f32[256,768]{1,0:T(8,128)}, bf16[4,256,192]{2,1,0:T(8,128)(2,1)}, bf16[256,768]{1,0:T(8,128)(2,1)}, bf16[256,768]{...) custom-call(s32[2]{0:T(128)} %get-tuple-element.144.sc, ...), custom_call_target="tpu_custom_call" | custom-call | flops 17250000896 | bytes 1048576 | tf_op jit(solution)/shard_map/dense/pallas_call | solution.py:459
  195.7 5.5 all-to-all-start.8
  202.2 16.8 %dense.2 = (bf16[256,768]{1,0:T(8,128)(2,1)}, f32[256,768]{1,0:T(8,128)}, bf16[4,256,192]{2,1,0:T(8,128)(2,1)}, bf16[256,768]{1,0:T(8,128)(2,1)}, bf16[256,768]{...) custom-call(s32[2]{0:T(128)} %get-tuple-element.125.sc, ...), custom_call_target="tpu_custom_call" | custom-call | flops 17250000896 | bytes 1048576 | tf_op jit(solution)/shard_map/dense/pallas_call | solution.py:459
  221.0 5.1 all-to-all-start.6
  227.1 17.4 %attend_back.3 = (bf16[8,128,192]{2,1,0:T(8,128)(2,1)}, bf16[8,128,384]{2,1,0:T(8,128)(2,1)}, bf16[8,128,384]{2,1,0:T(8,128)(2,1)}, bf16[8,128,384]{2,1,0:T(8,128)(2,1)}, bf16[8,128,384]{2,1,0:T(8,128)(2,1)}) custom-call(s32[48]{0:T(128)} %concatenate.36.sc, bf16[8,128,192]{2,1,0:T(8,128)(2,1)} %bitcast.135, bf16[8,128,192]{2,1,0:T(8,128)(2,1)} %bitcast.142, ...), custom_call_target="tpu_custom_call" | custom-call | flops 51749998592 | bytes 1048576 | tf_op jit(solution)/shard_map/attend_back/pallas_call | solution.py:334
  246.1 43.6 %attend_back.2 = (bf16[8,128,192]{2,1,0:T(8,128)(2,1)}, bf16[8,128,384]{2,1,0:T(8,128)(2,1)}, bf16[8,128,384]{2,1,0:T(8,128)(2,1)}, bf16[8,128,384]{2,1,0:T(8,128)(2,1)}, bf16[8,128,384]{2,1,0:T(8,128)(2,1)}) custom-call(s32[48]{0:T(128)} %concatenate.33.sc, bf16[8,128,192]{2,1,0:T(8,128)(2,1)} %bitcast.133, bf16[8,128,192]{2,1,0:T(8,128)(2,1)} %bitcast.143, ...), custom_call_target="tpu_custom_call" | custom-call | flops 51749998592 | bytes 1048576 | tf_op jit(solution)/shard_map/attend_back/pallas_call | solution.py:334
  292.0 5.1 all-to-all-start.9
  300.3 9.9 %collective-permute-start.20 = (bf16[8,128,384]{2,1,0:T(8,128)(2,1)}, bf16[8,128,384]{2,1,0:T(8,128)(2,1)}, u32[]{:S(2)}, u32[]{:S(2)}) collective-permute-start(bf16[8,128,384]{2,1,0:T(8,128)(2,1)} %add_convert_fusion.1), channel_id=1, source_target_pairs={{0,4},{2,6},{4,0},{6,2},{8,12},{10,14},{12,8},{14,10},{16,20},{18,... | collective-permute-start | bytes 2359304 | tf_op jit(solution)/shard_map/ppermute | solution.py:627
  312.2 5.4 all-to-all-start.7
  319.9 5.1 collective-permute-start.17
  325.0 3.8 collective-permute-done.20
  331.1 5.1 all-to-all-start.11
  336.3 11.8 %dense_grads.1 = (bf16[4,192,768]{2,1,0:T(8,128)(2,1)}, bf16[4,192,3072]{2,1,0:T(8,128)(2,1)}, bf16[4,768,768]{2,1,0:T(8,128)(2,1)}) custom-call(bf16[256,768]{1,0:T(8,128)(2,1)} %get-tuple-element.101.refs_0_, bf16[256,768]{1,0:T(8,128)(2,1)} %get-tuple-element.102.refs_1_, bf16[256,768]{1,0:T(8,128)(2,1)} %get-tuple-element.103.refs_2_, ...), custom_call_target="tpu_custom_call" | custom-call | flops 11500000256 | bytes 1048576 | tf_op jit(solution)/shard_map/dense_grads/pallas_call | solution.py:506
  350.4 4.0 all-to-all-done.11.refs_5_
  354.5 4.2 all-to-all-start.10
  364.4 3.0 collective-permute-done.24
  369.5 27.3 %collective-permute-start.25 = (bf16[192,768]{1,0:T(8,128)(2,1)}, bf16[192,768]{1,0:T(8,128)(2,1)}, u32[]{:S(2)}, u32[]{:S(2)}) collective-permute-start(bf16[192,768]{1,0:T(8,128)(2,1)} %dynamic-slice_bitcast_fusion.7), channel_id=1, source_target_pairs={{0,1},{1,0},{2,3},{3,2},{4,5},{5,4},{6,7},{7,6},{8,9},{9,8},{10,11... | collective-permute-start | bytes 884744 | tf_op jit(solution)/shard_map/ppermute | solution.py:624
  399.9 10.4 %project_grads.1 = (f32[2,256,768]{2,1,0:T(8,128)}, bf16[4,576,768]{2,1,0:T(8,128)(2,1)}, f32[8,768]{1,0:T(8,128)}) custom-call(bf16[2,256,768]{2,1,0:T(8,128)(2,1)} %tok.3, f32[256,768]{1,0:T(8,128)} %get-tuple-element.78.refs_0_, f32[256,768]{1,0:T(8,128)} %get-tuple-element.79.refs_1_, bf16[4,256,192]{2,1,0:T(8,128)(2,1)} %copy.79.refs_2_, ...), custom_call_target="tpu_custom_call" | custom-call | flops 11500000256 | bytes 1048576 | tf_op jit(solution)/shard_map/project_grads/pallas_call | solution.py:570
  410.3 3.0 dynamic-slice_bitcast_fusion.2
  413.3 3.0 fusion
  417.4 5.5 collective-permute-start.31
  422.9 2.6 fusion.1
  434.3 15.7 %collective-permute-done.31 = bf16[768,768]{1,0:T(8,128)(2,1)} collective-permute-done((bf16[768,768]{1,0:T(8,128)(2,1)}, bf16[768,768]{1,0:T(8,128)(2,1)}, u32[]{:S(2)}, u32[]{:S(2)}) %collective-permute-start.31) | collective-permute-done | bytes 1179680 | tf_op jit(solution)/shard_map/ppermute | solution.py:624
  450.0 2.6 fusion.3
  452.5 22.7 %collective-permute-done.28 = bf16[192,3072]{1,0:T(8,128)(2,1)} collective-permute-done((bf16[192,3072]{1,0:T(8,128)(2,1)}, bf16[192,3072]{1,0:T(8,128)(2,1)}, u32[]{:S(2)}, u32[]{:S(2)}) %collective-permute-start.28) | collective-permute-done | bytes 1179680 | tf_op jit(solution)/shard_map/ppermute | solution.py:624
  475.3 2.7 fusion.4
  478.0 15.9 %collective-permute-done.22 = bf16[576,768]{1,0:T(8,128)(2,1)S(1)} collective-permute-done((bf16[576,768]{1,0:T(8,128)(2,1)S(1)}, bf16[576,768]{1,0:T(8,128)(2,1)S(1)}, u32[]{:S(2)}, u32[]{:S(2)}) %collective-permute-start.22) | collective-permute-done | bytes 884768 | tf_op jit(solution)/shard_map/ppermute | solution.py:624
  495.1 139.1 %all-reduce.3.cloned.1.call-done = (bf16[576,768]{1,0:T(8,128)(2,1)}, bf16[192,768]{1,0:T(8,128)(2,1)}, bf16[192,3072]{1,0:T(8,128)(2,1)}, bf16[768,768]{1,0:T(8,128)(2,1)}) async-done(((bf16[576,768]{1,0:T(8,128)(2,1)}, bf16[192,768]{1,0:T(8,128)(2,1)}, bf16[192,3072]{1,0:T(8,128)(2,1)}, bf16[768,768]{1,0:T(8,128)(2,1)}), (bf16[576,768]{1,0:T(8,128)(2,1)}, bf16[192,768]{1,0:T(8,128)(2,1)}, ...) | async-done | bytes 3538960 | tf_op jit(solution)/shard_map/psum | solution.py:753
  644.5 40.3 %psum.36 = f32[9218]{0:T(1024)} all-reduce(f32[9218]{0:T(1024)} %concatenate.37), channel_id=1, replica_groups=mesh['ctx'=16,'wa'=2] {'ctx','wa'}, use_global_device_ids=true, to_apply=%region_12.13 | all-reduce | flops 9218 | bytes 73744 | tf_op jit(solution)/shard_map/psum | solution.py:770
  696.8 2.7 bitcast_convert_fusion
  699.9 2.9 bitcast_convert_fusion.1
  (240 shorter events, 108.6 us)
Async XLA Ops:
  9.5 22.7 %collective-permute-start.1 = (bf16[576,768]{1,0:T(8,128)(2,1)S(1)}, bf16[576,768]{1,0:T(8,128)(2,1)S(1)}, u32[]{:S(2)}, u32[]{:S(2)}) collective-permute-start(bf16[576,768]{1,0:T(8,128)(2,1)S(1)} %pad_maximum_fusion), channel_id=1, source_target_pairs={{0,1},{1,0},{2,3},{3,2},{4,5},{5,4},{6,7},{7,6},{8,9},{9,8},{10,11... | collective-permute-start | bytes 2654216 | tf_op jit(solution)/shard_map/ppermute | solution.py:624
  32.2 6.4 collective-permute-start.2
  34.0 3.8 collective-permute-start
  46.1 24.9 %all-to-all-start.4 = ((bf16[4,256,384]{2,1,0:T(8,128)(2,1)}), bf16[4,256,384]{2,1,0:T(8,128)(2,1)}, u32[]{:S(2)}, u32[]{:S(2)}) async-start(bf16[4,256,384]{2,1,0:T(8,128)(2,1)} %get-tuple-element.75), calls=%async_computation.4 | async-start | bytes 1572864 | tf_op jit(solution)/shard_map/all_to_all | solution.py:632
  52.4 8.0 %collective-permute-start.6 = (bf16[192,768]{1,0:T(8,128)(2,1)S(1)}, bf16[192,768]{1,0:T(8,128)(2,1)S(1)}, u32[]{:S(2)}, u32[]{:S(2)}) collective-permute-start(bf16[192,768]{1,0:T(8,128)(2,1)S(1)} %constant_dynamic-slice_fusion.2), channel_id=1, source_target_pairs={{0,1},{1,0},{2,3},{3,2},{4,5},{5,4},{6,7},{7,6},{8,9},{9,8},{10,11... | collective-permute-start | bytes 884744 | tf_op jit(solution)/shard_map/ppermute | solution.py:624
  60.4 26.2 %collective-permute-start.8 = (bf16[192,3072]{1,0:T(8,128)(2,1)S(1)}, bf16[192,3072]{1,0:T(8,128)(2,1)}, u32[]{:S(2)}, u32[]{:S(2)}) collective-permute-start(bf16[192,3072]{1,0:T(8,128)(2,1)S(1)} %constant_dynamic-slice_fusion.1), channel_id=1, source_target_pairs={{0,1},{1,0},{2,3},{3,2},{4,5},{5,4},{6,7},{7,6},{8,9},{9,8},{10,11... | collective-permute-start | bytes 3538952 | tf_op jit(solution)/shard_map/ppermute | solution.py:624
  71.0 23.9 %all-to-all-start.1 = ((bf16[4,256,384]{2,1,0:T(8,128)(2,1)}), bf16[4,256,384]{2,1,0:T(8,128)(2,1)}, u32[]{:S(2)}, u32[]{:S(2)}) async-start(bf16[4,256,384]{2,1,0:T(8,128)(2,1)} %get-tuple-element.68), calls=%async_computation.1 | async-start | bytes 1572864 | tf_op jit(solution)/shard_map/all_to_all | solution.py:632
  79.3 23.7 %collective-permute-start.12 = (bf16[8,128,384]{2,1,0:T(8,128)(2,1)}, bf16[8,128,384]{2,1,0:T(8,128)(2,1)}, u32[]{:S(2)}, u32[]{:S(2)}) collective-permute-start(bf16[8,128,384]{2,1,0:T(8,128)(2,1)} %bitcast.15.rest_0_), channel_id=1, source_target_pairs={{0,4},{2,6},{4,0},{6,2},{8,12},{10,14},{12,8},{14,10},{16,20},{18,... | collective-permute-start | bytes 2359304 | tf_op jit(solution)/shard_map/ppermute | solution.py:627
  86.6 39.7 %collective-permute-start.10 = (bf16[768,768]{1,0:T(8,128)(2,1)S(1)}, bf16[768,768]{1,0:T(8,128)(2,1)}, u32[]{:S(2)}, u32[]{:S(2)}) collective-permute-start(bf16[768,768]{1,0:T(8,128)(2,1)S(1)} %constant_dynamic-slice_fusion), channel_id=1, source_target_pairs={{0,1},{1,0},{2,3},{3,2},{4,5},{5,4},{6,7},{7,6},{8,9},{9,8},{10,11... | collective-permute-start | bytes 3538952 | tf_op jit(solution)/shard_map/ppermute | solution.py:624
  94.9 14.6 %all-to-all-start = ((bf16[4,256,192]{1,2,0:T(8,128)(2,1)}), bf16[4,256,192]{1,2,0:T(8,128)(2,1)S(1)}, u32[]{:S(2)}, u32[]{:S(2)}) async-start(bf16[4,256,192]{1,2,0:T(8,128)(2,1)} %copy.65), calls=%async_computation | async-start | bytes 786432 | tf_op jit(solution)/shard_map/all_to_all | solution.py:632
  101.5 25.7 %collective-permute-start.13 = (bf16[8,128,384]{2,1,0:T(8,128)(2,1)}, bf16[8,128,384]{2,1,0:T(8,128)(2,1)}, u32[]{:S(2)}, u32[]{:S(2)}) collective-permute-start(bf16[8,128,384]{2,1,0:T(8,128)(2,1)} %bitcast.15.rest_0_), channel_id=1, source_target_pairs={{0,2},{2,0},{4,6},{6,4},{8,10},{10,8},{12,14},{14,12},{16,18},{18,... | collective-permute-start | bytes 2359304 | tf_op jit(solution)/shard_map/ppermute | solution.py:627
  101.5 24.8 %collective-permute-start.3 = (bf16[8,128,384]{2,1,0:T(8,128)(2,1)}, bf16[8,128,384]{2,1,0:T(8,128)(2,1)S(1)}, u32[]{:S(2)}, u32[]{:S(2)}) collective-permute-start(bf16[8,128,384]{2,1,0:T(8,128)(2,1)} %bitcast.6.rest_0_), channel_id=1, source_target_pairs={{0,4},{2,6},{4,0},{6,2},{8,12},{10,14},{12,8},{14,10},{16,20},{18,... | collective-permute-start | bytes 2359304 | tf_op jit(solution)/shard_map/ppermute | solution.py:627
  103.0 24.7 %collective-permute-start.14 = (bf16[8,128,384]{2,1,0:T(8,128)(2,1)}, bf16[8,128,384]{2,1,0:T(8,128)(2,1)}, u32[]{:S(2)}, u32[]{:S(2)}) collective-permute-start(bf16[8,128,384]{2,1,0:T(8,128)(2,1)} %collective-permute-done.12.rest_1_), channel_id=1, source_target_pairs={{0,2},{2,0},{4,6},{6,4},{8,10},{10,8},{12,14},{14,12},{16,18},{18,... | collective-permute-start | bytes 2359304 | tf_op jit(solution)/shard_map/ppermute | solution.py:627
  109.5 15.8 %all-to-all-start.3 = ((bf16[4,256,192]{1,2,0:T(8,128)(2,1)}), bf16[4,256,192]{1,2,0:T(8,128)(2,1)S(1)}, u32[]{:S(2)}, u32[]{:S(2)}) async-start(bf16[4,256,192]{1,2,0:T(8,128)(2,1)} %copy.69), calls=%async_computation.3 | async-start | bytes 786432 | tf_op jit(solution)/shard_map/all_to_all | solution.py:632
  114.4 61.1 %collective-permute-start.7 = (bf16[192,768]{1,0:T(8,128)(2,1)S(1)}, bf16[192,768]{1,0:T(8,128)(2,1)}, u32[]{:S(2)}, u32[]{:S(2)}) collective-permute-start(bf16[192,768]{1,0:T(8,128)(2,1)S(1)} %collective-permute-done.6.rest_1_), channel_id=1, source_target_pairs={{0,2},{2,0},{4,6},{6,4},{8,10},{10,8},{12,14},{14,12},{16,18},{18,... | collective-permute-start | bytes 884744 | tf_op jit(solution)/shard_map/ppermute | solution.py:627
  126.3 49.2 %collective-permute-start.9 = (bf16[192,3072]{1,0:T(8,128)(2,1)}, bf16[192,3072]{1,0:T(8,128)(2,1)S(1)}, u32[]{:S(2)}, u32[]{:S(2)}) collective-permute-start(bf16[192,3072]{1,0:T(8,128)(2,1)} %collective-permute-done.8.rest_4_), channel_id=1, source_target_pairs={{0,2},{2,0},{4,6},{6,4},{8,10},{10,8},{12,14},{14,12},{16,18},{18,... | collective-permute-start | bytes 3538952 | tf_op jit(solution)/shard_map/ppermute | solution.py:627
  126.3 21.8 %collective-permute-start.4 = (bf16[8,128,384]{2,1,0:T(8,128)(2,1)}, bf16[8,128,384]{2,1,0:T(8,128)(2,1)}, u32[]{:S(2)}, u32[]{:S(2)}) collective-permute-start(bf16[8,128,384]{2,1,0:T(8,128)(2,1)} %bitcast.6.rest_0_), channel_id=1, source_target_pairs={{0,2},{2,0},{4,6},{6,4},{8,10},{10,8},{12,14},{14,12},{16,18},{18,... | collective-permute-start | bytes 2359304 | tf_op jit(solution)/shard_map/ppermute | solution.py:627
  127.2 48.3 %collective-permute-start.11 = (bf16[768,768]{1,0:T(8,128)(2,1)}, bf16[768,768]{1,0:T(8,128)(2,1)S(1)}, u32[]{:S(2)}, u32[]{:S(2)}) collective-permute-start(bf16[768,768]{1,0:T(8,128)(2,1)} %collective-permute-done.10.rest_7_), channel_id=1, source_target_pairs={{0,2},{2,0},{4,6},{6,4},{8,10},{10,8},{12,14},{14,12},{16,18},{18,... | collective-permute-start | bytes 3538952 | tf_op jit(solution)/shard_map/ppermute | solution.py:627
  127.7 20.4 %collective-permute-start.5 = (bf16[8,128,384]{2,1,0:T(8,128)(2,1)}, bf16[8,128,384]{2,1,0:T(8,128)(2,1)}, u32[]{:S(2)}, u32[]{:S(2)}) collective-permute-start(bf16[8,128,384]{2,1,0:T(8,128)(2,1)} %copy-done.37), channel_id=1, source_target_pairs={{0,2},{2,0},{4,6},{6,4},{8,10},{10,8},{12,14},{14,12},{16,18},{18,... | collective-permute-start | bytes 2359304 | tf_op jit(solution)/shard_map/ppermute | solution.py:627
  144.6 24.5 %all-to-all-start.5 = ((bf16[4,256,192]{1,2,0:T(8,128)(2,1)}), bf16[4,256,192]{1,2,0:T(8,128)(2,1)S(1)}, u32[]{:S(2)}, u32[]{:S(2)}) async-start(bf16[4,256,192]{1,2,0:T(8,128)(2,1)} %copy.71), calls=%async_computation.5 | async-start | bytes 786432 | tf_op jit(solution)/shard_map/all_to_all | solution.py:632
  169.1 26.6 %all-to-all-start.2 = ((bf16[4,256,192]{1,2,0:T(8,128)(2,1)}), bf16[4,256,192]{1,2,0:T(8,128)(2,1)S(1)}, u32[]{:S(2)}, u32[]{:S(2)}) async-start(bf16[4,256,192]{1,2,0:T(8,128)(2,1)} %copy.67), calls=%async_computation.2 | async-start | bytes 786432 | tf_op jit(solution)/shard_map/all_to_all | solution.py:632
  195.7 25.3 %all-to-all-start.8 = ((bf16[4,256,192]{1,2,0:T(8,128)(2,1)}), bf16[4,256,192]{1,2,0:T(8,128)(2,1)S(1)}, u32[]{:S(2)}, u32[]{:S(2)}) async-start(bf16[4,256,192]{1,2,0:T(8,128)(2,1)} %copy.76), calls=%async_computation.8 | async-start | bytes 786432 | tf_op jit(solution)/shard_map/all_to_all | solution.py:632
  221.0 24.1 %all-to-all-start.6 = ((bf16[4,256,192]{1,2,0:T(8,128)(2,1)}), bf16[4,256,192]{1,2,0:T(8,128)(2,1)S(1)}, u32[]{:S(2)}, u32[]{:S(2)}) async-start(bf16[4,256,192]{1,2,0:T(8,128)(2,1)} %copy.73), calls=%async_computation.6 | async-start | bytes 786432 | tf_op jit(solution)/shard_map/all_to_all | solution.py:632
  244.5 52.6 %collective-permute-start.19 = (bf16[8,128,384]{2,1,0:T(8,128)(2,1)}, bf16[8,128,384]{2,1,0:T(8,128)(2,1)S(1)}, u32[]{:S(2)}, u32[]{:S(2)}) collective-permute-start(bf16[8,128,384]{2,1,0:T(8,128)(2,1)} %get-tuple-element.93), channel_id=1, source_target_pairs={{0,2},{2,0},{4,6},{6,4},{8,10},{10,8},{12,14},{14,12},{16,18},{18,... | collective-permute-start | bytes 2359304 | tf_op jit(solution)/shard_map/ppermute | solution.py:627
  244.6 80.4 %collective-permute-start.18 = (bf16[8,128,384]{2,1,0:T(8,128)(2,1)}, bf16[8,128,384]{2,1,0:T(8,128)(2,1)S(1)}, u32[]{:S(2)}, u32[]{:S(2)}) collective-permute-start(bf16[8,128,384]{2,1,0:T(8,128)(2,1)} %get-tuple-element.91), channel_id=1, source_target_pairs={{0,2},{2,0},{4,6},{6,4},{8,10},{10,8},{12,14},{14,12},{16,18},{18,... | collective-permute-start | bytes 2359304 | tf_op jit(solution)/shard_map/ppermute | solution.py:627
  289.8 27.9 %collective-permute-start.16 = (bf16[8,128,384]{2,1,0:T(8,128)(2,1)}, bf16[8,128,384]{2,1,0:T(8,128)(2,1)}, u32[]{:S(2)}, u32[]{:S(2)}) collective-permute-start(bf16[8,128,384]{2,1,0:T(8,128)(2,1)} %get-tuple-element.89), channel_id=1, source_target_pairs={{0,2},{2,0},{4,6},{6,4},{8,10},{10,8},{12,14},{14,12},{16,18},{18,... | collective-permute-start | bytes 2359304 | tf_op jit(solution)/shard_map/ppermute | solution.py:627
  292.0 20.1 %all-to-all-start.9 = ((bf16[4,256,192]{1,2,0:T(8,128)(2,1)}), bf16[4,256,192]{1,2,0:T(8,128)(2,1)S(1)}, u32[]{:S(2)}, u32[]{:S(2)}) async-start(bf16[4,256,192]{1,2,0:T(8,128)(2,1)} %copy.78), calls=%async_computation.9 | async-start | bytes 786432 | tf_op jit(solution)/shard_map/all_to_all | solution.py:632
  300.3 28.6 %collective-permute-start.20 = (bf16[8,128,384]{2,1,0:T(8,128)(2,1)}, bf16[8,128,384]{2,1,0:T(8,128)(2,1)}, u32[]{:S(2)}, u32[]{:S(2)}) collective-permute-start(bf16[8,128,384]{2,1,0:T(8,128)(2,1)} %add_convert_fusion.1), channel_id=1, source_target_pairs={{0,4},{2,6},{4,0},{6,2},{8,12},{10,14},{12,8},{14,10},{16,20},{18,... | collective-permute-start | bytes 2359304 | tf_op jit(solution)/shard_map/ppermute | solution.py:627
  312.2 19.0 %all-to-all-start.7 = ((bf16[4,256,192]{1,2,0:T(8,128)(2,1)}), bf16[4,256,192]{1,2,0:T(8,128)(2,1)S(1)}, u32[]{:S(2)}, u32[]{:S(2)}) async-start(bf16[4,256,192]{1,2,0:T(8,128)(2,1)} %copy.75), calls=%async_computation.7 | async-start | bytes 786432 | tf_op jit(solution)/shard_map/all_to_all | solution.py:632
  317.6 30.5 %collective-permute-start.15 = (bf16[8,128,384]{2,1,0:T(8,128)(2,1)}, bf16[8,128,384]{2,1,0:T(8,128)(2,1)}, u32[]{:S(2)}, u32[]{:S(2)}) collective-permute-start(bf16[8,128,384]{2,1,0:T(8,128)(2,1)} %get-tuple-element.87), channel_id=1, source_target_pairs={{0,2},{2,0},{4,6},{6,4},{8,10},{10,8},{12,14},{14,12},{16,18},{18,... | collective-permute-start | bytes 2359304 | tf_op jit(solution)/shard_map/ppermute | solution.py:627
  319.9 28.2 %collective-permute-start.17 = (bf16[8,128,384]{2,1,0:T(8,128)(2,1)}, bf16[8,128,384]{2,1,0:T(8,128)(2,1)S(1)}, u32[]{:S(2)}, u32[]{:S(2)}) collective-permute-start(bf16[8,128,384]{2,1,0:T(8,128)(2,1)} %add_convert_fusion.4), channel_id=1, source_target_pairs={{0,4},{2,6},{4,0},{6,2},{8,12},{10,14},{12,8},{14,10},{16,20},{18,... | collective-permute-start | bytes 2359304 | tf_op jit(solution)/shard_map/ppermute | solution.py:627
  331.1 23.3 %all-to-all-start.11 = ((bf16[4,256,384]{2,1,0:T(8,128)(2,1)}), bf16[4,256,384]{2,1,0:T(8,128)(2,1)S(1)}, u32[]{:S(2)}, u32[]{:S(2)}) async-start(bf16[4,256,384]{2,1,0:T(8,128)(2,1)} %bitcast.27), calls=%async_computation.11 | async-start | bytes 1572864 | tf_op jit(solution)/shard_map/all_to_all | solution.py:632
  354.5 45.4 %all-to-all-start.10 = ((bf16[4,256,384]{2,1,0:T(8,128)(2,1)}), bf16[4,256,384]{2,1,0:T(8,128)(2,1)}, u32[]{:S(2)}, u32[]{:S(2)}) async-start(bf16[4,256,384]{2,1,0:T(8,128)(2,1)} %bitcast.26), calls=%async_computation.10 | async-start | bytes 1572864 | tf_op jit(solution)/shard_map/all_to_all | solution.py:632
  358.7 275.5 %all-reduce.3.cloned.1.call-start = ((), (), s32[]{:S(2)}) async-start(), calls=%async_computation.12 | async-start | bytes 7077888 | tf_op jit(solution)/shard_map/psum | solution.py:753
  361.0 52.3 %collective-permute-start.30 = (bf16[2,768,768]{2,1,0:T(8,128)(2,1)S(1)}, bf16[2,768,768]{2,1,0:T(8,128)(2,1)}, u32[]{:S(2)}, u32[]{:S(2)}) collective-permute-start(bf16[2,768,768]{2,1,0:T(8,128)(2,1)S(1)} %dynamic-slice_bitcast_fusion), channel_id=1, source_target_pairs={{0,2},{2,0},{4,6},{6,4},{8,10},{10,8},{12,14},{14,12},{16,18},{18,... | collective-permute-start | bytes 7077896 | tf_op jit(solution)/shard_map/ppermute | solution.py:627
  362.2 5.2 collective-permute-start.24
  364.3 58.5 %collective-permute-start.27 = (bf16[2,192,3072]{2,1,0:T(8,128)(2,1)}, bf16[2,192,3072]{2,1,0:T(8,128)(2,1)}, u32[]{:S(2)}, u32[]{:S(2)}) collective-permute-start(bf16[2,192,3072]{2,1,0:T(8,128)(2,1)} %dynamic-slice_bitcast_fusion.1), channel_id=1, source_target_pairs={{0,2},{2,0},{4,6},{6,4},{8,10},{10,8},{12,14},{14,12},{16,18},{18,... | collective-permute-start | bytes 7077896 | tf_op jit(solution)/shard_map/ppermute | solution.py:627
  369.5 58.4 %collective-permute-start.25 = (bf16[192,768]{1,0:T(8,128)(2,1)}, bf16[192,768]{1,0:T(8,128)(2,1)}, u32[]{:S(2)}, u32[]{:S(2)}) collective-permute-start(bf16[192,768]{1,0:T(8,128)(2,1)} %dynamic-slice_bitcast_fusion.7), channel_id=1, source_target_pairs={{0,1},{1,0},{2,3},{3,2},{4,5},{5,4},{6,7},{7,6},{8,9},{9,8},{10,11... | collective-permute-start | bytes 884744 | tf_op jit(solution)/shard_map/ppermute | solution.py:624
  413.3 16.4 %collective-permute-start.21 = (bf16[2,576,768]{2,1,0:T(8,128)(2,1)}, bf16[2,576,768]{2,1,0:T(8,128)(2,1)}, u32[]{:S(2)}, u32[]{:S(2)}) collective-permute-start(bf16[2,576,768]{2,1,0:T(8,128)(2,1)} %dynamic-slice_bitcast_fusion.2), channel_id=1, source_target_pairs={{0,2},{2,0},{4,6},{6,4},{8,10},{10,8},{12,14},{14,12},{16,18},{18,... | collective-permute-start | bytes 5308424 | tf_op jit(solution)/shard_map/ppermute | solution.py:627
  417.4 32.6 %collective-permute-start.31 = (bf16[768,768]{1,0:T(8,128)(2,1)}, bf16[768,768]{1,0:T(8,128)(2,1)}, u32[]{:S(2)}, u32[]{:S(2)}) collective-permute-start(bf16[768,768]{1,0:T(8,128)(2,1)} %dynamic-slice_bitcast_fusion.3), channel_id=1, source_target_pairs={{0,1},{1,0},{2,3},{3,2},{4,5},{5,4},{6,7},{7,6},{8,9},{9,8},{10,11... | collective-permute-start | bytes 3538952 | tf_op jit(solution)/shard_map/ppermute | solution.py:624
  427.9 47.3 %collective-permute-start.28 = (bf16[192,3072]{1,0:T(8,128)(2,1)}, bf16[192,3072]{1,0:T(8,128)(2,1)}, u32[]{:S(2)}, u32[]{:S(2)}) collective-permute-start(bf16[192,3072]{1,0:T(8,128)(2,1)} %dynamic-slice_bitcast_fusion.4), channel_id=1, source_target_pairs={{0,1},{1,0},{2,3},{3,2},{4,5},{5,4},{6,7},{7,6},{8,9},{9,8},{10,11... | collective-permute-start | bytes 3538952 | tf_op jit(solution)/shard_map/ppermute | solution.py:624
  432.2 61.7 %collective-permute-start.22 = (bf16[576,768]{1,0:T(8,128)(2,1)S(1)}, bf16[576,768]{1,0:T(8,128)(2,1)S(1)}, u32[]{:S(2)}, u32[]{:S(2)}) collective-permute-start(bf16[576,768]{1,0:T(8,128)(2,1)S(1)} %dynamic-slice_bitcast_fusion.5), channel_id=1, source_target_pairs={{0,1},{1,0},{2,3},{3,2},{4,5},{5,4},{6,7},{7,6},{8,9},{9,8},{10,11... | collective-permute-start | bytes 2654216 | tf_op jit(solution)/shard_map/ppermute | solution.py:624
  495.0 140.6 %copy-start.16 = (bf16[256,768]{1,0:T(8,128)(2,1)S(1)}, bf16[256,768]{1,0:T(8,128)(2,1)}, u32[]{:S(2)}) copy-start(bf16[256,768]{1,0:T(8,128)(2,1)} %get-tuple-element.77) | copy-start | bytes 1179652
  495.0 140.6 %copy-start.17 = (bf16[256,768]{1,0:T(8,128)(2,1)S(1)}, bf16[256,768]{1,0:T(8,128)(2,1)}, u32[]{:S(2)}) copy-start(bf16[256,768]{1,0:T(8,128)(2,1)} %get-tuple-element.73) | copy-start | bytes 1179652
  634.1 58.6 %collective-permute-start.23 = (bf16[576,768]{1,0:T(8,128)(2,1)}, bf16[576,768]{1,0:T(8,128)(2,1)}, u32[]{:S(2)}, u32[]{:S(2)}) collective-permute-start(bf16[576,768]{1,0:T(8,128)(2,1)} %get-tuple-element.118), channel_id=1, source_target_pairs={{0,2},{2,0},{4,6},{6,4},{8,10},{10,8},{12,14},{14,12},{16,18},{18,... | collective-permute-start | bytes 2654216 | tf_op jit(solution)/shard_map/ppermute | solution.py:627
  636.6 59.9 %collective-permute-start.32 = (bf16[768,768]{1,0:T(8,128)(2,1)}, bf16[768,768]{1,0:T(8,128)(2,1)S(1)}, u32[]{:S(2)}, u32[]{:S(2)}) collective-permute-start(bf16[768,768]{1,0:T(8,128)(2,1)} %get-tuple-element.121), channel_id=1, source_target_pairs={{0,2},{2,0},{4,6},{6,4},{8,10},{10,8},{12,14},{14,12},{16,18},{18,... | collective-permute-start | bytes 3538952 | tf_op jit(solution)/shard_map/ppermute | solution.py:627
  637.0 53.5 %collective-permute-start.26 = (bf16[192,768]{1,0:T(8,128)(2,1)}, bf16[192,768]{1,0:T(8,128)(2,1)}, u32[]{:S(2)}, u32[]{:S(2)}) collective-permute-start(bf16[192,768]{1,0:T(8,128)(2,1)} %get-tuple-element.119), channel_id=1, source_target_pairs={{0,2},{2,0},{4,6},{6,4},{8,10},{10,8},{12,14},{14,12},{16,18},{18,... | collective-permute-start | bytes 884744 | tf_op jit(solution)/shard_map/ppermute | solution.py:627
  690.4 9.2 %collective-permute-start.29 = (bf16[192,3072]{1,0:T(8,128)(2,1)S(1)}, bf16[192,3072]{1,0:T(8,128)(2,1)S(1)}, u32[]{:S(2)}, u32[]{:S(2)}) collective-permute-start(bf16[192,3072]{1,0:T(8,128)(2,1)S(1)} %copy-done.4), channel_id=1, source_target_pairs={{0,2},{2,0},{4,6},{6,4},{8,10},{10,8},{12,14},{14,12},{16,18},{18,... | collective-permute-start | bytes 3538952 | tf_op jit(solution)/shard_map/ppermute | solution.py:627
  (41 other events, 1002.9 us)
Sparse Core Ops, SparseCore 0:
  495.2 138.8 all-reduce.2

commit v2 on v1

--- a/solution.py
+++ b/solution.py
@@ -557,8 +557,12 @@
     for i, grad in enumerate((dq, *halves)):
         total += dot(grad, full[i], NT)
         found = dot(flat, grad, TN).astype(BF16)
-        for n in range(4):
-            grads[n, i * quarter : (i + 1) * quarter, :] = found[n * quarter : (n + 1) * quarter]
+        half = width // 2
+        for n in range(2):
+            for t in range(width // 128):
+                grads[t % 3, t // 3, n, i * half : (i + 1) * half, :] = found[
+                    n * half : (n + 1) * half, t * 128 : (t + 1) * 128
+                ]
     tg[...] = total.reshape(seqs, rows, width)
     sums[0:1, :] = jnp.sum(dq.astype(F32), 0, keepdims=True)
     sums[1:2, :] = jnp.sum(halves[1].astype(F32), 0, keepdims=True)
@@ -571,7 +575,7 @@
         functools.partial(project_grads_kernel, seqs),
         out_shape=[
             jax.ShapeDtypeStruct(tok.shape, F32),
-            jax.ShapeDtypeStruct((4, 3 * (width // 4), width), BF16),
+            jax.ShapeDtypeStruct((3, 2, 2, 3 * (width // 2), 128), BF16),
             jax.ShapeDtypeStruct((8, width), F32),
         ],
         in_specs=[VMEM] * (1 + 3 * seqs) + [ANY] * 5,
@@ -581,6 +585,263 @@
         cost_estimate=cost(10),
         name="project_grads",
     )(tok, *fgs, *dqs, *dkvs, wq, wk, wv, first, second)
+
+
+MESH = pl.DeviceIdType.MESH
+
+
+def position():
+    ctx = lax.axis_index("ctx")
+    return ctx // 4, lax.rem(ctx // 2, 2), lax.rem(ctx, 2), lax.axis_index("wa")
+
+
+def device(z, y, c, x):
+    return z * 4 + y * 2 + c, x
+
+
+def greet(others):
+    barrier = pltpu.get_barrier_semaphore()
+    for other in others:
+        pl.semaphore_signal(barrier, inc=1, device_id=other, device_id_type=MESH)
+    pl.semaphore_wait(barrier, len(others))
+
+
+def send(src, dst, sems, to):
+    copy = pltpu.make_async_remote_copy(
+        src_ref=src,
+        dst_ref=dst,
+        send_sem=sems[0],
+        recv_sem=sems[1],
+        device_id=to,
+        device_id_type=MESH,
+    )
+    copy.start()
+    return copy
+
+
+def add_low(left, right):
+    return (left.astype(F32) + right.astype(F32)).astype(BF16)
+
+
+def return_kernel(seqs, *refs):
+    ins, outs = refs[: 5 * seqs], refs[5 * seqs : 7 * seqs]
+    held, from_core, from_y, local_sem, q_sem, c_sem, y_sem, z_sem = refs[7 * seqs :]
+    z, y, c, x = position()
+    sibling, beside = device(z, y, 1 - c, x), device(z, 1 - y, c, x)
+    line = [None] + [device(z ^ d, y, c, x) for d in range(1, GROUPS)]
+    greet([sibling, beside] + line[1:])
+    waits = []
+    for s in range(seqs):
+        for d in range(1, GROUPS):
+            sems = q_sem.at[0, s, d], q_sem.at[1, s, d]
+            waits.append(send(ins[5 * s].at[z ^ d], outs[2 * s].at[z], sems, line[d]))
+    core = {}
+    for s in range(seqs):
+        for d in range(GROUPS):
+            for i in (1, 0):
+                sems = c_sem.at[0, s, d, i], c_sem.at[1, s, d, i]
+                core[s, d, i] = send(
+                    ins[5 * s + 3 + i].at[z ^ d], from_core.at[s, i, z ^ d], sems, sibling
+                )
+    local = {}
+    for s in range(seqs):
+        for i in (1, 0):
+            local[s, i] = pltpu.make_async_copy(
+                ins[5 * s + 1 + i], held.at[s, i], local_sem.at[s, i]
+            )
+            local[s, i].start()
+        own = pltpu.make_async_copy(ins[5 * s].at[z], outs[2 * s].at[z], local_sem.at[s, 2])
+        own.start()
+        waits.append(own)
+    order = [1, 2, 3, 0]
+    to_y = {}
+    for s in range(seqs):
+        local[s, 1].wait()
+        local[s, 0].wait()
+        for d in order:
+            core[s, d, 1].wait()
+            held[s, 1, z ^ d] = add_low(held[s, 1, z ^ d], from_core[s, 1, z ^ d])
+            sems = y_sem.at[0, s, d], y_sem.at[1, s, d]
+            to_y[s, d] = send(held.at[s, 1, z ^ d], from_y.at[s, z ^ d], sems, beside)
+            core[s, d, 0].wait()
+            held[s, 0, z ^ d] = add_low(held[s, 0, z ^ d], from_core[s, 0, z ^ d])
+    for s in range(seqs):
+        for d in order:
+            to_y[s, d].wait()
+            held[s, 0, z ^ d] = add_low(held[s, 0, z ^ d], from_y[s, z ^ d])
+            if d == 0:
+                own = pltpu.make_async_copy(
+                    held.at[s, 0, z], outs[2 * s + 1].at[z], local_sem.at[s, 3]
+                )
+                own.start()
+                waits.append(own)
+            else:
+                sems = z_sem.at[0, s, d], z_sem.at[1, s, d]
+                waits.append(send(held.at[s, 0, z ^ d], outs[2 * s + 1].at[z], sems, line[d]))
+    for copy in waits:
+        copy.wait()
+
+
+def return_grads(dqs, dkvs):
+    seqs = len(dqs)
+    groups, rows, per = dqs[0].shape
+    args, shapes = [], []
+    for dq, pieces in zip(dqs, dkvs):
+        args += [dq, *pieces]
+        shapes += [jax.ShapeDtypeStruct(dq.shape, BF16), jax.ShapeDtypeStruct(pieces[0].shape, BF16)]
+    dma = pltpu.SemaphoreType.DMA
+    slab = (groups, rows, 2 * per)
+    return pl.pallas_call(
+        functools.partial(return_kernel, seqs),
+        out_shape=shapes,
+        in_specs=[ANY] * len(args),
+        out_specs=[ANY] * len(shapes),
+        scratch_shapes=[
+            pltpu.VMEM((seqs, 2, *slab), BF16),
+            pltpu.VMEM((seqs, 2, *slab), BF16),
+            pltpu.VMEM((seqs, *slab), BF16),
+            dma((seqs, 4)),
+            dma((2, seqs, groups)),
+            dma((2, seqs, groups, 2)),
+            dma((2, seqs, groups)),
+            dma((2, seqs, groups)),
+        ],
+        compiler_params=pltpu.CompilerParams(
+            vmem_limit_bytes=40 * 2**20, collective_id=1, has_side_effects=True
+        ),
+        cost_estimate=cost(70),
+        name="return_grads",
+    )(*args)
+
+
+def sum_kernel(grads, small, out, small_out, *rest):
+    acc, from_core, from_x, from_y, from_z, res, vec, vec_in, sems, small_sems, last_sem = rest
+    z, y, c, x = position()
+    sibling, beside, over = device(z, y, 1 - c, x), device(z, 1 - y, c, x), device(z, y, c, 1 - x)
+    line = [None] + [device(z ^ d, y, c, x) for d in range(1, GROUPS)]
+    parts, rows = grads.shape[0], grads.shape[3]
+    half, piece = rows // 2, rows // 8
+    own_half = pl.ds(pl.multiple_of(y * half, half), half)
+    other_half = pl.ds(pl.multiple_of((1 - y) * half, half), half)
+
+    def piece_of(g):
+        return pl.ds(pl.multiple_of(y * half + g * piece, piece), piece)
+
+    greet([sibling, beside, over] + line[1:])
+
+    def pair(k, p):
+        return sems.at[0, k, p], sems.at[1, k, p]
+
+    def small_pair(k):
+        return small_sems.at[0, k], small_sems.at[1, k]
+
+    core = [
+        send(grads.at[p, 1 - c], from_core.at[p], pair(0, p), sibling) for p in range(parts)
+    ]
+    short = send(small, vec_in.at[0], small_pair(0), sibling)
+    flows = []
+    for p in range(parts):
+        core[p].wait()
+        acc[p] = add_low(grads[p, c], from_core[p])
+        if p == 1:
+            flows.append(send(acc.at[p, :, other_half], from_y.at[p], pair(1, p), beside))
+        else:
+            flows.append(send(acc.at[p, 1 - x], from_x.at[p], pair(1, p), over))
+    short.wait()
+    vec[...] = small[...] + vec_in[0]
+    short = send(vec, vec_in.at[1], small_pair(1), over)
+    for p in (1, 0, 2):
+        flows[p].wait()
+        if p == 1:
+            for k in range(2):
+                acc[p, k, own_half] = add_low(acc[p, k, own_half], from_y[p, k])
+            flows[p] = send(acc.at[p, 1 - x, own_half], from_x.at[p, own_half], pair(2, p), over)
+        else:
+            acc[p, x] = add_low(acc[p, x], from_x[p])
+            flows[p] = send(acc.at[p, x, other_half], from_y.at[p, 0], pair(2, p), beside)
+    short.wait()
+    vec[...] = vec[...] + vec_in[1]
+    short = send(vec, vec_in.at[2], small_pair(2), beside)
+    lines = {}
+    for p in (1, 0, 2):
+        flows[p].wait()
+        if p == 1:
+            acc[p, x, own_half] = add_low(acc[p, x, own_half], from_x[p, own_half])
+        else:
+            acc[p, x, own_half] = add_low(acc[p, x, own_half], from_y[p, 0])
+        for d in range(1, GROUPS):
+            lines[p, d] = send(
+                acc.at[p, x, piece_of(z ^ d)], from_z.at[p, d], pair(2 + d, p), line[d]
+            )
+    short.wait()
+    vec[...] = vec[...] + vec_in[2]
+    vec_in[4 + z] = vec[...]
+    shorts = [
+        send(vec, vec_in.at[4 + z], small_pair(2 + d), line[d]) for d in range(1, GROUPS)
+    ]
+    spread = {}
+    for p in (1, 0, 2):
+        total = acc[p, x, piece_of(z)].astype(F32)
+        for d in range(1, GROUPS):
+            lines[p, d].wait()
+            total += from_z[p, d].astype(F32)
+        res[c, p, piece_of(z)] = total.astype(BF16)
+        for d in range(1, GROUPS):
+            spread[p, d] = send(
+                res.at[c, p, piece_of(z)],
+                res.at[c, p, piece_of(z)],
+                pair(5 + d, p),
+                line[d],
+            )
+    for p in (1, 0, 2):
+        for d in range(1, GROUPS):
+            spread[p, d].wait()
+        flows[p] = send(
+            res.at[c, p, own_half], res.at[c, p, own_half], pair(9, p), beside
+        )
+    for copy in shorts:
+        copy.wait()
+    small_out[...] = vec_in[4] + vec_in[5] + (vec_in[6] + vec_in[7])
+    for p in (1, 0, 2):
+        flows[p].wait()
+        flows[p] = send(res.at[c, p], res.at[c, p], pair(10, p), sibling)
+    for p in (1, 0, 2):
+        flows[p].wait()
+    done = pltpu.make_async_copy(res, out, last_sem)
+    done.start()
+    done.wait()
+
+
+def sum_grads(grads, small):
+    parts, _, _, rows, lanes = grads.shape
+    dma = pltpu.SemaphoreType.DMA
+    return pl.pallas_call(
+        sum_kernel,
+        out_shape=[
+            jax.ShapeDtypeStruct((2, parts, rows, lanes), BF16),
+            jax.ShapeDtypeStruct(small.shape, F32),
+        ],
+        in_specs=[VMEM, VMEM],
+        out_specs=[ANY, VMEM],
+        scratch_shapes=[
+            pltpu.VMEM((parts, 2, rows, lanes), BF16),
+            pltpu.VMEM((parts, 2, rows, lanes), BF16),
+            pltpu.VMEM((parts, rows, lanes), BF16),
+            pltpu.VMEM((parts, 2, rows // 2, lanes), BF16),
+            pltpu.VMEM((parts, GROUPS, rows // 8, lanes), BF16),
+            pltpu.VMEM((2, parts, rows, lanes), BF16),
+            pltpu.VMEM(small.shape, F32),
+            pltpu.VMEM((8, *small.shape), F32),
+            dma((2, 11, parts)),
+            dma((2, 6)),
+            dma,
+        ],
+        compiler_params=pltpu.CompilerParams(
+            vmem_limit_bytes=40 * 2**20, collective_id=2, has_side_effects=True
+        ),
+        cost_estimate=cost(50),
+        name="sum_grads",
+    )(grads, small)
 
 
 def pick(table, index):
@@ -631,6 +892,31 @@
     def turn(value):
         return lax.all_to_all(value, "ctx", 0, 0, axis_index_groups=lines)
 
+    cores = [[i for i in range(size) if i % 2 == k] for k in range(2)]
+
+    def paired(mine):
+        sibling = flip(mine, 1)
+        return jnp.where(c == 0, jnp.stack([mine, sibling]), jnp.stack([sibling, mine]))
+
+    def reduced(grad):
+        four = grad.reshape(2, 2, *grad.shape[1:])
+        keep = lax.dynamic_index_in_dim(four, c, 1, False)
+        give = lax.dynamic_index_in_dim(four, 1 - c, 1, False)
+        keep = add_low(keep, flip(give, 1))
+        mine = lax.dynamic_index_in_dim(keep, x, 0, False)
+        mine = add_low(mine, across(lax.dynamic_index_in_dim(keep, 1 - x, 0, False)))
+        return paired(lax.psum(mine, "ctx", axis_index_groups=cores))
+
+    def reduced_dense(grad):
+        four = grad.reshape(2, 2, *grad.shape[1:])
+        keep = lax.dynamic_index_in_dim(four, c, 1, False)
+        give = lax.dynamic_index_in_dim(four, 1 - c, 1, False)
+        keep = add_low(keep, flip(give, 1))
+        mine = lax.psum_scatter(
+            keep.reshape(-1, keep.shape[-1]), "wa", scatter_dimension=0, tiled=True
+        )
+        return lax.psum(mine, "ctx", axis_index_groups=cores)
+
     vectors = (
         query_bias,
         value_bias,
@@ -714,20 +1000,26 @@
     heads_grad = [turn(d[2]).reshape(queries[s].shape) for s, d in enumerate(dense_out)]
     g_dense = dense_grads(saved)
 
+    dense_sums = [reduced_dense(g) for g in g_dense]
+    fused = per_plane == 4
     dqs, dkvs = [], []
     for s in range(seqs):
         found = attend_back(
             scalars[s], queries[s], heads_grad[s], attended[s], lses[s], pieces[s]
         )
-        dqs.append(turn(found[0].reshape(GROUPS, rows, -1)))
-        held = list(found[1:])
-        for m in reversed(masks):
-            n = len(held) // 2
-            held = [
-                (mine.astype(F32) + flip(theirs, m).astype(F32)).astype(BF16)
-                for mine, theirs in zip(held[:n], held[n:])
-            ]
-        dkvs.append(turn(held[0].reshape(GROUPS, rows, -1)))
+        dqs.append(found[0].reshape(GROUPS, rows, -1))
+        dkvs.append([piece.reshape(GROUPS, rows, -1) for piece in found[1:]])
+    if fused:
+        returned = return_grads(dqs, dkvs)
+        dqs, dkvs = returned[0::2], returned[1::2]
+    else:
+        for s in range(seqs):
+            dqs[s] = turn(dqs[s])
+            held = dkvs[s]
+            for m in reversed(masks):
+                n = len(held) // 2
+                held = [add_low(mine, flip(theirs, m)) for mine, theirs in zip(held[:n], held[n:])]
+            dkvs[s] = turn(held[0])
     tokens_grad, g_qkv, sums_qkv = project_grads(
         tokens,
         [d[1] for d in dense_out],
@@ -740,34 +1032,33 @@
         second_qkv,
     )
 
-    cores = [[i for i in range(size) if i % 2 == k] for k in range(2)]
-
-    def reduced(grad):
-        four = grad.reshape(2, 2, *grad.shape[1:])
-        keep = lax.dynamic_index_in_dim(four, c, 1, False)
-        send = lax.dynamic_index_in_dim(four, 1 - c, 1, False)
-        keep = (keep.astype(F32) + flip(send, 1).astype(F32)).astype(BF16)
-        mine = lax.dynamic_index_in_dim(keep, x, 0, False)
-        theirs = across(lax.dynamic_index_in_dim(keep, 1 - x, 0, False))
-        mine = (mine.astype(F32) + theirs.astype(F32)).astype(BF16)
-        mine = lax.psum(mine, "ctx", axis_index_groups=cores)
-        sibling = flip(mine, 1)
-        return jnp.where(c == 0, jnp.stack([mine, sibling]), jnp.stack([sibling, mine]))
-
-    out_grad, inner_grad, outer_grad = (
-        reduced(g).reshape(-1, g.shape[2]).astype(F32) for g in g_dense
-    )
-    qkv = reduced(g_qkv).reshape(2, 3, width // 4, width).astype(F32)
-    query_grad, key_grad, value_grad = (qkv[:, i].reshape(half, width) for i in range(3))
-
     sums = sum(d[9] for d in dense_out)
     wide_sums = sum(d[10] for d in dense_out)
     loss_part = jnp.sum(sums[6])
     valid = sum(jnp.sum(r) for r in row_counts).astype(F32)
     small = jnp.concatenate(
-        [sums[:6].reshape(-1), sums_qkv[:2].reshape(-1), wide_sums[0], jnp.stack([loss_part, valid])]
-    )
-    small = lax.psum(small, ("ctx", "wa"))
+        [
+            sums[:6].reshape(-1),
+            sums_qkv[:2].reshape(-1),
+            wide_sums[0],
+            jnp.stack([loss_part, valid]),
+        ]
+    )
+    small = jnp.pad(small, (0, -small.shape[0] % 1024)).reshape(-1, 128)
+    if fused:
+        qkv, small = sum_grads(g_qkv, small)
+    else:
+        small = lax.psum(small, ("ctx", "wa"))
+        qkv = reduced(jnp.moveaxis(g_qkv, (2, 1), (0, 1)).reshape(4, 3, -1, 128))
+    *dense_sums, small = lax.optimization_barrier((*dense_sums, small))
+    small = small.reshape(-1)
+    qkv = qkv.reshape(6, 3, half, 128).astype(F32)
+    query_grad, key_grad, value_grad = (
+        qkv[:, i].swapaxes(0, 1).reshape(half, width) for i in range(3)
+    )
+    out_grad, inner_grad, outer_grad = (
+        paired(g).reshape(-1, g.shape[-1]).astype(F32) for g in dense_sums
+    )
 
     def vector(start, length):
         return lax.dynamic_slice_in_dim(small, start + x * (length // 2), length // 2, 0)

time: 724 us -> 620 us (0.86)
  Pallas kernels: 157 us -> 317 us
  waiting for transfers between devices: 261 us -> 118 us
  starting transfers between devices: 121 us -> 52.4 us
  blocking collectives: 40.3 us -> 0 us
  other arithmetic: 44.9 us -> 28.4 us
  local copies, waits for them, and re-layouts: 67 us -> 74.6 us
    pallas_call x0 -> x2, Pallas kernels: none -> 133 us  [the longest x1 73.9 us: sum_grads(): pl.pallas_call(sum_kernel, out_shape=[jax.ShapeDtypeStruct((2, parts, row...]
    psum x1, waiting for transfers between devices: 139 us -> 62.3 us  [reduced_dense(): return lax.psum(mine, 'ctx', axis_index_groups=cores)]
    ppermute x9 -> x5, waiting for transfers between devices: 83.7 us -> 29.6 us  [across(): return lax.ppermute(value, 'wa', [(0, 1), (1, 0)])]
    psum x1 -> x0, blocking collectives: 40.3 us -> none  [shards(): small = lax.psum(small, ('ctx', 'wa'))]
    ppermute x9 -> x5, starting transfers between devices: 44.2 us -> 9.32 us  [across(): return lax.ppermute(value, 'wa', [(0, 1), (1, 0)])]
    unnamed x99 -> x117, local copies, waits for them, and re-layouts: 8.73 us -> 31.1 us
    pallas_call x2, Pallas kernels: 61 us -> 82.2 us  [attend_back(): pl.pallas_call(functools.partial(backward_kernel, 4, 4, len(pieces)), out...]
    all_to_all x12 -> x8, starting transfers between devices: 55.7 us -> 36.7 us  [turn(): return lax.all_to_all(value, 'ctx', 0, 0, axis_index_groups=lines)]
  transfers between devices with their start and end apart: 46 -> 33, of which waited for: 15 -> 8; matrix products, arithmetic and copies ran while one was open for 14% -> 13% of each run, Pallas kernels for 21% -> 51%
where the time goes in v2:
time: 620 us; the launch traced here: 608 us
  Pallas kernels  317 us (51%)
  waiting for transfers between devices  118 us (19%)
  local copies, waits for them, and re-layouts  74.6 us (12%)
  starting transfers between devices  52.4 us (8%)
  other arithmetic  28.4 us (5%)
  between operations  18.5 us (3%)
    pallas_call x2, Pallas kernels, attend_back(): pl.pallas_call(functools.partial(backward_kernel, 4, 4, len(pieces)), out...  82.2 us
    pallas_call x1, Pallas kernels, sum_grads(): pl.pallas_call(sum_kernel, out_shape=[jax.ShapeDtypeStruct((2, parts, row...  73.9 us
    psum x1, waiting for transfers between devices, reduced_dense(): return lax.psum(mine, 'ctx', axis_index_groups=cores)  62.3 us
    pallas_call x1, Pallas kernels, return_grads(): pl.pallas_call(functools.partial(return_kernel, seqs), out_shape=shapes,...  58.8 us
    pallas_call x2, Pallas kernels, attend(): pl.pallas_call(functools.partial(forward_kernel, 8, 2, len(pieces)), out_...  39.3 us
    all_to_all x8, starting transfers between devices, turn(): return lax.all_to_all(value, 'ctx', 0, 0, axis_index_groups=lines)  36.7 us
    pallas_call x2, Pallas kernels, dense(): pl.pallas_call(dense_kernel, out_shape=[narrow, jax.ShapeDtypeStruct((row...  33.6 us
    unnamed x117, local copies, waits for them, and re-layouts  31.1 us
  transfers between devices with their start and end apart: 33, of which 8 were waited for; matrix products, arithmetic and copies ran while one was open for 13% of the time, Pallas kernels for 51%

profile of v2, /device:TPU:0, one launch (start us, length us, event | category | flops | bytes accessed | tf_op | source)
XLA Modules:
  0.0 608.4 jit_solution(15533108710412102354)
XLA Ops:
  9.5 3.0 collective-permute-start.1
  12.5 19.6 %collective-permute-done.1.first.refs_9_ = bf16[576,768]{1,0:T(8,128)(2,1)S(1)} collective-permute-done((bf16[576,768]{1,0:T(8,128)(2,1)S(1)}, bf16[576,768]{1,0:T(8,128)(2,1)S(1)}, u32[]{:S(2)}, u32[]{:S(2)}) %collective-permute-start.1) | collective-permute-done | bytes 884768 | tf_op jit(solution)/shard_map/ppermute | solution.py:885
  35.8 2.0 collective-permute-done
  39.4 6.7 %project.1 = (bf16[4,256,192]{2,1,0:T(8,128)(2,1)}, bf16[4,256,384]{2,1,0:T(8,128)(2,1)}, bf16[4,256,192]{2,1,0:T(8,128)(2,1)}, bf16[4,256,384]{2,1,0:T(8,128)(2,1)}) custom-call(bf16[2,256,768]{2,1,0:T(8,128)(2,1)} %tok.3, f32[8,768]{1,0:T(8,128)} %bitcast.154, bf16[384,768]{1,0:T(8,128)(2,1)} %refs_6_.1, bf16[384,768]{1,0:T(8,128)(2,1)} %refs_7_.1, ...), custom_call_target="tpu_custom_call" | custom-call | flops 5750000128 | bytes 1048576 | tf_op jit(solution)/shard_map/project/pallas_call | solution.py:97
  46.1 5.1 all-to-all-start.1
  55.2 5.1 collective-permute-done.6.rest_1_
  61.8 9.2 %all-to-all-done.1 = bf16[4,256,384]{2,1,0:T(8,128)(2,1)} async-done(((bf16[4,256,384]{2,1,0:T(8,128)(2,1)}), bf16[4,256,384]{2,1,0:T(8,128)(2,1)}, u32[]{:S(2)}, u32[]{:S(2)}) %all-to-all-start.1) | async-done | bytes 786464 | tf_op jit(solution)/shard_map/all_to_all | solution.py:893
  70.9 4.2 all-to-all-start.4
  76.6 2.4 fusion.14
  81.6 2.0 copy.73
  83.6 2.8 collective-permute-done.8.rest_4_
  87.9 6.9 %all-to-all-done.4 = bf16[4,256,384]{2,1,0:T(8,128)(2,1)} async-done(((bf16[4,256,384]{2,1,0:T(8,128)(2,1)}), bf16[4,256,384]{2,1,0:T(8,128)(2,1)}, u32[]{:S(2)}, u32[]{:S(2)}) %all-to-all-start.4) | async-done | bytes 786464 | tf_op jit(solution)/shard_map/all_to_all | solution.py:893
  94.8 3.5 all-to-all-start.3
  98.3 1.9 fusion.10
  100.4 2.1 slice_bitcast_fusion.2
  109.5 2.0 copy.69
  111.5 5.1 all-to-all-start
  118.8 9.9 %all-to-all-done = bf16[4,256,192]{1,2,0:T(8,128)(2,1)S(1)} async-done(((bf16[4,256,192]{1,2,0:T(8,128)(2,1)}), bf16[4,256,192]{1,2,0:T(8,128)(2,1)S(1)}, u32[]{:S(2)}, u32[]{:S(2)}) %all-to-all-start) | async-done | bytes 393248 | tf_op jit(solution)/shard_map/all_to_all | solution.py:893
  131.1 18.7 %attend.2 = (bf16[1024,192]{1,0:T(8,128)(2,1)}, f32[3,8,1024]{2,1,0:T(8,128)}) custom-call(s32[48]{0:T(128)} %concatenate.31.sc, bf16[8,128,192]{2,1,0:T(8,128)(2,1)} %bitcast.139, bf16[8,128,384]{2,1,0:T(8,128)(2,1)} %bitcast.6.rest_0_, bf16[8,128,384]{2,1,0:T(8,128)(2,1)} %collective-permute-done.3.rest_1_, ...), custom_call_target="tpu_custom_call" | custom-call | flops 23000000512 | bytes 1048576 | tf_op jit(solution)/shard_map/attend/pallas_call | solution.py:217
  149.8 2.0 copy.71
  151.8 3.5 all-to-all-start.2
  155.3 20.6 %attend.3 = (bf16[1024,192]{1,0:T(8,128)(2,1)}, f32[3,8,1024]{2,1,0:T(8,128)}) custom-call(s32[48]{0:T(128)} %concatenate.34.sc, bf16[8,128,192]{2,1,0:T(8,128)(2,1)} %bitcast.137, bf16[8,128,384]{2,1,0:T(8,128)(2,1)} %bitcast.15.rest_0_, bf16[8,128,384]{2,1,0:T(8,128)(2,1)} %copy-done.45, bf16[8,128,384]{2,1,0:T(8,128)(2,1)} %collective-permute-done.13.rest_2_, ...), custom_call_target="tpu_custom_call" | custom-call | flops 23000000512 | bytes 1048576 | tf_op jit(solution)/shard_map/attend/pallas_call | solution.py:217
  175.9 2.0 copy.75
  177.9 5.2 all-to-all-start.5
  185.6 16.8 %dense.2 = (bf16[256,768]{1,0:T(8,128)(2,1)}, f32[256,768]{1,0:T(8,128)}, bf16[4,256,192]{2,1,0:T(8,128)(2,1)}, bf16[256,768]{1,0:T(8,128)(2,1)}, bf16[256,768]{...) custom-call(s32[2]{0:T(128)} %get-tuple-element.198.sc, ...), custom_call_target="tpu_custom_call" | custom-call | flops 17250000896 | bytes 1048576 | tf_op jit(solution)/shard_map/dense/pallas_call | solution.py:459
  202.4 2.0 copy.77
  204.4 5.1 all-to-all-start.6
  210.9 16.8 %dense.3 = (bf16[256,768]{1,0:T(8,128)(2,1)}, f32[256,768]{1,0:T(8,128)}, bf16[4,256,192]{2,1,0:T(8,128)(2,1)}, bf16[256,768]{1,0:T(8,128)(2,1)}, bf16[256,768]{...) custom-call(s32[2]{0:T(128)} %get-tuple-element.217.sc, ...), custom_call_target="tpu_custom_call" | custom-call | flops 17250000896 | bytes 1048576 | tf_op jit(solution)/shard_map/dense/pallas_call | solution.py:459
  227.8 11.9 %dense_grads.1 = (bf16[4,192,768]{2,1,0:T(8,128)(2,1)}, bf16[4,192,3072]{2,1,0:T(8,128)(2,1)}, bf16[4,768,768]{2,1,0:T(8,128)(2,1)}) custom-call(bf16[256,768]{1,0:T(8,128)(2,1)} %get-tuple-element.116.refs_0_, bf16[256,768]{1,0:T(8,128)(2,1)} %get-tuple-element.117.refs_1_, bf16[256,768]{1,0:T(8,128)(2,1)} %get-tuple-element.118.refs_2_, ...), custom_call_target="tpu_custom_call" | custom-call | flops 11500000256 | bytes 1048576 | tf_op jit(solution)/shard_map/dense_grads/pallas_call | solution.py:506
  241.6 3.3 dynamic-slice_bitcast_fusion.1
  247.0 3.3 dynamic-slice_bitcast_fusion
  251.5 2.0 fusion.2
  253.6 5.1 all-to-all-start.7
  259.7 38.6 %attend_back.2 = (bf16[8,128,192]{2,1,0:T(8,128)(2,1)}, bf16[8,128,384]{2,1,0:T(8,128)(2,1)}, bf16[8,128,384]{2,1,0:T(8,128)(2,1)}, bf16[8,128,384]{2,1,0:T(8,128)(2,1)}, bf16[8,128,384]{2,1,0:T(8,128)(2,1)}) custom-call(s32[48]{0:T(128)} %concatenate.31.sc, bf16[8,128,192]{2,1,0:T(8,128)(2,1)} %bitcast.140, bf16[8,128,192]{2,1,0:T(8,128)(2,1)} %bitcast.146, ...), custom_call_target="tpu_custom_call" | custom-call | flops 51749998592 | bytes 1048576 | tf_op jit(solution)/shard_map/attend_back/pallas_call | solution.py:334
  299.3 4.7 fusion.1
  304.3 43.6 %attend_back.3 = (bf16[8,128,192]{2,1,0:T(8,128)(2,1)}, bf16[8,128,384]{2,1,0:T(8,128)(2,1)}, bf16[8,128,384]{2,1,0:T(8,128)(2,1)}, bf16[8,128,384]{2,1,0:T(8,128)(2,1)}, bf16[8,128,384]{2,1,0:T(8,128)(2,1)}) custom-call(s32[48]{0:T(128)} %concatenate.34.sc, bf16[8,128,192]{2,1,0:T(8,128)(2,1)} %bitcast.138, bf16[8,128,192]{2,1,0:T(8,128)(2,1)} %bitcast.145, ...), custom_call_target="tpu_custom_call" | custom-call | flops 51749998592 | bytes 1048576 | tf_op jit(solution)/shard_map/attend_back/pallas_call | solution.py:334
  348.0 3.7 fusion
  360.2 58.8 %return_grads.1 = (bf16[4,256,192]{2,1,0:T(8,128)(2,1)S(1)}, bf16[4,256,384]{2,1,0:T(8,128)(2,1)S(1)}, bf16[4,256,192]{2,1,0:T(8,128)(2,1)S(1)}, bf16[4,256,384]{2,1,0:T(8,128)(2,1)S(1)}) custom-call(bf16[4,256,192]{2,1,0:T(8,128)(2,1)S(1)} %bitcast.120, bf16[4,256,384]{2,1,0:T(8,128)(2,1)S(1)} %bitcast.112, bf16[4,256,384]{2,1,0:T(8,128)(2,1)S(1)} %bitcast.113, ...), custom_call_target="tpu_custom_call" | custom-call | flops 80499998720 | bytes 1048576 | tf_op jit(solution)/shard_map/return_grads/pallas_call | solution.py:694
  422.3 10.2 %project_grads.1 = (f32[2,256,768]{2,1,0:T(8,128)}, bf16[3,2,2,1152,128]{4,3,2,1,0:T(8,128)(2,1)}, f32[8,768]{1,0:T(8,128)}) custom-call(bf16[2,256,768]{2,1,0:T(8,128)(2,1)} %tok.3, f32[256,768]{1,0:T(8,128)} %get-tuple-element.88.refs_0_, f32[256,768]{1,0:T(8,128)} %get-tuple-element.89.refs_1_, bf16[4,256,192]{2,1,0:T(8,128)(2,1)} %copy-done.13, ...), custom_call_target="tpu_custom_call" | custom-call | flops 11500000256 | bytes 1048576 | tf_op jit(solution)/shard_map/project_grads/pallas_call | solution.py:574
  434.1 2.0 copy-done.10
  436.1 73.9 %sum_grads.1 = (bf16[2,3,1152,128]{3,2,1,0:T(8,128)(2,1)S(1)}, f32[80,128]{1,0:T(8,128)S(1)}) custom-call(bf16[3,2,2,1152,128]{4,3,2,1,0:T(8,128)(2,1)S(1)} %copy-done.10, f32[80,128]{1,0:T(8,128)S(1)} %pad_bitcast_fusion.small), custom_call_target="tpu_custom_call" | custom-call | flops 57500000256 | bytes 1048576 | tf_op jit(solution)/shard_map/sum_grads/pallas_call | solution.py:818
  510.0 62.3 %all-reduce.4.cloned.1.call-done = (bf16[192,768]{1,0:T(8,128)(2,1)}, bf16[192,3072]{1,0:T(8,128)(2,1)}, bf16[768,768]{1,0:T(8,128)(2,1)}) async-done(((bf16[192,768]{1,0:T(8,128)(2,1)}, bf16[192,3072]{1,0:T(8,128)(2,1)}, bf16[768,768]{1,0:T(8,128)(2,1)}), (bf16[192,768]{1,0:T(8,128)(2,1)}, bf16[192,3072]{1,0:T(8,128)(2,1)}, bf16[768,768]{1,0:T(8,128)(2,1)})) %all-reduce.4.cloned.1.call-update) | async-done | bytes 2654224 | tf_op jit(solution)/shard_map/psum | solution.py:918
  575.5 2.7 copy.87
  578.2 2.7 copy.84
  582.2 2.7 copy.85
  592.2 2.1 maximum_select_fusion
  594.3 2.9 bitcast_convert_fusion.1
  597.6 2.7 bitcast_convert_fusion
  (217 shorter events, 64.5 us)
Async XLA Ops:
  7.2 25.0 %copy-start.33 = (bf16[384]{0:T(512)(128)(2,1)S(1)}, bf16[384]{0:T(512)(128)(2,1)}, u32[]{:S(2)}) copy-start(bf16[384]{0:T(512)(128)(2,1)} %param.25) | copy-start | bytes 2308
  7.2 25.2 %copy-start.34 = (bf16[384]{0:T(512)(128)(2,1)S(1)}, bf16[384]{0:T(512)(128)(2,1)}, u32[]{:S(2)}) copy-start(bf16[384]{0:T(512)(128)(2,1)} %param.28) | copy-start | bytes 2308
  7.2 25.4 %copy-start.35 = (bf16[384]{0:T(512)(128)(2,1)S(1)}, bf16[384]{0:T(512)(128)(2,1)}, u32[]{:S(2)}) copy-start(bf16[384]{0:T(512)(128)(2,1)} %param.30) | copy-start | bytes 2308
  7.2 25.6 %copy-start.36 = (bf16[384]{0:T(512)(128)(2,1)S(1)}, bf16[384]{0:T(512)(128)(2,1)}, u32[]{:S(2)}) copy-start(bf16[384]{0:T(512)(128)(2,1)} %param.31) | copy-start | bytes 2308
  7.2 25.8 %copy-start.37 = (bf16[384]{0:T(512)(128)(2,1)S(1)}, bf16[384]{0:T(512)(128)(2,1)}, u32[]{:S(2)}) copy-start(bf16[384]{0:T(512)(128)(2,1)} %param.32) | copy-start | bytes 2308
  7.2 26.0 %copy-start.38 = (bf16[384]{0:T(512)(128)(2,1)S(1)}, bf16[384]{0:T(512)(128)(2,1)}, u32[]{:S(2)}) copy-start(bf16[384]{0:T(512)(128)(2,1)} %param.36) | copy-start | bytes 2308
  7.3 26.3 %copy-start.39 = (bf16[384]{0:T(512)(128)(2,1)S(1)}, bf16[384]{0:T(512)(128)(2,1)}, u32[]{:S(2)}) copy-start(bf16[384]{0:T(512)(128)(2,1)} %param.37) | copy-start | bytes 2308
  7.3 26.5 %copy-start.40 = (bf16[384]{0:T(512)(128)(2,1)S(1)}, bf16[384]{0:T(512)(128)(2,1)}, u32[]{:S(2)}) copy-start(bf16[384]{0:T(512)(128)(2,1)} %param.38) | copy-start | bytes 2308
  7.3 26.7 %copy-start.31 = (bf16[1536]{0:T(1024)(128)(2,1)S(1)}, bf16[1536]{0:T(1024)(128)(2,1)}, u32[]{:S(2)}) copy-start(bf16[1536]{0:T(1024)(128)(2,1)} %param.34) | copy-start | bytes 9220
  9.5 22.7 %collective-permute-start.1 = (bf16[576,768]{1,0:T(8,128)(2,1)S(1)}, bf16[576,768]{1,0:T(8,128)(2,1)S(1)}, u32[]{:S(2)}, u32[]{:S(2)}) collective-permute-start(bf16[576,768]{1,0:T(8,128)(2,1)S(1)} %pad_maximum_fusion), channel_id=1, source_target_pairs={{0,1},{1,0},{2,3},{3,2},{4,5},{5,4},{6,7},{7,6},{8,9},{9,8},{10,11... | collective-permute-start | bytes 2654216 | tf_op jit(solution)/shard_map/ppermute | solution.py:885
  32.1 6.4 %collective-permute-start.2 = (bf16[576,768]{1,0:T(8,128)(2,1)S(1)}, bf16[576,768]{1,0:T(8,128)(2,1)S(1)}, u32[]{:S(2)}, u32[]{:S(2)}) collective-permute-start(bf16[576,768]{1,0:T(8,128)(2,1)S(1)} %collective-permute-done.1.first.refs_9_), channel_id=1, source_target_pairs={{0,2},{2,0},{4,6},{6,4},{8,10},{10,8},{12,14},{14,12},{16,18},{18,... | collective-permute-start | bytes 2654216 | tf_op jit(solution)/shard_map/ppermute | solution.py:888
  34.0 3.8 collective-permute-start
  39.4 12.8 %copy-start.24 = (bf16[384,768]{1,0:T(8,128)(2,1)S(1)}, bf16[384,768]{1,0:T(8,128)(2,1)}, u32[]{:S(2)}) copy-start(bf16[384,768]{1,0:T(8,128)(2,1)} %rest_0_.3) | copy-start | bytes 1769476
  46.1 24.8 %all-to-all-start.1 = ((bf16[4,256,384]{2,1,0:T(8,128)(2,1)}), bf16[4,256,384]{2,1,0:T(8,128)(2,1)}, u32[]{:S(2)}, u32[]{:S(2)}) async-start(bf16[4,256,384]{2,1,0:T(8,128)(2,1)} %get-tuple-element.78), calls=%async_computation.1 | async-start | bytes 1572864 | tf_op jit(solution)/shard_map/all_to_all | solution.py:893
  51.3 23.9 %copy-start.48 = (s32[4]{0:T(128)S(1)}, s32[4]{0:T(128)}, u32[]{:S(2)}) copy-start(s32[4]{0:T(128)} %constant.158.clone) | copy-start | bytes 52
  52.3 8.0 %collective-permute-start.6 = (bf16[192,768]{1,0:T(8,128)(2,1)S(1)}, bf16[192,768]{1,0:T(8,128)(2,1)S(1)}, u32[]{:S(2)}, u32[]{:S(2)}) collective-permute-start(bf16[192,768]{1,0:T(8,128)(2,1)S(1)} %constant_dynamic-slice_fusion.2), channel_id=1, source_target_pairs={{0,1},{1,0},{2,3},{3,2},{4,5},{5,4},{6,7},{7,6},{8,9},{9,8},{10,11... | collective-permute-start | bytes 884744 | tf_op jit(solution)/shard_map/ppermute | solution.py:885
  55.2 25.5 %copy-start.19 = (bf16[2,256,768]{2,1,0:T(8,128)(2,1)S(1)}, bf16[2,256,768]{2,1,0:T(8,128)(2,1)}, u32[]{:S(2)}) copy-start(bf16[2,256,768]{2,1,0:T(8,128)(2,1)} %tok.3) | copy-start | bytes 2359300
  60.3 57.5 %copy-start.46 = (bf16[192,768]{1,0:T(8,128)(2,1)}, bf16[192,768]{1,0:T(8,128)(2,1)S(1)}, u32[]{:S(2)}) copy-start(bf16[192,768]{1,0:T(8,128)(2,1)S(1)} %collective-permute-done.6.rest_1_) | copy-start | bytes 884740
  60.3 26.2 %collective-permute-start.8 = (bf16[192,3072]{1,0:T(8,128)(2,1)S(1)}, bf16[192,3072]{1,0:T(8,128)(2,1)}, u32[]{:S(2)}, u32[]{:S(2)}) collective-permute-start(bf16[192,3072]{1,0:T(8,128)(2,1)S(1)} %constant_dynamic-slice_fusion.1), channel_id=1, source_target_pairs={{0,1},{1,0},{2,3},{3,2},{4,5},{5,4},{6,7},{7,6},{8,9},{9,8},{10,11... | collective-permute-start | bytes 3538952 | tf_op jit(solution)/shard_map/ppermute | solution.py:885
  70.9 23.9 %all-to-all-start.4 = ((bf16[4,256,384]{2,1,0:T(8,128)(2,1)}), bf16[4,256,384]{2,1,0:T(8,128)(2,1)}, u32[]{:S(2)}, u32[]{:S(2)}) async-start(bf16[4,256,384]{2,1,0:T(8,128)(2,1)} %get-tuple-element.85), calls=%async_computation.4 | async-start | bytes 1572864 | tf_op jit(solution)/shard_map/all_to_all | solution.py:893
  79.1 25.0 %collective-permute-start.3 = (bf16[8,128,384]{2,1,0:T(8,128)(2,1)}, bf16[8,128,384]{2,1,0:T(8,128)(2,1)}, u32[]{:S(2)}, u32[]{:S(2)}) collective-permute-start(bf16[8,128,384]{2,1,0:T(8,128)(2,1)} %bitcast.6.rest_0_), channel_id=1, source_target_pairs={{0,4},{2,6},{4,0},{6,2},{8,12},{10,14},{12,8},{14,10},{16,20},{18,... | collective-permute-start | bytes 2359304 | tf_op jit(solution)/shard_map/ppermute | solution.py:888
  86.5 43.2 %collective-permute-start.10 = (bf16[768,768]{1,0:T(8,128)(2,1)S(1)}, bf16[768,768]{1,0:T(8,128)(2,1)}, u32[]{:S(2)}, u32[]{:S(2)}) collective-permute-start(bf16[768,768]{1,0:T(8,128)(2,1)S(1)} %constant_dynamic-slice_fusion), channel_id=1, source_target_pairs={{0,1},{1,0},{2,3},{3,2},{4,5},{5,4},{6,7},{7,6},{8,9},{9,8},{10,11... | collective-permute-start | bytes 3538952 | tf_op jit(solution)/shard_map/ppermute | solution.py:885
  94.8 16.7 %all-to-all-start.3 = ((bf16[4,256,192]{1,2,0:T(8,128)(2,1)}), bf16[4,256,192]{1,2,0:T(8,128)(2,1)S(1)}, u32[]{:S(2)}, u32[]{:S(2)}) async-start(bf16[4,256,192]{1,2,0:T(8,128)(2,1)} %copy.73), calls=%async_computation.3 | async-start | bytes 786432 | tf_op jit(solution)/shard_map/all_to_all | solution.py:893
  102.5 28.1 %collective-permute-start.4 = (bf16[8,128,384]{2,1,0:T(8,128)(2,1)}, bf16[8,128,384]{2,1,0:T(8,128)(2,1)}, u32[]{:S(2)}, u32[]{:S(2)}) collective-permute-start(bf16[8,128,384]{2,1,0:T(8,128)(2,1)} %bitcast.6.rest_0_), channel_id=1, source_target_pairs={{0,2},{2,0},{4,6},{6,4},{8,10},{10,8},{12,14},{14,12},{16,18},{18,... | collective-permute-start | bytes 2359304 | tf_op jit(solution)/shard_map/ppermute | solution.py:888
  102.5 27.2 %collective-permute-start.12 = (bf16[8,128,384]{2,1,0:T(8,128)(2,1)}, bf16[8,128,384]{2,1,0:T(8,128)(2,1)S(1)}, u32[]{:S(2)}, u32[]{:S(2)}) collective-permute-start(bf16[8,128,384]{2,1,0:T(8,128)(2,1)} %bitcast.15.rest_0_), channel_id=1, source_target_pairs={{0,4},{2,6},{4,0},{6,2},{8,12},{10,14},{12,8},{14,10},{16,20},{18,... | collective-permute-start | bytes 2359304 | tf_op jit(solution)/shard_map/ppermute | solution.py:888
  104.0 27.1 %collective-permute-start.5 = (bf16[8,128,384]{2,1,0:T(8,128)(2,1)}, bf16[8,128,384]{2,1,0:T(8,128)(2,1)}, u32[]{:S(2)}, u32[]{:S(2)}) collective-permute-start(bf16[8,128,384]{2,1,0:T(8,128)(2,1)} %collective-permute-done.3.rest_1_), channel_id=1, source_target_pairs={{0,2},{2,0},{4,6},{6,4},{8,10},{10,8},{12,14},{14,12},{16,18},{18,... | collective-permute-start | bytes 2359304 | tf_op jit(solution)/shard_map/ppermute | solution.py:888
  111.5 17.2 %all-to-all-start = ((bf16[4,256,192]{1,2,0:T(8,128)(2,1)}), bf16[4,256,192]{1,2,0:T(8,128)(2,1)S(1)}, u32[]{:S(2)}, u32[]{:S(2)}) async-start(bf16[4,256,192]{1,2,0:T(8,128)(2,1)} %copy.69), calls=%async_computation | async-start | bytes 786432 | tf_op jit(solution)/shard_map/all_to_all | solution.py:893
  117.7 66.4 %collective-permute-start.7 = (bf16[192,768]{1,0:T(8,128)(2,1)S(1)}, bf16[192,768]{1,0:T(8,128)(2,1)}, u32[]{:S(2)}, u32[]{:S(2)}) collective-permute-start(bf16[192,768]{1,0:T(8,128)(2,1)S(1)} %collective-permute-done.6.rest_1_), channel_id=1, source_target_pairs={{0,2},{2,0},{4,6},{6,4},{8,10},{10,8},{12,14},{14,12},{16,18},{18,... | collective-permute-start | bytes 884744 | tf_op jit(solution)/shard_map/ppermute | solution.py:888
  129.7 54.5 %collective-permute-start.9 = (bf16[192,3072]{1,0:T(8,128)(2,1)}, bf16[192,3072]{1,0:T(8,128)(2,1)S(1)}, u32[]{:S(2)}, u32[]{:S(2)}) collective-permute-start(bf16[192,3072]{1,0:T(8,128)(2,1)} %collective-permute-done.8.rest_4_), channel_id=1, source_target_pairs={{0,2},{2,0},{4,6},{6,4},{8,10},{10,8},{12,14},{14,12},{16,18},{18,... | collective-permute-start | bytes 3538952 | tf_op jit(solution)/shard_map/ppermute | solution.py:888
  129.7 25.6 %collective-permute-start.13 = (bf16[8,128,384]{2,1,0:T(8,128)(2,1)}, bf16[8,128,384]{2,1,0:T(8,128)(2,1)}, u32[]{:S(2)}, u32[]{:S(2)}) collective-permute-start(bf16[8,128,384]{2,1,0:T(8,128)(2,1)} %bitcast.15.rest_0_), channel_id=1, source_target_pairs={{0,2},{2,0},{4,6},{6,4},{8,10},{10,8},{12,14},{14,12},{16,18},{18,... | collective-permute-start | bytes 2359304 | tf_op jit(solution)/shard_map/ppermute | solution.py:888
  130.6 53.6 %collective-permute-start.11 = (bf16[768,768]{1,0:T(8,128)(2,1)}, bf16[768,768]{1,0:T(8,128)(2,1)S(1)}, u32[]{:S(2)}, u32[]{:S(2)}) collective-permute-start(bf16[768,768]{1,0:T(8,128)(2,1)} %collective-permute-done.10.rest_7_), channel_id=1, source_target_pairs={{0,2},{2,0},{4,6},{6,4},{8,10},{10,8},{12,14},{14,12},{16,18},{18,... | collective-permute-start | bytes 3538952 | tf_op jit(solution)/shard_map/ppermute | solution.py:888
  131.1 24.2 %collective-permute-start.14 = (bf16[8,128,384]{2,1,0:T(8,128)(2,1)}, bf16[8,128,384]{2,1,0:T(8,128)(2,1)}, u32[]{:S(2)}, u32[]{:S(2)}) collective-permute-start(bf16[8,128,384]{2,1,0:T(8,128)(2,1)} %copy-done.45), channel_id=1, source_target_pairs={{0,2},{2,0},{4,6},{6,4},{8,10},{10,8},{12,14},{14,12},{16,18},{18,... | collective-permute-start | bytes 2359304 | tf_op jit(solution)/shard_map/ppermute | solution.py:888
  151.8 26.1 %all-to-all-start.2 = ((bf16[4,256,192]{1,2,0:T(8,128)(2,1)}), bf16[4,256,192]{1,2,0:T(8,128)(2,1)S(1)}, u32[]{:S(2)}, u32[]{:S(2)}) async-start(bf16[4,256,192]{1,2,0:T(8,128)(2,1)} %copy.71), calls=%async_computation.2 | async-start | bytes 786432 | tf_op jit(solution)/shard_map/all_to_all | solution.py:893
  177.9 26.5 %all-to-all-start.5 = ((bf16[4,256,192]{1,2,0:T(8,128)(2,1)}), bf16[4,256,192]{1,2,0:T(8,128)(2,1)S(1)}, u32[]{:S(2)}, u32[]{:S(2)}) async-start(bf16[4,256,192]{1,2,0:T(8,128)(2,1)} %copy.75), calls=%async_computation.5 | async-start | bytes 786432 | tf_op jit(solution)/shard_map/all_to_all | solution.py:893
  204.4 49.1 %all-to-all-start.6 = ((bf16[4,256,192]{1,2,0:T(8,128)(2,1)}), bf16[4,256,192]{1,2,0:T(8,128)(2,1)S(1)}, u32[]{:S(2)}, u32[]{:S(2)}) async-start(bf16[4,256,192]{1,2,0:T(8,128)(2,1)} %copy.77), calls=%async_computation.6 | async-start | bytes 786432 | tf_op jit(solution)/shard_map/all_to_all | solution.py:893
  209.5 224.5 %reduce-scatter.4.cloned.1.call-start = ((), (), s32[]{:S(2)}) async-start(), calls=%async_computation.11 | async-start | bytes 884736 | tf_op jit(solution)/shard_map/reduce_scatter | solution.py:915
  241.6 9.9 %collective-permute-start.15 = (bf16[2,192,768]{2,1,0:T(8,128)(2,1)}, bf16[2,192,768]{2,1,0:T(8,128)(2,1)}, u32[]{:S(2)}, u32[]{:S(2)}) collective-permute-start(bf16[2,192,768]{2,1,0:T(8,128)(2,1)} %dynamic-slice_bitcast_fusion.2), channel_id=1, source_target_pairs={{0,2},{2,0},{4,6},{6,4},{8,10},{10,8},{12,14},{14,12},{16,18},{18,... | collective-permute-start | bytes 1769480 | tf_op jit(solution)/shard_map/ppermute | solution.py:888
  246.5 52.8 %collective-permute-start.16 = (bf16[2,192,3072]{2,1,0:T(8,128)(2,1)}, bf16[2,192,3072]{2,1,0:T(8,128)(2,1)}, u32[]{:S(2)}, u32[]{:S(2)}) collective-permute-start(bf16[2,192,3072]{2,1,0:T(8,128)(2,1)} %dynamic-slice_bitcast_fusion.1), channel_id=1, source_target_pairs={{0,2},{2,0},{4,6},{6,4},{8,10},{10,8},{12,14},{14,12},{16,18},{18,... | collective-permute-start | bytes 7077896 | tf_op jit(solution)/shard_map/ppermute | solution.py:888
  250.3 97.7 %collective-permute-start.17 = (bf16[2,768,768]{2,1,0:T(8,128)(2,1)}, bf16[2,768,768]{2,1,0:T(8,128)(2,1)S(1)}, u32[]{:S(2)}, u32[]{:S(2)}) collective-permute-start(bf16[2,768,768]{2,1,0:T(8,128)(2,1)} %dynamic-slice_bitcast_fusion), channel_id=1, source_target_pairs={{0,2},{2,0},{4,6},{6,4},{8,10},{10,8},{12,14},{14,12},{16,18},{18,... | collective-permute-start | bytes 7077896 | tf_op jit(solution)/shard_map/ppermute | solution.py:888
  253.6 44.7 %all-to-all-start.7 = ((bf16[4,256,192]{1,2,0:T(8,128)(2,1)}), bf16[4,256,192]{1,2,0:T(8,128)(2,1)S(1)}, u32[]{:S(2)}, u32[]{:S(2)}) async-start(bf16[4,256,192]{1,2,0:T(8,128)(2,1)} %copy.79), calls=%async_computation.7 | async-start | bytes 786432 | tf_op jit(solution)/shard_map/all_to_all | solution.py:893
  258.7 175.3 %reduce-scatter.6.cloned.1.call-start = ((), (), s32[]{:S(2)}) async-start(), calls=%async_computation.12 | async-start | bytes 3538944 | tf_op jit(solution)/shard_map/reduce_scatter | solution.py:915
  304.1 130.0 %reduce-scatter.8.cloned.1.call-start = ((), (), s32[]{:S(2)}) async-start(), calls=%async_computation.13 | async-start | bytes 3538944 | tf_op jit(solution)/shard_map/reduce_scatter | solution.py:915
  351.7 220.6 %all-reduce.4.cloned.1.call-start = ((), (), s32[]{:S(2)}) async-start(), calls=%async_computation.14 | async-start | bytes 5308416 | tf_op jit(solution)/shard_map/psum | solution.py:918
  436.1 136.2 %copy-start.21 = (bf16[256,768]{1,0:T(8,128)(2,1)S(1)}, bf16[256,768]{1,0:T(8,128)(2,1)}, u32[]{:S(2)}) copy-start(bf16[256,768]{1,0:T(8,128)(2,1)} %get-tuple-element.83) | copy-start | bytes 1179652
  436.1 136.2 %copy-start.22 = (bf16[256,768]{1,0:T(8,128)(2,1)S(1)}, bf16[256,768]{1,0:T(8,128)(2,1)}, u32[]{:S(2)}) copy-start(bf16[256,768]{1,0:T(8,128)(2,1)} %get-tuple-element.87) | copy-start | bytes 1179652
  572.3 19.9 %collective-permute-start.19 = (bf16[192,3072]{1,0:T(8,128)(2,1)}, bf16[192,3072]{1,0:T(8,128)(2,1)}, u32[]{:S(2)}, u32[]{:S(2)}) collective-permute-start(bf16[192,3072]{1,0:T(8,128)(2,1)} %get-tuple-element.134), channel_id=1, source_target_pairs={{0,2},{2,0},{4,6},{6,4},{8,10},{10,8},{12,14},{14,12},{16,18},{18,... | collective-permute-start | bytes 3538952 | tf_op jit(solution)/shard_map/ppermute | solution.py:888
  573.3 16.7 %collective-permute-start.18 = (bf16[192,768]{1,0:T(8,128)(2,1)}, bf16[192,768]{1,0:T(8,128)(2,1)}, u32[]{:S(2)}, u32[]{:S(2)}) collective-permute-start(bf16[192,768]{1,0:T(8,128)(2,1)} %get-tuple-element.133), channel_id=1, source_target_pairs={{0,2},{2,0},{4,6},{6,4},{8,10},{10,8},{12,14},{14,12},{16,18},{18,... | collective-permute-start | bytes 884744 | tf_op jit(solution)/shard_map/ppermute | solution.py:888
  586.7 10.6 %collective-permute-start.20 = (bf16[768,768]{1,0:T(8,128)(2,1)S(1)}, bf16[768,768]{1,0:T(8,128)(2,1)S(1)}, u32[]{:S(2)}, u32[]{:S(2)}) collective-permute-start(bf16[768,768]{1,0:T(8,128)(2,1)S(1)} %copy-done.16), channel_id=1, source_target_pairs={{0,2},{2,0},{4,6},{6,4},{8,10},{10,8},{12,14},{14,12},{16,18},{18,... | collective-permute-start | bytes 3538952 | tf_op jit(solution)/shard_map/ppermute | solution.py:888
  (34 other events, 117.7 us)
Sparse Core Ops, SparseCore 0:
  253.7 14.9 reduce-scatter.3
  304.2 34.2 reduce-scatter.5
  351.8 34.2 reduce-scatter.7
  434.2 138.0 all-reduce.3

commit v3 on v2

--- a/solution.py
+++ b/solution.py
@@ -714,8 +714,259 @@
     )(*args)
 
 
-def sum_kernel(grads, small, out, small_out, *rest):
-    acc, from_core, from_x, from_y, from_z, res, vec, vec_in, sems, small_sems, last_sem = rest
+def middle_stage(s, att, mask, tok, teach, vec, wide_vec, weights, keep, outs, first_done):
+    wo, wi, wu, slope = weights
+    att_k, br_k, hl_k, il_k, act_k, ol_k = keep
+    out, fg, sums, wide_sums = outs
+    rows = att.shape[0]
+    hidden = wi.shape[1]
+    tile = 512
+    rs = slice(s * rows, (s + 1) * rows)
+    out_bias, gain_one, shift_one = vec[0:1, :], vec[1:2, :], vec[2:3, :]
+    outer_bias, gain_two, shift_two = vec[3:4, :], vec[4:5, :], vec[5:6, :]
+    add = functools.partial(jnp.sum, axis=0, keepdims=True)
+
+    def collect(target, value):
+        if s == 0:
+            target[...] = value
+        else:
+            target[...] += value
+
+    att_k[rs, :] = att
+    first_done[0]()
+    first = tok[s].astype(F32) + dot(att, wo[...]) + out_bias
+    normed_one, inverse_one = norm(first)
+    hidden_in = normed_one * gain_one + shift_one
+    hl = hidden_in.astype(BF16)
+    hl_k[rs, :] = hl
+    first_done[1]()
+    second = hidden_in + outer_bias
+    for n in range(hidden // tile):
+        cols = slice(n * tile, (n + 1) * tile)
+        inner = dot(hl, wi[:, cols]) + wide_vec[0:1, cols]
+        below, density = normal_parts(inner)
+        act = (inner * below).astype(BF16)
+        act_k[rs, cols] = act
+        slope[:, cols] = below + inner * density
+        second += dot(act, wu[cols, :])
+    normed_two, inverse_two = norm(second)
+    final = normed_two * gain_two + shift_two
+    out[s] = final.astype(BF16)
+    residue = (final - teach[s].astype(F32)) * mask
+    collect(sums.at[0:1], add(residue * normed_two))
+    collect(sums.at[1:2], add(residue))
+    collect(sums.at[6:7], add(residue * residue))
+    second_grad = norm_back(residue * gain_two, normed_two, inverse_two)
+    ol = second_grad.astype(BF16)
+    ol_k[rs, :] = ol
+    collect(sums.at[2:3], add(ol.astype(F32)))
+    hidden_grad = second_grad
+    for n in range(hidden // tile):
+        cols = slice(n * tile, (n + 1) * tile)
+        il = (dot(ol, wu[cols, :], NT) * slope[:, cols]).astype(BF16)
+        il_k[rs, cols] = il
+        collect(wide_sums.at[0:1, cols], add(il.astype(F32)))
+        hidden_grad += dot(il, wi[:, cols], NT)
+    first_grad = norm_back(hidden_grad * gain_one, normed_one, inverse_one)
+    fg[s] = first_grad
+    br = first_grad.astype(BF16)
+    br_k[rs, :] = br
+    collect(sums.at[3:4], add(hidden_grad * normed_one))
+    collect(sums.at[4:5], add(hidden_grad))
+    collect(sums.at[5:6], add(br.astype(F32)))
+    return dot(br, wo[...], NT).astype(BF16)
+
+
+def middle_kernel(seqs, sc, tok, teach, vec, wide_vec, *refs):
+    attended, weights, refs = refs[:seqs], refs[seqs : seqs + 9], refs[seqs + 9 :]
+    out, fg, sums, wide_sums, a_own, a_give, b_own, b_give = refs[:8]
+    grads_in, refs = refs[8 : 8 + seqs], refs[8 + seqs :]
+    wo, wi, wu, slope, o_in, g_out, att_k, br_k, hl_k, il_k, act_k, ol_k = refs[:12]
+    mine, give, given, w_sem, o_sem, g_sem, c_sem = refs[12:]
+    z, y, c, x = position()
+    sibling = device(z, y, 1 - c, x)
+    line = [None] + [device(z ^ d, y, c, x) for d in range(1, GROUPS)]
+    greet([sibling] + line[1:])
+    coming, going = {}, {}
+    for s in range(seqs):
+        for d in range(1, GROUPS):
+            sems = o_sem.at[0, s, d], o_sem.at[1, s, d]
+            coming[s, d] = send(attended[s].at[z ^ d], o_in.at[s, z], sems, line[d])
+        coming[s, 0] = pltpu.make_async_copy(attended[s].at[z], o_in.at[s, z], o_sem.at[0, s, 0])
+        coming[s, 0].start()
+    copies = [
+        weight_copies(full, *weights[3 * i : 3 * i + 3], w_sem, 3 * i)
+        for i, full in enumerate((wo, wi, wu))
+    ]
+    for group in copies:
+        for copy in group:
+            copy.start()
+
+    def loaded(which):
+        for i in which:
+            for copy in copies[i]:
+                copy.wait()
+
+    rows = tok.shape[1]
+    per = o_in.shape[3]
+    row = lax.broadcasted_iota(jnp.int32, (rows, 1), 0)
+    for s in range(seqs):
+        for d in range(GROUPS):
+            coming[s, d].wait()
+        att = jnp.concatenate([o_in[s, g] for g in range(GROUPS)], 1)
+        first, later = (jnp.where(row < sc[2 * s], 1.0, 0.0), jnp.where(row - BLK < sc[2 * s + 1], 1.0, 0.0))
+        mask = jnp.where(row < BLK, first, later)
+        waits = (lambda: loaded([0]), lambda: loaded([1, 2])) if s == 0 else (lambda: None,) * 2
+        found = middle_stage(
+            s,
+            att,
+            mask,
+            tok,
+            teach,
+            vec,
+            wide_vec,
+            (wo, wi, wu, slope),
+            (att_k, br_k, hl_k, il_k, act_k, ol_k),
+            (out, fg, sums, wide_sums),
+            waits,
+        )
+        for g in range(GROUPS):
+            g_out[s, g] = found[:, g * per : (g + 1) * per]
+        for d in range(1, GROUPS):
+            sems = g_sem.at[0, s, d], g_sem.at[1, s, d]
+            going[s, d] = send(g_out.at[s, z ^ d], grads_in[s].at[z], sems, line[d])
+        going[s, 0] = pltpu.make_async_copy(g_out.at[s, z], grads_in[s].at[z], g_sem.at[0, s, 0])
+        going[s, 0].start()
+    sums[7:8, :] = jnp.zeros((1, sums.shape[1]), F32)
+
+    half = wo.shape[0] // 2
+    hidden = wi.shape[1]
+    blocks = hidden // (2 * half)
+
+    def weight_grads(target, part):
+        def cols(start):
+            return pl.ds(pl.multiple_of(start + part * half, 128), half)
+
+        for k in range(2):
+            ks = slice(k * half, (k + 1) * half)
+            target[k, 0:half, :] = dot(att_k[:, ks], br_k[:, cols(0)], TN).astype(BF16)
+            for t in range(blocks):
+                target[k, (1 + t) * half : (2 + t) * half, :] = dot(
+                    hl_k[:, ks], il_k[:, cols(2 * t * half)], TN
+                ).astype(BF16)
+            base = (1 + blocks) * half
+            for t in range(blocks):
+                rows_of = slice((k * blocks + t) * half, (k * blocks + t + 1) * half)
+                target[k, base + t * half : base + (t + 1) * half, :] = dot(
+                    act_k[:, rows_of], ol_k[:, cols(0)], TN
+                ).astype(BF16)
+
+    weight_grads(give, 1 - c)
+    core = [
+        send(give.at[k], given.at[k], (c_sem.at[0, k], c_sem.at[1, k]), sibling) for k in range(2)
+    ]
+    weight_grads(mine, c)
+    for copy in core:
+        copy.wait()
+    cut, b_half = a_own.shape[0], b_own.shape[1]
+    a_own[...] = add_low(mine[x, 0:cut], given[x, 0:cut])
+    a_give[...] = add_low(mine[1 - x, 0:cut], given[1 - x, 0:cut])
+    for k in range(2):
+        for target, which in ((b_own, y), (b_give, 1 - y)):
+            part = pl.ds(pl.multiple_of(cut + which * b_half, 16), b_half)
+            target[k] = add_low(mine[k, part], given[k, part])
+    for copy in going.values():
+        copy.wait()
+
+
+def cut_of(total):
+    return total // 256 * 128
+
+
+def middle(sc, tok, teach, vec, wide_vec, attended, weights):
+    seqs, rows, width = tok.shape
+    hidden = wide_vec.shape[1]
+    half = width // 2
+    total = half + hidden
+    cut = cut_of(total)
+    dma = pltpu.SemaphoreType.DMA
+    narrow, wide = (seqs * rows, width), (seqs * rows, hidden)
+    b_shape = jax.ShapeDtypeStruct((2, (total - cut) // 2, half), BF16)
+    a_shape = jax.ShapeDtypeStruct((cut, half), BF16)
+    groups, _, per = attended[0].shape
+    return pl.pallas_call(
+        functools.partial(middle_kernel, seqs),
+        out_shape=[
+            jax.ShapeDtypeStruct(tok.shape, BF16),
+            jax.ShapeDtypeStruct(tok.shape, F32),
+            jax.ShapeDtypeStruct((8, width), F32),
+            jax.ShapeDtypeStruct((1, hidden), F32),
+            a_shape,
+            a_shape,
+            b_shape,
+            b_shape,
+        ]
+        + [jax.ShapeDtypeStruct(a.shape, BF16) for a in attended],
+        in_specs=[SMEM] + [VMEM] * 4 + [ANY] * (seqs + 9),
+        out_specs=[VMEM] * 8 + [ANY] * seqs,
+        scratch_shapes=[
+            pltpu.VMEM((width, width), BF16),
+            pltpu.VMEM((width, hidden), BF16),
+            pltpu.VMEM((hidden, width), BF16),
+            pltpu.VMEM((rows, hidden), F32),
+            pltpu.VMEM((seqs, groups, rows, per), BF16),
+            pltpu.VMEM((seqs, groups, rows, per), BF16),
+            pltpu.VMEM(narrow, BF16),
+            pltpu.VMEM(narrow, BF16),
+            pltpu.VMEM(narrow, BF16),
+            pltpu.VMEM(wide, BF16),
+            pltpu.VMEM(wide, BF16),
+            pltpu.VMEM(narrow, BF16),
+            pltpu.VMEM((2, total, half), BF16),
+            pltpu.VMEM((2, total, half), BF16),
+            pltpu.VMEM((2, total, half), BF16),
+            dma((9,)),
+            dma((2, seqs, groups)),
+            dma((2, seqs, groups)),
+            dma((2, 2)),
+        ],
+        compiler_params=pltpu.CompilerParams(
+            vmem_limit_bytes=62 * 2**20, collective_id=3, has_side_effects=True
+        ),
+        cost_estimate=cost(60),
+        name="middle",
+    )(sc, tok, teach, vec, wide_vec, *attended, *weights)
+
+
+def halve_kernel(a_own, a_in, b_own, b_in, a_keep, a_give, b_keep, b_give):
+    _, y, _, x = position()
+    half = a_keep.shape[0]
+    for target, which in ((a_keep, y), (a_give, 1 - y)):
+        part = pl.ds(pl.multiple_of(which * half, 16), half)
+        target[...] = add_low(a_own[part, :], a_in[part, :])
+    for target, which in ((b_keep, x), (b_give, 1 - x)):
+        target[...] = add_low(b_own[which], b_in[which])
+
+
+def halve(a_own, a_in, b_own, b_in):
+    a = jax.ShapeDtypeStruct((a_own.shape[0] // 2, a_own.shape[1]), BF16)
+    b = jax.ShapeDtypeStruct(b_own.shape[1:], BF16)
+    return pl.pallas_call(
+        halve_kernel,
+        out_shape=[a, a, b, b],
+        in_specs=[VMEM] * 4,
+        out_specs=[VMEM] * 4,
+        compiler_params=ROOM,
+        cost_estimate=cost(3),
+        name="halve",
+    )(a_own, a_in, b_own, b_in)
+
+
+def sum_kernel(grads, small, *rest):
+    ready, rest = rest[:4], rest[4:]
+    out, dense_out, small_out, *rest = rest
+    acc, from_core, from_x, from_y, from_z, res, vec, vec_in = rest[:8]
+    two, a_in, b_in, dense_res, sems, small_sems, d_sems, last_sem = rest[8:]
     z, y, c, x = position()
     sibling, beside, over = device(z, y, 1 - c, x), device(z, 1 - y, c, x), device(z, y, c, 1 - x)
     line = [None] + [device(z ^ d, y, c, x) for d in range(1, GROUPS)]
@@ -738,6 +989,23 @@
     core = [
         send(grads.at[p, 1 - c], from_core.at[p], pair(0, p), sibling) for p in range(parts)
     ]
+    a_cut = 2 * ready[0].shape[0]
+    parts_of = []
+    for i, landing in enumerate((a_in, b_in)):
+        keep, other = ready[2 * i], ready[2 * i + 1]
+        n = keep.shape[0]
+        own = two.at[i, 0:n]
+        own[...] = add_low(keep[...], other[...])
+        parts_of.append((own, landing, n, n // GROUPS, i * a_cut + y * n))
+
+    def d_pair(k, i):
+        return d_sems.at[0, k, i], d_sems.at[1, k, i]
+
+    dense_lines = {}
+    for i, (own, landing, n, size, _) in enumerate(parts_of):
+        for d in range(1, GROUPS):
+            src = own.at[pl.ds(pl.multiple_of((z ^ d) * size, 16), size)]
+            dense_lines[i, d] = send(src, landing.at[d], d_pair(d, i), line[d])
     short = send(small, vec_in.at[0], small_pair(0), sibling)
     flows = []
     for p in range(parts):
@@ -779,6 +1047,16 @@
     shorts = [
         send(vec, vec_in.at[4 + z], small_pair(2 + d), line[d]) for d in range(1, GROUPS)
     ]
+    dense_spread = {}
+    for i, (own, landing, n, size, base) in enumerate(parts_of):
+        total = own[pl.ds(pl.multiple_of(z * size, 16), size), :].astype(F32)
+        for d in range(1, GROUPS):
+            dense_lines[i, d].wait()
+            total += landing[d].astype(F32)
+        place = dense_res.at[c, pl.ds(pl.multiple_of(base + z * size, 16), size)]
+        place[...] = total.astype(BF16)
+        for d in range(1, GROUPS):
+            dense_spread[i, d] = send(place, place, d_pair(3 + d, i), line[d])
     spread = {}
     for p in (1, 0, 2):
         total = acc[p, x, piece_of(z)].astype(F32)
@@ -799,30 +1077,51 @@
         flows[p] = send(
             res.at[c, p, own_half], res.at[c, p, own_half], pair(9, p), beside
         )
+    dense_flows = []
+    for i, (own, landing, n, size, base) in enumerate(parts_of):
+        for d in range(1, GROUPS):
+            dense_spread[i, d].wait()
+        place = dense_res.at[c, pl.ds(pl.multiple_of(base, 16), n)]
+        dense_flows.append(send(place, place, d_pair(7, i), beside))
     for copy in shorts:
         copy.wait()
     small_out[...] = vec_in[4] + vec_in[5] + (vec_in[6] + vec_in[7])
     for p in (1, 0, 2):
         flows[p].wait()
         flows[p] = send(res.at[c, p], res.at[c, p], pair(10, p), sibling)
+    for i, (own, landing, n, size, base) in enumerate(parts_of):
+        dense_flows[i].wait()
+        place = dense_res.at[c, pl.ds(i * a_cut, 2 * n)]
+        dense_flows[i] = send(place, place, d_pair(8, i), sibling)
     for p in (1, 0, 2):
         flows[p].wait()
-    done = pltpu.make_async_copy(res, out, last_sem)
-    done.start()
-    done.wait()
-
-
-def sum_grads(grads, small):
+    for copy in dense_flows:
+        copy.wait()
+    done = [
+        pltpu.make_async_copy(res, out, last_sem.at[0]),
+        pltpu.make_async_copy(dense_res, dense_out, last_sem.at[1]),
+    ]
+    for copy in done:
+        copy.start()
+    for copy in done:
+        copy.wait()
+
+
+def sum_grads(grads, small, ready):
     parts, _, _, rows, lanes = grads.shape
+    a, b = ready[0].shape, ready[2].shape
+    total = 2 * (a[0] + b[0])
+    most = max(a[0], b[0])
     dma = pltpu.SemaphoreType.DMA
     return pl.pallas_call(
         sum_kernel,
         out_shape=[
             jax.ShapeDtypeStruct((2, parts, rows, lanes), BF16),
+            jax.ShapeDtypeStruct((2, total, a[1]), BF16),
             jax.ShapeDtypeStruct(small.shape, F32),
         ],
-        in_specs=[VMEM, VMEM],
-        out_specs=[ANY, VMEM],
+        in_specs=[VMEM] * 6,
+        out_specs=[ANY, ANY, VMEM],
         scratch_shapes=[
             pltpu.VMEM((parts, 2, rows, lanes), BF16),
             pltpu.VMEM((parts, 2, rows, lanes), BF16),
@@ -832,16 +1131,21 @@
             pltpu.VMEM((2, parts, rows, lanes), BF16),
             pltpu.VMEM(small.shape, F32),
             pltpu.VMEM((8, *small.shape), F32),
+            pltpu.VMEM((2, most, a[1]), BF16),
+            pltpu.VMEM((GROUPS, a[0] // GROUPS, a[1]), BF16),
+            pltpu.VMEM((GROUPS, b[0] // GROUPS, b[1]), BF16),
+            pltpu.VMEM((2, total, a[1]), BF16),
             dma((2, 11, parts)),
             dma((2, 6)),
-            dma,
+            dma((2, 9, 2)),
+            dma((2,)),
         ],
         compiler_params=pltpu.CompilerParams(
-            vmem_limit_bytes=40 * 2**20, collective_id=2, has_side_effects=True
+            vmem_limit_bytes=48 * 2**20, collective_id=2, has_side_effects=True
         ),
         cost_estimate=cost(50),
         name="sum_grads",
-    )(grads, small)
+    )(grads, small, *ready)
 
 
 def pick(table, index):
@@ -984,29 +1288,47 @@
             held += [flip(piece, m) for piece in held]
         pieces.append(held)
 
-    attended, lses, dense_out = [], [], []
+    fused = per_plane == 4
+    attended, lses = [], []
     for s in range(seqs):
         o, lse = attend(scalars[s], queries[s], pieces[s])
         attended.append(o.reshape(queries[s].shape))
         lses.append(lse)
-    for s in range(seqs):
-        o4 = turn(attended[s].reshape(GROUPS, rows, -1))
-        dense_out.append(
-            dense(
-                row_counts[s], o4, tokens[s], teacher[s], narrow[2:], wide_vec, dense_weights
+    if fused:
+        fours = [a.reshape(GROUPS, rows, -1) for a in attended]
+        found = middle(
+            jnp.concatenate(row_counts), tokens, teacher, narrow[2:], wide_vec, fours, dense_weights
+        )
+        output, firsts, sums, wide_sums, a_own, a_give, b_own, b_give = found[:8]
+        heads_grad = [g.reshape(queries[0].shape) for g in found[8:]]
+        first_grads = [firsts[s] for s in range(seqs)]
+        a_in, b_in = across(a_give), flip(b_give, 2)
+    else:
+        dense_out = []
+        for s in range(seqs):
+            o4 = turn(attended[s].reshape(GROUPS, rows, -1))
+            dense_out.append(
+                dense(
+                    row_counts[s], o4, tokens[s], teacher[s], narrow[2:], wide_vec, dense_weights
+                )
             )
-        )
-    saved = [d[3:9] for d in dense_out]
-    heads_grad = [turn(d[2]).reshape(queries[s].shape) for s, d in enumerate(dense_out)]
-    g_dense = dense_grads(saved)
-
-    dense_sums = [reduced_dense(g) for g in g_dense]
-    fused = per_plane == 4
+        output = jnp.stack([d[0] for d in dense_out])
+        first_grads = [d[1] for d in dense_out]
+        heads_grad = [turn(d[2]).reshape(queries[s].shape) for s, d in enumerate(dense_out)]
+        sums = sum(d[9] for d in dense_out)
+        wide_sums = sum(d[10] for d in dense_out)
+        dense_sums = [reduced_dense(g) for g in dense_grads([d[3:9] for d in dense_out])]
+
     dqs, dkvs = [], []
     for s in range(seqs):
         found = attend_back(
             scalars[s], queries[s], heads_grad[s], attended[s], lses[s], pieces[s]
         )
+        if fused and s == 0:
+            a_in, b_in, *found = lax.optimization_barrier((a_in, b_in, *found))
+            a_keep, a_give, b_keep, b_give = halve(a_own, a_in, b_own, b_in)
+            a_more, b_more = flip(a_give, 2), across(b_give)
+            scalars[1], a_keep, b_keep = lax.optimization_barrier((scalars[1], a_keep, b_keep))
         dqs.append(found[0].reshape(GROUPS, rows, -1))
         dkvs.append([piece.reshape(GROUPS, rows, -1) for piece in found[1:]])
     if fused:
@@ -1022,7 +1344,7 @@
             dkvs[s] = turn(held[0])
     tokens_grad, g_qkv, sums_qkv = project_grads(
         tokens,
-        [d[1] for d in dense_out],
+        first_grads,
         dqs,
         dkvs,
         query_weight,
@@ -1032,8 +1354,6 @@
         second_qkv,
     )
 
-    sums = sum(d[9] for d in dense_out)
-    wide_sums = sum(d[10] for d in dense_out)
     loss_part = jnp.sum(sums[6])
     valid = sum(jnp.sum(r) for r in row_counts).astype(F32)
     small = jnp.concatenate(
@@ -1045,29 +1365,32 @@
         ]
     )
     small = jnp.pad(small, (0, -small.shape[0] % 1024)).reshape(-1, 128)
+    hidden = wide_vec.shape[1]
     if fused:
-        qkv, small = sum_grads(g_qkv, small)
+        qkv, total, small = sum_grads(g_qkv, small, (a_keep, a_more, b_keep, b_more))
+        out_grad = total[:, :half].swapaxes(0, 1).reshape(half, width)
+        inner_grad = total[:, half : half + hidden // 2].reshape(2, hidden // width, half, half)
+        inner_grad = inner_grad.transpose(2, 1, 0, 3).reshape(half, hidden)
+        outer_grad = total[:, half + hidden // 2 :].swapaxes(0, 1).reshape(hidden // 2, width)
+        dense_sums = (out_grad, inner_grad, outer_grad)
     else:
         small = lax.psum(small, ("ctx", "wa"))
         qkv = reduced(jnp.moveaxis(g_qkv, (2, 1), (0, 1)).reshape(4, 3, -1, 128))
-    *dense_sums, small = lax.optimization_barrier((*dense_sums, small))
+        dense_sums = [paired(g).reshape(-1, g.shape[-1]) for g in dense_sums]
     small = small.reshape(-1)
     qkv = qkv.reshape(6, 3, half, 128).astype(F32)
     query_grad, key_grad, value_grad = (
         qkv[:, i].swapaxes(0, 1).reshape(half, width) for i in range(3)
     )
-    out_grad, inner_grad, outer_grad = (
-        paired(g).reshape(-1, g.shape[-1]).astype(F32) for g in dense_sums
-    )
+    out_grad, inner_grad, outer_grad = (g.astype(F32) for g in dense_sums)
 
     def vector(start, length):
         return lax.dynamic_slice_in_dim(small, start + x * (length // 2), length // 2, 0)
 
     end = 8 * width
-    hidden = wide_vec.shape[1]
     loss = small[end + hidden] / (small[end + hidden + 1] * width)
     return (
-        jnp.stack([d[0] for d in dense_out]),
+        output,
         tokens_grad,
         query_grad,
         vector(6 * width, width),

time: 620 us -> 583 us (0.940)
  waiting for transfers between devices: 118 us -> 72.6 us
  Pallas kernels: 317 us -> 358 us
  other arithmetic: 28.4 us -> 13.7 us
  between operations: 18.5 us -> 5.41 us
  starting transfers between devices: 52.4 us -> 42.1 us
    pallas_call x1, Pallas kernels: 73.9 us -> 139 us  [sum_grads(): pl.pallas_call(sum_kernel, out_shape=[jax.ShapeDtypeStruct((2, parts, row...]
    psum x1 -> x0, waiting for transfers between devices: 62.3 us -> none  [reduced_dense(): return lax.psum(mine, 'ctx', axis_index_groups=cores)]
    pallas_call x2, Pallas kernels: 82.2 us -> 53.7 us  [attend_back(): pl.pallas_call(functools.partial(backward_kernel, 4, 4, len(pieces)), out...]
    all_to_all x8 -> x4, starting transfers between devices: 36.7 us -> 17.1 us  [turn(): return lax.all_to_all(value, 'ctx', 0, 0, axis_index_groups=lines)]
    convert_element_type x0 -> x4, local copies, waits for them, and re-layouts: none -> 19.3 us  [shards(): out_grad, inner_grad, outer_grad = (g.astype(F32) for g in dense_sums)]
    pallas_call x3 -> x2, Pallas kernels: 45.5 us -> 58.9 us  [the longest x1 54.7 us: middle(): pl.pallas_call(functools.partial(middle_kernel, seqs), out_shape=[jax.Sha...]
    all_to_all x8 -> x4, waiting for transfers between devices: 25.9 us -> 36.5 us  [turn(): return lax.all_to_all(value, 'ctx', 0, 0, axis_index_groups=lines)]
    squeeze x5 -> x1, local copies, waits for them, and re-layouts: 11.6 us -> 1.24 us  [shards(): first_grads = [firsts[s] for s in range(seqs)]]
  transfers between devices with their start and end apart: 33 -> 23, of which waited for: 8 -> 7; matrix products, arithmetic and copies ran while one was open for 13% -> 5% of each run, Pallas kernels for 51% -> 27%
where the time goes in v3:
time: 583 us; the launch traced here: 572 us
  Pallas kernels  358 us (61%)
  local copies, waits for them, and re-layouts  80.6 us (14%)
  waiting for transfers between devices  72.6 us (12%)
  starting transfers between devices  42.1 us (7%)
  other arithmetic  13.7 us (2%)
    pallas_call x1, Pallas kernels, sum_grads(): pl.pallas_call(sum_kernel, out_shape=[jax.ShapeDtypeStruct((2, parts, row...  139 us
    pallas_call x1, Pallas kernels, return_grads(): pl.pallas_call(functools.partial(return_kernel, seqs), out_shape=shapes,...  57.5 us
    pallas_call x1, Pallas kernels, middle(): pl.pallas_call(functools.partial(middle_kernel, seqs), out_shape=[jax.Sha...  54.7 us
    pallas_call x2, Pallas kernels, attend_back(): pl.pallas_call(functools.partial(backward_kernel, 4, 4, len(pieces)), out...  53.7 us
    unnamed x112, local copies, waits for them, and re-layouts  39 us
    all_to_all x4, waiting for transfers between devices, turn(): return lax.all_to_all(value, 'ctx', 0, 0, axis_index_groups=lines)  36.5 us
    ppermute x7, waiting for transfers between devices, across(): return lax.ppermute(value, 'wa', [(0, 1), (1, 0)])  36.1 us
    pallas_call x2, Pallas kernels, attend(): pl.pallas_call(functools.partial(forward_kernel, 8, 2, len(pieces)), out_...  32 us
  transfers between devices with their start and end apart: 23, of which 7 were waited for; matrix products, arithmetic and copies ran while one was open for 5% of the time, Pallas kernels for 27%

profile of v3, /device:TPU:0, one launch (start us, length us, event | category | flops | bytes accessed | tf_op | source)
XLA Modules:
  0.0 572.2 jit_solution(15859295111035438117)
XLA Ops:
  3.0 3.0 collective-permute-start.1
  6.0 19.6 %collective-permute-done.1.first.refs_9_ = bf16[576,768]{1,0:T(8,128)(2,1)S(1)} collective-permute-done((bf16[576,768]{1,0:T(8,128)(2,1)S(1)}, bf16[576,768]{1,0:T(8,128)(2,1)S(1)}, u32[]{:S(2)}, u32[]{:S(2)}) %collective-permute-start.1) | collective-permute-done | bytes 884768 | tf_op jit(solution)/shard_map/ppermute | solution.py:1189
  27.4 1.8 collective-permute-start
  29.3 2.0 collective-permute-done
  32.9 6.6 %project.1 = (bf16[4,256,192]{2,1,0:T(8,128)(2,1)}, bf16[4,256,384]{2,1,0:T(8,128)(2,1)}, bf16[4,256,192]{2,1,0:T(8,128)(2,1)}, bf16[4,256,384]{2,1,0:T(8,128)(2,1)}) custom-call(bf16[2,256,768]{2,1,0:T(8,128)(2,1)} %tok.5, f32[8,768]{1,0:T(8,128)} %bitcast.107, bf16[384,768]{1,0:T(8,128)(2,1)} %refs_6_.1, bf16[384,768]{1,0:T(8,128)(2,1)} %refs_7_.1, ...), custom_call_target="tpu_custom_call" | custom-call | flops 5750000128 | bytes 1048576 | tf_op jit(solution)/shard_map/project/pallas_call | solution.py:97
  39.6 5.3 all-to-all-start.3
  44.9 1.6 collective-permute-start.9
  47.8 16.7 %all-to-all-done.3 = bf16[4,256,384]{2,1,0:T(8,128)(2,1)} async-done(((bf16[4,256,384]{2,1,0:T(8,128)(2,1)}), bf16[4,256,384]{2,1,0:T(8,128)(2,1)}, u32[]{:S(2)}, u32[]{:S(2)}) %all-to-all-start.3) | async-done | bytes 786464 | tf_op jit(solution)/shard_map/all_to_all | solution.py:1197
  64.5 3.5 all-to-all-start.1
  68.0 1.6 collective-permute-start.11
  70.8 1.6 collective-permute-start.6
  72.3 1.9 fusion.9
  75.6 2.0 copy.74
  77.6 9.9 %all-to-all-done.1 = bf16[4,256,384]{2,1,0:T(8,128)(2,1)S(1)} async-done(((bf16[4,256,384]{2,1,0:T(8,128)(2,1)}), bf16[4,256,384]{2,1,0:T(8,128)(2,1)S(1)}, u32[]{:S(2)}, u32[]{:S(2)}) %all-to-all-start.1) | async-done | bytes 786464 | tf_op jit(solution)/shard_map/all_to_all | solution.py:1197
  88.4 3.5 all-to-all-start.2
  92.0 3.1 collective-permute-done.11.refs_6_
  95.1 1.5 collective-permute-start.13
  96.6 1.9 concatenate.38.sc
  98.5 1.9 concatenate.36.sc
  100.6 1.9 fusion.11
  103.9 1.6 collective-permute-start.3
  106.2 2.0 copy.72
  108.2 4.9 all-to-all-start
  115.4 9.9 %all-to-all-done = bf16[4,256,192]{1,2,0:T(8,128)(2,1)S(1)} async-done(((bf16[4,256,192]{1,2,0:T(8,128)(2,1)}), bf16[4,256,192]{1,2,0:T(8,128)(2,1)S(1)}, u32[]{:S(2)}, u32[]{:S(2)}) %all-to-all-start) | async-done | bytes 393248 | tf_op jit(solution)/shard_map/all_to_all | solution.py:1197
  127.3 20.3 %attend.3 = (bf16[1024,192]{1,0:T(8,128)(2,1)}, f32[3,8,1024]{2,1,0:T(8,128)}) custom-call(s32[48]{0:T(128)} %concatenate.38.sc, bf16[8,128,192]{2,1,0:T(8,128)(2,1)} %bitcast.100, bf16[8,128,384]{2,1,0:T(8,128)(2,1)} %bitcast.12.rest_0_, bf16[8,128,384]{2,1,0:T(8,128)(2,1)} %collective-permute-done.6.rest_1_, ...), custom_call_target="tpu_custom_call" | custom-call | flops 23000000512 | bytes 1048576 | tf_op jit(solution)/shard_map/attend/pallas_call | solution.py:217
  148.8 11.6 %attend.2 = (bf16[1024,192]{1,0:T(8,128)(2,1)}, f32[3,8,1024]{2,1,0:T(8,128)}) custom-call(s32[48]{0:T(128)} %concatenate.36.sc, bf16[8,128,192]{2,1,0:T(8,128)(2,1)} %bitcast.102, bf16[8,128,384]{2,1,0:T(8,128)(2,1)} %bitcast.97, bf16[8,128,384]{2,1,0:T(8,128)(2,1)} %collective-permute-done.3.rest_1_, bf16[8,128,384]{2,1,0:T(8,128)(2,1)} %copy-done.39, ...), custom_call_target="tpu_custom_call" | custom-call | flops 23000000512 | bytes 1048576 | tf_op jit(solution)/shard_map/attend/pallas_call | solution.py:217
  161.2 54.7 %middle.1 = (bf16[2,256,768]{2,1,0:T(8,128)(2,1)}, f32[2,256,768]{2,1,0:T(8,128)}, f32[8,768]{1,0:T(8,128)}, f32[1,3072]{1,0:T(1,128)}, bf16[1664,384]{1,0:T(8,1...) custom-call(s32[4]{0:T(128)} %pad_add_fusion.sc, ...), custom_call_target="tpu_custom_call" | custom-call | flops 69000003584 | bytes 1048576 | tf_op jit(solution)/shard_map/middle/pallas_call | solution.py:897
  216.5 6.5 %collective-permute-start.15 = (bf16[1664,384]{1,0:T(8,128)(2,1)}, bf16[1664,384]{1,0:T(8,128)(2,1)}, u32[]{:S(2)}, u32[]{:S(2)}) collective-permute-start(bf16[1664,384]{1,0:T(8,128)(2,1)} %get-tuple-element.84), channel_id=1, source_target_pairs={{0,1},{1,0},{2,3},{3,2},{4,5},{5,4},{6,7},{7,6},{8,9},{9,8},{10,11... | collective-permute-start | bytes 3833864 | tf_op jit(solution)/shard_map/ppermute | solution.py:1189
  223.0 14.8 %attend_back.2 = (bf16[8,128,192]{2,1,0:T(8,128)(2,1)}, bf16[8,128,384]{2,1,0:T(8,128)(2,1)}, bf16[8,128,384]{2,1,0:T(8,128)(2,1)}, bf16[8,128,384]{2,1,0:T(8,128)(2,1)}, bf16[8,128,384]{2,1,0:T(8,128)(2,1)}) custom-call(s32[48]{0:T(128)} %concatenate.36.sc, bf16[8,128,192]{2,1,0:T(8,128)(2,1)} %bitcast.103, bf16[8,128,192]{2,1,0:T(8,128)(2,1)} %bitcast.117, ...), custom_call_target="tpu_custom_call" | custom-call | flops 51749998592 | bytes 1048576 | tf_op jit(solution)/shard_map/attend_back/pallas_call | solution.py:334
  240.2 11.3 %collective-permute-done.15.a_in = bf16[1664,384]{1,0:T(8,128)(2,1)} collective-permute-done((bf16[1664,384]{1,0:T(8,128)(2,1)}, bf16[1664,384]{1,0:T(8,128)(2,1)}, u32[]{:S(2)}, u32[]{:S(2)}) %collective-permute-start.15) | collective-permute-done | bytes 1277984 | tf_op jit(solution)/shard_map/ppermute | solution.py:1189
  252.7 4.2 halve.1
  256.9 3.5 collective-permute-start.18
  260.9 38.9 %attend_back.3 = (bf16[8,128,192]{2,1,0:T(8,128)(2,1)}, bf16[8,128,384]{2,1,0:T(8,128)(2,1)}, bf16[8,128,384]{2,1,0:T(8,128)(2,1)}, bf16[8,128,384]{2,1,0:T(8,128)(2,1)}, bf16[8,128,384]{2,1,0:T(8,128)(2,1)}) custom-call(s32[48]{0:T(128)} %concatenate.38.sc, bf16[8,128,192]{2,1,0:T(8,128)(2,1)} %bitcast.101, bf16[8,128,192]{2,1,0:T(8,128)(2,1)} %bitcast.114, ...), custom_call_target="tpu_custom_call" | custom-call | flops 51749998592 | bytes 1048576 | tf_op jit(solution)/shard_map/attend_back/pallas_call | solution.py:334
  305.5 57.5 %return_grads.1 = (bf16[4,256,192]{2,1,0:T(8,128)(2,1)S(1)}, bf16[4,256,384]{2,1,0:T(8,128)(2,1)S(1)}, bf16[4,256,192]{2,1,0:T(8,128)(2,1)S(1)}, bf16[4,256,384]{2,1,0:T(8,128)(2,1)S(1)}) custom-call(bf16[4,256,192]{2,1,0:T(8,128)(2,1)S(1)} %bitcast.88, bf16[4,256,384]{2,1,0:T(8,128)(2,1)S(1)} %bitcast.80, bf16[4,256,384]{2,1,0:T(8,128)(2,1)S(1)} %bitcast.81, ...), custom_call_target="tpu_custom_call" | custom-call | flops 80499998720 | bytes 1048576 | tf_op jit(solution)/shard_map/return_grads/pallas_call | solution.py:694
  366.4 10.2 %project_grads.1 = (f32[2,256,768]{2,1,0:T(8,128)}, bf16[3,2,2,1152,128]{4,3,2,1,0:T(8,128)(2,1)}, f32[8,768]{1,0:T(8,128)}) custom-call(bf16[2,256,768]{2,1,0:T(8,128)(2,1)} %tok.5, f32[256,768]{1,0:T(8,128)} %get-tuple-element.194.refs_0_, f32[256,768]{1,0:T(8,128)} %get-tuple-element.193.refs_1_, bf16[4,256,192]{2,1,0:T(8,128)(2,1)} %copy-done.14, ...), custom_call_target="tpu_custom_call" | custom-call | flops 11500000256 | bytes 1048576 | tf_op jit(solution)/shard_map/project_grads/pallas_call | solution.py:574
  380.3 138.9 %sum_grads.1 = (bf16[2,3,1152,128]{3,2,1,0:T(8,128)(2,1)S(1)}, bf16[2,3456,384]{2,1,0:T(8,128)(2,1)}, f32[80,128]{1,0:T(8,128)S(1)}) custom-call(bf16[3,2,2,1152,128]{4,3,2,1,0:T(8,128)(2,1)} %get-tuple-element.117.grads, f32[80,128]{1,0:T(8,128)S(1)} %pad_bitcast_fusion.small, bf16[832,384]{1,0:T(8,128)(2,1)S(1)} %copy-done.11, ...), custom_call_target="tpu_custom_call" | custom-call | flops 57500000256 | bytes 1048576 | tf_op jit(solution)/shard_map/sum_grads/pallas_call | solution.py:1116
  519.2 5.1 convert_bitcast_fusion.1
  524.3 2.2 convert_bitcast_fusion.2
  527.4 5.8 %copy.80 = f32[384,4,2,384]{3,2,1,0:T(2,128)} copy(f32[384,4,2,384]{3,0,1,2:T(8,128)S(1)} %convert_bitcast_fusion) | data formatting | bytes 9437184 | tf_op jit(solution)/shard_map/convert_element_type | solution.py:1385
  533.2 7.0 %reshape.331 = f32[384,3072]{1,0:T(8,128)} reshape(f32[384,4,2,384]{3,2,1,0:T(2,128)} %copy.80) | data formatting | bytes 9437184 | tf_op jit(solution)/shard_map/convert_element_type | solution.py:1385
  540.2 6.1 %copy.81 = f32[1536,2,384]{0,2,1:T(8,128)} copy(f32[1536,2,384]{2,0,1:T(8,128)} %get-tuple-element.188) | data formatting | bytes 9437184 | tf_op jit(solution)/shard_map/convert_element_type | solution.py:1385
  546.3 6.0 %copy.86 = f32[1536,768]{1,0:T(8,128)} copy(f32[1536,768]{0,1:T(8,128)} %bitcast.90) | data formatting | bytes 9437184
  552.3 1.8 fusion.12
  554.1 2.7 copy.87
  556.8 2.7 copy.82
  560.9 2.7 copy.83
  563.9 1.4 copy.84
  565.7 1.4 copy.85
  (171 shorter events, 40.3 us)
Async XLA Ops:
  1.7 24.0 %copy-start.28 = (bf16[384]{0:T(512)(128)(2,1)S(1)}, bf16[384]{0:T(512)(128)(2,1)}, u32[]{:S(2)}) copy-start(bf16[384]{0:T(512)(128)(2,1)} %param.25) | copy-start | bytes 2308
  1.7 24.2 %copy-start.29 = (bf16[384]{0:T(512)(128)(2,1)S(1)}, bf16[384]{0:T(512)(128)(2,1)}, u32[]{:S(2)}) copy-start(bf16[384]{0:T(512)(128)(2,1)} %param.28) | copy-start | bytes 2308
  1.7 24.4 %copy-start.30 = (bf16[384]{0:T(512)(128)(2,1)S(1)}, bf16[384]{0:T(512)(128)(2,1)}, u32[]{:S(2)}) copy-start(bf16[384]{0:T(512)(128)(2,1)} %param.30) | copy-start | bytes 2308
  1.7 24.6 %copy-start.31 = (bf16[384]{0:T(512)(128)(2,1)S(1)}, bf16[384]{0:T(512)(128)(2,1)}, u32[]{:S(2)}) copy-start(bf16[384]{0:T(512)(128)(2,1)} %param.31) | copy-start | bytes 2308
  1.7 24.8 %copy-start.32 = (bf16[384]{0:T(512)(128)(2,1)S(1)}, bf16[384]{0:T(512)(128)(2,1)}, u32[]{:S(2)}) copy-start(bf16[384]{0:T(512)(128)(2,1)} %param.32) | copy-start | bytes 2308
  1.7 25.0 %copy-start.33 = (bf16[384]{0:T(512)(128)(2,1)S(1)}, bf16[384]{0:T(512)(128)(2,1)}, u32[]{:S(2)}) copy-start(bf16[384]{0:T(512)(128)(2,1)} %param.36) | copy-start | bytes 2308
  1.7 25.3 %copy-start.34 = (bf16[384]{0:T(512)(128)(2,1)S(1)}, bf16[384]{0:T(512)(128)(2,1)}, u32[]{:S(2)}) copy-start(bf16[384]{0:T(512)(128)(2,1)} %param.37) | copy-start | bytes 2308
  1.7 25.5 %copy-start.35 = (bf16[384]{0:T(512)(128)(2,1)S(1)}, bf16[384]{0:T(512)(128)(2,1)}, u32[]{:S(2)}) copy-start(bf16[384]{0:T(512)(128)(2,1)} %param.38) | copy-start | bytes 2308
  1.8 25.7 %copy-start.26 = (bf16[1536]{0:T(1024)(128)(2,1)S(1)}, bf16[1536]{0:T(1024)(128)(2,1)}, u32[]{:S(2)}) copy-start(bf16[1536]{0:T(1024)(128)(2,1)} %param.34) | copy-start | bytes 9220
  3.0 22.7 %collective-permute-start.1 = (bf16[576,768]{1,0:T(8,128)(2,1)S(1)}, bf16[576,768]{1,0:T(8,128)(2,1)S(1)}, u32[]{:S(2)}, u32[]{:S(2)}) collective-permute-start(bf16[576,768]{1,0:T(8,128)(2,1)S(1)} %pad_maximum_fusion), channel_id=1, source_target_pairs={{0,1},{1,0},{2,3},{3,2},{4,5},{5,4},{6,7},{7,6},{8,9},{9,8},{10,11... | collective-permute-start | bytes 2654216 | tf_op jit(solution)/shard_map/ppermute | solution.py:1189
  25.6 6.4 %copy-start.37 = (bf16[576,768]{1,0:T(8,128)(2,1)}, bf16[576,768]{1,0:T(8,128)(2,1)S(1)}, u32[]{:S(2)}) copy-start(bf16[576,768]{1,0:T(8,128)(2,1)S(1)} %collective-permute-done.1.first.refs_9_) | copy-start | bytes 2654212
  25.6 6.4 %collective-permute-start.2 = (bf16[576,768]{1,0:T(8,128)(2,1)S(1)}, bf16[576,768]{1,0:T(8,128)(2,1)S(1)}, u32[]{:S(2)}, u32[]{:S(2)}) collective-permute-start(bf16[576,768]{1,0:T(8,128)(2,1)S(1)} %collective-permute-done.1.first.refs_9_), channel_id=1, source_target_pairs={{0,2},{2,0},{4,6},{6,4},{8,10},{10,8},{12,14},{14,12},{16,18},{18,... | collective-permute-start | bytes 2654216 | tf_op jit(solution)/shard_map/ppermute | solution.py:1192
  27.4 3.8 collective-permute-start
  39.5 5.3 copy-start.22
  39.6 24.9 %all-to-all-start.3 = ((bf16[4,256,384]{2,1,0:T(8,128)(2,1)}), bf16[4,256,384]{2,1,0:T(8,128)(2,1)}, u32[]{:S(2)}, u32[]{:S(2)}) async-start(bf16[4,256,384]{2,1,0:T(8,128)(2,1)} %get-tuple-element.77), calls=%async_computation.3 | async-start | bytes 1572864 | tf_op jit(solution)/shard_map/all_to_all | solution.py:1197
  44.8 24.8 %copy-start.27 = (s32[2]{0:T(128)S(1)}, s32[2]{0:T(128)}, u32[]{:S(2)}) copy-start(s32[2]{0:T(128)} %param.22) | copy-start | bytes 28
  44.8 25.3 %copy-start.44 = (s32[4]{0:T(128)S(1)}, s32[4]{0:T(128)}, u32[]{:S(2)}) copy-start(s32[4]{0:T(128)} %constant.138.clone) | copy-start | bytes 52
  44.9 25.4 %copy-start.43 = (s32[32]{0:T(128)S(1)}, s32[32]{0:T(128)}, u32[]{:S(2)}) copy-start(s32[32]{0:T(128)} %param.23) | copy-start | bytes 388
  44.9 23.1 %collective-permute-start.9 = (bf16[192,768]{1,0:T(8,128)(2,1)S(1)}, bf16[192,768]{1,0:T(8,128)(2,1)S(1)}, u32[]{:S(2)}, u32[]{:S(2)}) collective-permute-start(bf16[192,768]{1,0:T(8,128)(2,1)S(1)} %constant_dynamic-slice_fusion.2), channel_id=1, source_target_pairs={{0,1},{1,0},{2,3},{3,2},{4,5},{5,4},{6,7},{7,6},{8,9},{9,8},{10,11... | collective-permute-start | bytes 884744 | tf_op jit(solution)/shard_map/ppermute | solution.py:1189
  64.5 23.1 %all-to-all-start.1 = ((bf16[4,256,384]{2,1,0:T(8,128)(2,1)}), bf16[4,256,384]{2,1,0:T(8,128)(2,1)S(1)}, u32[]{:S(2)}, u32[]{:S(2)}) async-start(bf16[4,256,384]{2,1,0:T(8,128)(2,1)} %get-tuple-element.74), calls=%async_computation.1 | async-start | bytes 1572864 | tf_op jit(solution)/shard_map/all_to_all | solution.py:1197
  68.0 46.4 %copy-start.41 = (bf16[192,768]{1,0:T(8,128)(2,1)}, bf16[192,768]{1,0:T(8,128)(2,1)S(1)}, u32[]{:S(2)}) copy-start(bf16[192,768]{1,0:T(8,128)(2,1)S(1)} %collective-permute-done.9.refs_3_) | copy-start | bytes 884740
  68.0 27.1 %collective-permute-start.11 = (bf16[192,3072]{1,0:T(8,128)(2,1)S(1)}, bf16[192,3072]{1,0:T(8,128)(2,1)}, u32[]{:S(2)}, u32[]{:S(2)}) collective-permute-start(bf16[192,3072]{1,0:T(8,128)(2,1)S(1)} %constant_dynamic-slice_fusion.1), channel_id=1, source_target_pairs={{0,1},{1,0},{2,3},{3,2},{4,5},{5,4},{6,7},{7,6},{8,9},{9,8},{10,11... | collective-permute-start | bytes 3538952 | tf_op jit(solution)/shard_map/ppermute | solution.py:1189
  70.8 34.7 %collective-permute-start.6 = (bf16[8,128,384]{2,1,0:T(8,128)(2,1)}, bf16[8,128,384]{2,1,0:T(8,128)(2,1)}, u32[]{:S(2)}, u32[]{:S(2)}) collective-permute-start(bf16[8,128,384]{2,1,0:T(8,128)(2,1)} %bitcast.12.rest_0_), channel_id=1, source_target_pairs={{0,4},{2,6},{4,0},{6,2},{8,12},{10,14},{12,8},{14,10},{16,20},{18,... | collective-permute-start | bytes 2359304 | tf_op jit(solution)/shard_map/ppermute | solution.py:1192
  88.4 19.8 %all-to-all-start.2 = ((bf16[4,256,192]{1,2,0:T(8,128)(2,1)}), bf16[4,256,192]{1,2,0:T(8,128)(2,1)S(1)}, u32[]{:S(2)}, u32[]{:S(2)}) async-start(bf16[4,256,192]{1,2,0:T(8,128)(2,1)} %copy.74), calls=%async_computation.2 | async-start | bytes 786432 | tf_op jit(solution)/shard_map/all_to_all | solution.py:1197
  95.1 31.2 %collective-permute-start.13 = (bf16[768,768]{1,0:T(8,128)(2,1)S(1)}, bf16[768,768]{1,0:T(8,128)(2,1)}, u32[]{:S(2)}, u32[]{:S(2)}) collective-permute-start(bf16[768,768]{1,0:T(8,128)(2,1)S(1)} %constant_dynamic-slice_fusion), channel_id=1, source_target_pairs={{0,1},{1,0},{2,3},{3,2},{4,5},{5,4},{6,7},{7,6},{8,9},{9,8},{10,11... | collective-permute-start | bytes 3538952 | tf_op jit(solution)/shard_map/ppermute | solution.py:1189
  103.8 22.5 %collective-permute-start.7 = (bf16[8,128,384]{2,1,0:T(8,128)(2,1)}, bf16[8,128,384]{2,1,0:T(8,128)(2,1)}, u32[]{:S(2)}, u32[]{:S(2)}) collective-permute-start(bf16[8,128,384]{2,1,0:T(8,128)(2,1)} %bitcast.12.rest_0_), channel_id=1, source_target_pairs={{0,2},{2,0},{4,6},{6,4},{8,10},{10,8},{12,14},{14,12},{16,18},{18,... | collective-permute-start | bytes 2359304 | tf_op jit(solution)/shard_map/ppermute | solution.py:1192
  103.9 22.9 %collective-permute-start.3 = (bf16[8,128,384]{2,1,0:T(8,128)(2,1)}, bf16[8,128,384]{2,1,0:T(8,128)(2,1)}, u32[]{:S(2)}, u32[]{:S(2)}) collective-permute-start(bf16[8,128,384]{2,1,0:T(8,128)(2,1)} %bitcast.96), channel_id=1, source_target_pairs={{0,4},{2,6},{4,0},{6,2},{8,12},{10,14},{12,8},{14,10},{16,20},{18,... | collective-permute-start | bytes 2359304 | tf_op jit(solution)/shard_map/ppermute | solution.py:1192
  105.5 21.4 %collective-permute-start.8 = (bf16[8,128,384]{2,1,0:T(8,128)(2,1)}, bf16[8,128,384]{2,1,0:T(8,128)(2,1)}, u32[]{:S(2)}, u32[]{:S(2)}) collective-permute-start(bf16[8,128,384]{2,1,0:T(8,128)(2,1)} %collective-permute-done.6.rest_1_), channel_id=1, source_target_pairs={{0,2},{2,0},{4,6},{6,4},{8,10},{10,8},{12,14},{14,12},{16,18},{18,... | collective-permute-start | bytes 2359304 | tf_op jit(solution)/shard_map/ppermute | solution.py:1192
  108.2 18.1 %copy-start.20 = (bf16[4,256,384]{2,1,0:T(8,128)(2,1)S(1)}, bf16[4,256,384]{2,1,0:T(8,128)(2,1)}, u32[]{:S(2)}) copy-start(bf16[4,256,384]{2,1,0:T(8,128)(2,1)} %copy-done.19) | copy-start | bytes 2359300
  108.2 17.1 %all-to-all-start = ((bf16[4,256,192]{1,2,0:T(8,128)(2,1)}), bf16[4,256,192]{1,2,0:T(8,128)(2,1)S(1)}, u32[]{:S(2)}, u32[]{:S(2)}) async-start(bf16[4,256,192]{1,2,0:T(8,128)(2,1)} %copy.72), calls=%async_computation | async-start | bytes 786432 | tf_op jit(solution)/shard_map/all_to_all | solution.py:1197
  114.3 46.1 %collective-permute-start.10 = (bf16[192,768]{1,0:T(8,128)(2,1)S(1)}, bf16[192,768]{1,0:T(8,128)(2,1)S(1)}, u32[]{:S(2)}, u32[]{:S(2)}) collective-permute-start(bf16[192,768]{1,0:T(8,128)(2,1)S(1)} %collective-permute-done.9.refs_3_), channel_id=1, source_target_pairs={{0,2},{2,0},{4,6},{6,4},{8,10},{10,8},{12,14},{14,12},{16,18},{18,... | collective-permute-start | bytes 884744 | tf_op jit(solution)/shard_map/ppermute | solution.py:1192
  126.3 34.2 %collective-permute-start.12 = (bf16[192,3072]{1,0:T(8,128)(2,1)}, bf16[192,3072]{1,0:T(8,128)(2,1)}, u32[]{:S(2)}, u32[]{:S(2)}) collective-permute-start(bf16[192,3072]{1,0:T(8,128)(2,1)} %collective-permute-done.11.refs_6_), channel_id=1, source_target_pairs={{0,2},{2,0},{4,6},{6,4},{8,10},{10,8},{12,14},{14,12},{16,18},{18,... | collective-permute-start | bytes 3538952 | tf_op jit(solution)/shard_map/ppermute | solution.py:1192
  126.3 21.4 %collective-permute-start.4 = (bf16[8,128,384]{2,1,0:T(8,128)(2,1)S(1)}, bf16[8,128,384]{2,1,0:T(8,128)(2,1)S(1)}, u32[]{:S(2)}, u32[]{:S(2)}) collective-permute-start(bf16[8,128,384]{2,1,0:T(8,128)(2,1)S(1)} %bitcast.99), channel_id=1, source_target_pairs={{0,2},{2,0},{4,6},{6,4},{8,10},{10,8},{12,14},{14,12},{16,18},{18,... | collective-permute-start | bytes 2359304 | tf_op jit(solution)/shard_map/ppermute | solution.py:1192
  126.8 33.7 %collective-permute-start.14 = (bf16[768,768]{1,0:T(8,128)(2,1)}, bf16[768,768]{1,0:T(8,128)(2,1)}, u32[]{:S(2)}, u32[]{:S(2)}) collective-permute-start(bf16[768,768]{1,0:T(8,128)(2,1)} %collective-permute-done.13.refs_9_), channel_id=1, source_target_pairs={{0,2},{2,0},{4,6},{6,4},{8,10},{10,8},{12,14},{14,12},{16,18},{18,... | collective-permute-start | bytes 3538952 | tf_op jit(solution)/shard_map/ppermute | solution.py:1192
  126.9 20.8 %collective-permute-start.5 = (bf16[8,128,384]{2,1,0:T(8,128)(2,1)}, bf16[8,128,384]{2,1,0:T(8,128)(2,1)S(1)}, u32[]{:S(2)}, u32[]{:S(2)}) collective-permute-start(bf16[8,128,384]{2,1,0:T(8,128)(2,1)} %collective-permute-done.3.rest_1_), channel_id=1, source_target_pairs={{0,2},{2,0},{4,6},{6,4},{8,10},{10,8},{12,14},{14,12},{16,18},{18,... | collective-permute-start | bytes 2359304 | tf_op jit(solution)/shard_map/ppermute | solution.py:1192
  215.9 35.7 %collective-permute-start.16 = (bf16[2,896,384]{2,1,0:T(8,128)(2,1)}, bf16[2,896,384]{2,1,0:T(8,128)(2,1)S(1)}, u32[]{:S(2)}, u32[]{:S(2)}) collective-permute-start(bf16[2,896,384]{2,1,0:T(8,128)(2,1)} %get-tuple-element.85), channel_id=1, source_target_pairs={{0,4},{2,6},{4,0},{6,2},{8,12},{10,14},{12,8},{14,10},{16,20},{18,... | collective-permute-start | bytes 4128776 | tf_op jit(solution)/shard_map/ppermute | solution.py:1192
  216.5 35.1 %collective-permute-start.15 = (bf16[1664,384]{1,0:T(8,128)(2,1)}, bf16[1664,384]{1,0:T(8,128)(2,1)}, u32[]{:S(2)}, u32[]{:S(2)}) collective-permute-start(bf16[1664,384]{1,0:T(8,128)(2,1)} %get-tuple-element.84), channel_id=1, source_target_pairs={{0,1},{1,0},{2,3},{3,2},{4,5},{5,4},{6,7},{7,6},{8,9},{9,8},{10,11... | collective-permute-start | bytes 3833864 | tf_op jit(solution)/shard_map/ppermute | solution.py:1189
  223.0 14.8 %copy-start.24 = (f32[8,768]{1,0:T(8,128)S(1)}, f32[8,768]{1,0:T(8,128)}, u32[]{:S(2)}) copy-start(f32[8,768]{1,0:T(8,128)} %get-tuple-element.118) | copy-start | bytes 73732
  223.0 16.0 %copy-start.18 = (f32[2,256,768]{2,1,0:T(8,128)S(1)}, f32[2,256,768]{2,1,0:T(8,128)}, u32[]{:S(2)}) copy-start(f32[2,256,768]{2,1,0:T(8,128)} %get-tuple-element.83) | copy-start | bytes 4718596
  256.9 121.2 %collective-permute-start.18 = (bf16[896,384]{1,0:T(8,128)(2,1)}, bf16[896,384]{1,0:T(8,128)(2,1)S(1)}, u32[]{:S(2)}, u32[]{:S(2)}) collective-permute-start(bf16[896,384]{1,0:T(8,128)(2,1)} %get-tuple-element.124), channel_id=1, source_target_pairs={{0,1},{1,0},{2,3},{3,2},{4,5},{5,4},{6,7},{7,6},{8,9},{9,8},{10,11... | collective-permute-start | bytes 2064392 | tf_op jit(solution)/shard_map/ppermute | solution.py:1189
  260.4 117.7 %collective-permute-start.17 = (bf16[832,384]{1,0:T(8,128)(2,1)}, bf16[832,384]{1,0:T(8,128)(2,1)S(1)}, u32[]{:S(2)}, u32[]{:S(2)}) collective-permute-start(bf16[832,384]{1,0:T(8,128)(2,1)} %get-tuple-element.122), channel_id=1, source_target_pairs={{0,4},{2,6},{4,0},{6,2},{8,12},{10,14},{12,8},{14,10},{16,20},{18,... | collective-permute-start | bytes 1916936 | tf_op jit(solution)/shard_map/ppermute | solution.py:1192
  260.9 39.0 %copy-start = (bf16[8,128,384]{2,1,0:T(8,128)(2,1)S(1)}, bf16[8,128,384]{2,1,0:T(8,128)(2,1)}, u32[]{:S(2)}) copy-start(bf16[8,128,384]{2,1,0:T(8,128)(2,1)} %get-tuple-element.94) | copy-start | bytes 2359300
  260.9 39.0 %copy-start.1 = (bf16[8,128,384]{2,1,0:T(8,128)(2,1)S(1)}, bf16[8,128,384]{2,1,0:T(8,128)(2,1)}, u32[]{:S(2)}) copy-start(bf16[8,128,384]{2,1,0:T(8,128)(2,1)} %get-tuple-element.95) | copy-start | bytes 2359300
  260.9 39.0 %copy-start.2 = (bf16[8,128,384]{2,1,0:T(8,128)(2,1)S(1)}, bf16[8,128,384]{2,1,0:T(8,128)(2,1)}, u32[]{:S(2)}) copy-start(bf16[8,128,384]{2,1,0:T(8,128)(2,1)} %get-tuple-element.96) | copy-start | bytes 2359300
  260.9 39.0 %copy-start.3 = (bf16[8,128,384]{2,1,0:T(8,128)(2,1)S(1)}, bf16[8,128,384]{2,1,0:T(8,128)(2,1)}, u32[]{:S(2)}) copy-start(bf16[8,128,384]{2,1,0:T(8,128)(2,1)} %get-tuple-element.97) | copy-start | bytes 2359300
  260.9 39.0 %copy-start.8 = (bf16[8,128,192]{2,1,0:T(8,128)(2,1)S(1)}, bf16[8,128,192]{2,1,0:T(8,128)(2,1)}, u32[]{:S(2)}) copy-start(bf16[8,128,192]{2,1,0:T(8,128)(2,1)} %get-tuple-element.93) | copy-start | bytes 1179652
  366.4 11.0 %copy-start.23 = (f32[4608]{0:T(1024)S(1)}, f32[4608]{0:T(1024)}, u32[]{:S(2)}) copy-start(f32[4608]{0:T(1024)} %reshape.322) | copy-start | bytes 55300
  366.4 11.0 %copy-start.25 = (f32[1,3072]{1,0:T(1,128)S(1)}, f32[1,3072]{1,0:T(1,128)}, u32[]{:S(2)}) copy-start(f32[1,3072]{1,0:T(1,128)} %get-tuple-element.120) | copy-start | bytes 36868
  (20 other events, 25.0 us)

commit v4 on v3

--- a/solution.py
+++ b/solution.py
@@ -49,7 +49,14 @@
     ]
 
 
-def project_kernel(tok, vec, wq, wk, wv, first, second, *rest):
+def valid_rows(sc, s, rows):
+    row = lax.broadcasted_iota(jnp.int32, (rows, 1), 0)
+    first = jnp.where(row < sc[2 * s], 1.0, 0.0)
+    later = jnp.where(row - BLK < sc[2 * s + 1], 1.0, 0.0)
+    return jnp.where(row < BLK, first, later)
+
+
+def project_kernel(sc, tok, vec, wq, wk, wv, first, second, *rest):
     seqs, rows, width = tok.shape
     outs, (full, sems) = rest[: 2 * seqs], rest[2 * seqs :]
     quarter = wq.shape[0] // 2
@@ -65,12 +72,13 @@
     flat = tok[...].reshape(seqs * rows, width)
     per = width // GROUPS
     heads = per // DH
+    valid = jnp.concatenate([valid_rows(sc, s, rows) for s in range(seqs)], 0) > 0.0
     for copy in copies[1]:
         copy.wait()
-    keys = dot(flat, full[1]).astype(BF16)
+    keys = jnp.where(valid, dot(flat, full[1]), 0.0).astype(BF16)
     for copy in copies[2]:
         copy.wait()
-    values = (dot(flat, full[2]) + vec[1:2, :]).astype(BF16)
+    values = jnp.where(valid, dot(flat, full[2]) + vec[1:2, :], 0.0).astype(BF16)
     for s in range(seqs):
         rs = slice(s * rows, (s + 1) * rows)
         for g in range(GROUPS):
@@ -88,7 +96,7 @@
             outs[2 * s][g] = queries[rs, g * per : (g + 1) * per]
 
 
-def project(tok, vec, wq, wk, wv, first, second):
+def project(sc, tok, vec, wq, wk, wv, first, second):
     seqs, rows, width = tok.shape
     per = width // GROUPS
     shapes = [
@@ -97,13 +105,13 @@
     return pl.pallas_call(
         project_kernel,
         out_shape=shapes,
-        in_specs=[VMEM, VMEM] + [ANY] * 5,
+        in_specs=[SMEM, VMEM, VMEM] + [ANY] * 5,
         out_specs=[VMEM] * len(shapes),
         scratch_shapes=[pltpu.VMEM((3, width, width), BF16), pltpu.SemaphoreType.DMA((9,))],
         compiler_params=ROOM,
         cost_estimate=cost(5),
         name="project",
-    )(tok, vec, wq, wk, wv, first, second)
+    )(sc, tok, vec, wq, wk, wv, first, second)
 
 
 def load_pieces(pieces, kv, sems):
@@ -518,10 +526,14 @@
     )(*[member for group in saved for member in group])
 
 
-def project_grads_kernel(seqs, tok, *refs):
-    fgs, refs = refs[:seqs], refs[seqs:]
-    dqs, refs = refs[:seqs], refs[seqs:]
-    dkvs, refs = refs[:seqs], refs[seqs:]
+def project_grads_kernel(seqs, paired, sc, tok, *refs):
+    count = 2 if paired else 2 * seqs
+    if paired:
+        fg, refs = refs[0], refs[1:]
+        fgs = [fg.at[s] for s in range(seqs)]
+    else:
+        fgs, refs = refs[:seqs], refs[seqs:]
+    grads_in, refs = refs[:count], refs[count:]
     wq, wk, wv, first, second, tg, grads, sums, full, sems = refs
     rows, width = tok.shape[1:]
     per = width // GROUPS
@@ -533,23 +545,27 @@
         copies += weight_copies(full.at[i], own, first.at[part], second.at[part], sems, 3 * i)
     for copy in copies:
         copy.start()
-    dq = jnp.concatenate(
-        [jnp.concatenate([dqs[s][g] for g in range(GROUPS)], 1) for s in range(seqs)], 0
-    )
-    pair = [
-        jnp.concatenate([dkvs[s][g] for g in range(GROUPS)], 1) for s in range(seqs)
-    ]
-    pair = jnp.concatenate(pair, 0)
-    halves = [
-        jnp.concatenate(
-            [
-                pair[:, n * 128 + part * DH : n * 128 + (part + 1) * DH]
-                for n in range(GROUPS * heads)
-            ],
-            1,
-        )
-        for part in (0, 1)
-    ]
+
+    def head(i, s, g, h):
+        if paired:
+            if i == 0:
+                return grads_in[0][h, g, :, s * DH : (s + 1) * DH]
+            return grads_in[1][h * seqs + s, g, :, (i - 1) * DH : i * DH]
+        if i == 0:
+            return grads_in[s][g, :, h * DH : (h + 1) * DH]
+        start = h * 128 + (i - 1) * DH
+        return grads_in[seqs + s][g, :, start : start + DH]
+
+    def whole(i):
+        each = [
+            jnp.concatenate([head(i, s, g, h) for g in range(GROUPS) for h in range(heads)], 1)
+            for s in range(seqs)
+        ]
+        return jnp.concatenate(each, 0)
+
+    valid = jnp.concatenate([valid_rows(sc, s, rows) for s in range(seqs)], 0) > 0.0
+    dq = whole(0)
+    halves = [jnp.where(valid, whole(i), jnp.zeros((), BF16)) for i in (1, 2)]
     flat = tok[...].reshape(seqs * rows, width)
     for copy in copies:
         copy.wait()
@@ -569,22 +585,22 @@
     sums[2:8, :] = jnp.zeros((6, width), F32)
 
 
-def project_grads(tok, fgs, dqs, dkvs, wq, wk, wv, first, second):
+def project_grads(sc, tok, fgs, grads, wq, wk, wv, first, second, paired):
     seqs, rows, width = tok.shape
     return pl.pallas_call(
-        functools.partial(project_grads_kernel, seqs),
+        functools.partial(project_grads_kernel, seqs, paired),
         out_shape=[
             jax.ShapeDtypeStruct(tok.shape, F32),
             jax.ShapeDtypeStruct((3, 2, 2, 3 * (width // 2), 128), BF16),
             jax.ShapeDtypeStruct((8, width), F32),
         ],
-        in_specs=[VMEM] * (1 + 3 * seqs) + [ANY] * 5,
+        in_specs=[SMEM] + [VMEM] * (1 + len(fgs) + len(grads)) + [ANY] * 5,
         out_specs=[VMEM] * 3,
         scratch_shapes=[pltpu.VMEM((3, width, width), BF16), pltpu.SemaphoreType.DMA((9,))],
         compiler_params=ROOM,
         cost_estimate=cost(10),
         name="project_grads",
-    )(tok, *fgs, *dqs, *dkvs, wq, wk, wv, first, second)
+    )(sc, tok, *fgs, *grads, wq, wk, wv, first, second)
 
 
 MESH = pl.DeviceIdType.MESH
@@ -623,95 +639,253 @@
     return (left.astype(F32) + right.astype(F32)).astype(BF16)
 
 
-def return_kernel(seqs, *refs):
-    ins, outs = refs[: 5 * seqs], refs[5 * seqs : 7 * seqs]
-    held, from_core, from_y, local_sem, q_sem, c_sem, y_sem, z_sem = refs[7 * seqs :]
+def back_kernel(seqs, *refs):
+    per_seq = 8
+    ins = [refs[per_seq * s : per_seq * (s + 1)] for s in range(seqs)]
+    a_own, a_give, b_own, b_give, rq, rkv, dense_out, *refs = refs[per_seq * seqs :]
+    q_v, do_v, o_v, lse_v, kv_v, both, dkv, dq, delta, obuf, qbuf = refs[:11]
+    from_core, from_y, a_v, b_v, a_in, b_in, a2, b2, a2_in, b2_in = refs[11:21]
+    az_in, bz_in, dres, in_sem, c_sem, y_sem, z_sem, q_sem, l_sem, x_sem, dz_sem, g_sem = refs[21:]
     z, y, c, x = position()
-    sibling, beside = device(z, y, 1 - c, x), device(z, 1 - y, c, x)
+    sibling, beside, over = device(z, y, 1 - c, x), device(z, 1 - y, c, x), device(z, y, c, 1 - x)
     line = [None] + [device(z ^ d, y, c, x) for d in range(1, GROUPS)]
-    greet([sibling, beside] + line[1:])
+    greet([sibling, beside, over] + line[1:])
+
+    def pair(sems, *index):
+        return sems.at[(0, *index)], sems.at[(1, *index)]
+
+    flow = {}
+    flow["a"] = send(a_give, a_in, pair(x_sem, 0), over)
+    flow["b"] = send(b_give, b_in, pair(x_sem, 1), beside)
+    loads = []
+    for s in range(seqs):
+        q, do, o, lse, *pieces = ins[s]
+        n = pieces[0].shape[0]
+        targets = [q_v.at[s], do_v.at[s], o_v.at[s], lse_v.at[s]]
+        targets += [kv_v.at[s, pl.ds(i * n, n)] for i in range(len(pieces))]
+        group = [
+            pltpu.make_async_copy(src, dst, in_sem.at[s, i])
+            for i, (src, dst) in enumerate(zip(ins[s], targets))
+        ]
+        for copy in group:
+            copy.start()
+        loads.append(group)
+    own_loads = [
+        pltpu.make_async_copy(a_own, a_v, l_sem.at[0]),
+        pltpu.make_async_copy(b_own, b_v, l_sem.at[1]),
+    ]
+    for copy in own_loads:
+        copy.start()
+
+    rows = q_v.shape[1]
+    heads = q_v.shape[2] // DH
+    keys = kv_v.shape[1]
+    tile, ktile = rows // 2, 1024
+    quarter = keys // 4
+    chunk = quarter // GROUPS
+    ones = jnp.ones((8, DH), BF16)
+    level = jnp.where(lax.broadcasted_iota(jnp.int32, (1, 128), 1) < DH, LN2, 1.0)
     waits = []
-    for s in range(seqs):
+
+    def group_rows(g):
+        return pl.ds(pl.multiple_of(g * chunk, chunk), chunk)
+
+    def core_stage(u):
+        flow["c", u] = send(
+            obuf.at[u, pl.ds(2 * quarter, 2 * quarter)], from_core.at[u], pair(c_sem, u), sibling
+        )
+
+    def y_stage(u):
+        flow["c", u].wait()
+        second = pl.ds(quarter, quarter)
+        obuf[u, second] = add_low(obuf[u, second], from_core[u, second])
+        flow["y", u] = send(obuf.at[u, second], from_y.at[u], pair(y_sem, u), beside)
+        obuf[u, 0:quarter] = add_low(obuf[u, 0:quarter], from_core[u, 0:quarter])
+
+    def z_stage(u):
+        flow["y", u].wait()
+        obuf[u, 0:quarter] = add_low(obuf[u, 0:quarter], from_y[u])
         for d in range(1, GROUPS):
-            sems = q_sem.at[0, s, d], q_sem.at[1, s, d]
-            waits.append(send(ins[5 * s].at[z ^ d], outs[2 * s].at[z], sems, line[d]))
-    core = {}
-    for s in range(seqs):
-        for d in range(GROUPS):
-            for i in (1, 0):
-                sems = c_sem.at[0, s, d, i], c_sem.at[1, s, d, i]
-                core[s, d, i] = send(
-                    ins[5 * s + 3 + i].at[z ^ d], from_core.at[s, i, z ^ d], sems, sibling
-                )
-    local = {}
-    for s in range(seqs):
-        for i in (1, 0):
-            local[s, i] = pltpu.make_async_copy(
-                ins[5 * s + 1 + i], held.at[s, i], local_sem.at[s, i]
-            )
-            local[s, i].start()
-        own = pltpu.make_async_copy(ins[5 * s].at[z], outs[2 * s].at[z], local_sem.at[s, 2])
+            src = obuf.at[u, group_rows(z ^ d)]
+            waits.append(send(src, rkv.at[u, z], pair(z_sem, u, d), line[d]))
+        own = pltpu.make_async_copy(obuf.at[u, group_rows(z)], rkv.at[u, z], z_sem.at[0, u, 0])
         own.start()
         waits.append(own)
-    order = [1, 2, 3, 0]
-    to_y = {}
-    for s in range(seqs):
-        local[s, 1].wait()
-        local[s, 0].wait()
-        for d in order:
-            core[s, d, 1].wait()
-            held[s, 1, z ^ d] = add_low(held[s, 1, z ^ d], from_core[s, 1, z ^ d])
-            sems = y_sem.at[0, s, d], y_sem.at[1, s, d]
-            to_y[s, d] = send(held.at[s, 1, z ^ d], from_y.at[s, z ^ d], sems, beside)
-            core[s, d, 0].wait()
-            held[s, 0, z ^ d] = add_low(held[s, 0, z ^ d], from_core[s, 0, z ^ d])
-    for s in range(seqs):
-        for d in order:
-            to_y[s, d].wait()
-            held[s, 0, z ^ d] = add_low(held[s, 0, z ^ d], from_y[s, z ^ d])
-            if d == 0:
-                own = pltpu.make_async_copy(
-                    held.at[s, 0, z], outs[2 * s + 1].at[z], local_sem.at[s, 3]
-                )
-                own.start()
-                waits.append(own)
-            else:
-                sems = z_sem.at[0, s, d], z_sem.at[1, s, d]
-                waits.append(send(held.at[s, 0, z ^ d], outs[2 * s + 1].at[z], sems, line[d]))
+
+    def q_stage(h):
+        for d in range(1, GROUPS):
+            waits.append(send(qbuf.at[h, z ^ d], rq.at[h, z], pair(q_sem, h, d), line[d]))
+        own = pltpu.make_async_copy(qbuf.at[h, z], rq.at[h, z], q_sem.at[0, h, 0])
+        own.start()
+        waits.append(own)
+
+    a_half, b_half = a2.shape[1], b2.shape[1]
+
+    def dense_second():
+        for copy in own_loads:
+            copy.wait()
+        flow["a"].wait()
+        for slot, which in ((0, y), (1, 1 - y)):
+            part = pl.ds(pl.multiple_of(which * a_half, 16), a_half)
+            a2[slot] = add_low(a_v[part, :], a_in[part, :])
+        flow["a"] = send(a2.at[1], a2_in, pair(x_sem, 2), beside)
+        flow["b"].wait()
+        for slot, which in ((0, x), (1, 1 - x)):
+            b2[slot] = add_low(b_v[which], b_in[which])
+        flow["b"] = send(b2.at[1], b2_in, pair(x_sem, 3), over)
+
+    def dense_third():
+        for i, (name, held, arrived, landing) in enumerate(
+            (("a", a2, a2_in, az_in), ("b", b2, b2_in, bz_in))
+        ):
+            flow[name].wait()
+            held[0] = add_low(held[0], arrived[...])
+            size = held.shape[1] // GROUPS
+            for d in range(1, GROUPS):
+                src = held.at[0, pl.ds(pl.multiple_of((z ^ d) * size, 16), size)]
+                flow["z", i, d] = send(src, landing.at[d], pair(dz_sem, i, d), line[d])
+
+    def dense_fourth():
+        base = 0
+        for i, (held, landing) in enumerate(((a2, az_in), (b2, bz_in))):
+            size = held.shape[1] // GROUPS
+            total = held[0, pl.ds(pl.multiple_of(z * size, 16), size), :].astype(F32)
+            for d in range(1, GROUPS):
+                flow["z", i, d].wait()
+                total += landing[d].astype(F32)
+            place = dres.at[pl.ds(pl.multiple_of(base + z * size, 16), size)]
+            place[...] = total.astype(BF16)
+            for d in range(1, GROUPS):
+                waits.append(send(place, place, pair(g_sem, i, d), line[d]))
+            base += held.shape[1]
+
+    units = [(h, s) for h in range(heads) for s in range(seqs)]
+    slots = {}
+    for u in range(len(units) - 1):
+        slots.setdefault(2 * u + 3, []).append(functools.partial(y_stage, u))
+        slots.setdefault(2 * u + 4, []).append(functools.partial(z_stage, u))
+    slots.setdefault(4, []).append(dense_second)
+    slots.setdefault(6, []).append(dense_third)
+    slots.setdefault(11, []).append(dense_fourth)
+
+    for u, (h, s) in enumerate(units):
+        hs = slice(h * DH, (h + 1) * DH)
+        lanes = slice(h * 128, (h + 1) * 128)
+        if h == 0:
+            for copy in loads[s]:
+                copy.wait()
+        for n in range(2):
+            for work in slots.get(2 * u + n, []):
+                work()
+            part = slice(n * tile, (n + 1) * tile)
+            q, do, o = q_v[s, part, hs], do_v[s, part, hs], o_v[s, part, hs]
+            zero = jnp.zeros_like(q)
+            both[0:tile, :] = jnp.concatenate([q, zero], 1)
+            both[tile : 2 * tile, :] = jnp.concatenate([zero, do], 1)
+            product = do.astype(F32) * o.astype(F32)
+            high = product.astype(BF16)
+            remains = (product - high.astype(F32)).astype(BF16)
+            delta[...] = dot(ones, high, NT) + dot(ones, remains, NT)
+            dq[...] = jnp.zeros_like(dq)
+
+            def step(j, _, u=u, s=s, h=h, n=n, part=part, lanes=lanes):
+                span = pl.ds(pl.multiple_of(j * ktile, ktile), ktile)
+                kv = kv_v[s, span, lanes]
+                b = both[...]
+                found = dot(kv, b, NT)
+                p = jnp.exp2(jnp.minimum(found[:, :tile] - lse_v[s, h, 0:1, part], 1.0))
+                ds = (p * (found[:, tile:] - delta[0:1, :])).astype(BF16)
+                grads = dot(jnp.concatenate([ds, p.astype(BF16)], 1), b)
+                if n == 0:
+                    dkv[span, :] = grads
+                else:
+                    obuf[u, span, :] = ((dkv[span, :] + grads) * level).astype(BF16)
+                dq[...] += dot(ds, kv, TN)
+                return 0
+
+            lax.fori_loop(0, keys // ktile, step, 0)
+            found = (dq[:, :DH] * DH**-0.5).astype(BF16)
+            for i in range(2):
+                qbuf[h, 2 * n + i, :, s * DH : (s + 1) * DH] = found[
+                    i * (tile // 2) : (i + 1) * (tile // 2)
+                ]
+        core_stage(u)
+        if s == seqs - 1:
+            q_stage(h)
+    last = len(units) - 1
+    for n in sorted(n for n in slots if n >= 2 * len(units)):
+        for work in slots[n]:
+            work()
+    y_stage(last)
+    z_stage(last)
     for copy in waits:
         copy.wait()
-
-
-def return_grads(dqs, dkvs):
-    seqs = len(dqs)
-    groups, rows, per = dqs[0].shape
-    args, shapes = [], []
-    for dq, pieces in zip(dqs, dkvs):
-        args += [dq, *pieces]
-        shapes += [jax.ShapeDtypeStruct(dq.shape, BF16), jax.ShapeDtypeStruct(pieces[0].shape, BF16)]
+    done = pltpu.make_async_copy(dres, dense_out, l_sem.at[0])
+    done.start()
+    done.wait()
+
+
+def attend_back_all(seqs_in, ready):
+    seqs = len(seqs_in)
+    q, _, _, lse, piece = seqs_in[0][:5]
+    rows, per = q.shape
+    heads = per // DH
+    units = heads * seqs
+    keys = 4 * piece.shape[0]
+    chunk = rows // GROUPS
+    a, b = ready[0].shape, ready[2].shape
+    a_half, b_half, half = a[0] // 2, b[1], a[1]
     dma = pltpu.SemaphoreType.DMA
-    slab = (groups, rows, 2 * per)
     return pl.pallas_call(
-        functools.partial(return_kernel, seqs),
-        out_shape=shapes,
-        in_specs=[ANY] * len(args),
-        out_specs=[ANY] * len(shapes),
+        functools.partial(back_kernel, seqs),
+        out_shape=[
+            jax.ShapeDtypeStruct((heads, GROUPS, chunk, 128), BF16),
+            jax.ShapeDtypeStruct((units, GROUPS, chunk, 128), BF16),
+            jax.ShapeDtypeStruct((a_half + b_half, half), BF16),
+        ],
+        in_specs=[ANY] * (8 * seqs + 4),
+        out_specs=[ANY] * 3,
         scratch_shapes=[
-            pltpu.VMEM((seqs, 2, *slab), BF16),
-            pltpu.VMEM((seqs, 2, *slab), BF16),
-            pltpu.VMEM((seqs, *slab), BF16),
-            dma((seqs, 4)),
-            dma((2, seqs, groups)),
-            dma((2, seqs, groups, 2)),
-            dma((2, seqs, groups)),
-            dma((2, seqs, groups)),
+            pltpu.VMEM((seqs, rows, per), BF16),
+            pltpu.VMEM((seqs, rows, per), BF16),
+            pltpu.VMEM((seqs, rows, per), BF16),
+            pltpu.VMEM((seqs, *lse.shape), F32),
+            pltpu.VMEM((seqs, keys, 2 * per), BF16),
+            pltpu.VMEM((rows, 128), BF16),
+            pltpu.VMEM((keys, 128), F32),
+            pltpu.VMEM((rows // 2, 128), F32),
+            pltpu.VMEM((8, rows // 2), F32),
+            pltpu.VMEM((units, keys, 128), BF16),
+            pltpu.VMEM((heads, GROUPS, chunk, 128), BF16),
+            pltpu.VMEM((units, keys // 2, 128), BF16),
+            pltpu.VMEM((units, keys // 4, 128), BF16),
+            pltpu.VMEM(a, BF16),
+            pltpu.VMEM(b, BF16),
+            pltpu.VMEM(a, BF16),
+            pltpu.VMEM(b, BF16),
+            pltpu.VMEM((2, a_half, half), BF16),
+            pltpu.VMEM((2, b_half, half), BF16),
+            pltpu.VMEM((a_half, half), BF16),
+            pltpu.VMEM((b_half, half), BF16),
+            pltpu.VMEM((GROUPS, a_half // GROUPS, half), BF16),
+            pltpu.VMEM((GROUPS, b_half // GROUPS, half), BF16),
+            pltpu.VMEM((a_half + b_half, half), BF16),
+            dma((seqs, 8)),
+            dma((2, units)),
+            dma((2, units)),
+            dma((2, units, GROUPS)),
+            dma((2, heads, GROUPS)),
+            dma((2,)),
+            dma((2, 4)),
+            dma((2, 2, GROUPS)),
+            dma((2, 2, GROUPS)),
         ],
         compiler_params=pltpu.CompilerParams(
-            vmem_limit_bytes=40 * 2**20, collective_id=1, has_side_effects=True
+            vmem_limit_bytes=62 * 2**20, collective_id=1, has_side_effects=True
         ),
-        cost_estimate=cost(70),
-        name="return_grads",
-    )(*args)
+        cost_estimate=cost(120),
+        name="attend_back_all",
+    )(*[member for group in seqs_in for member in group], *ready)
 
 
 def middle_stage(s, att, mask, tok, teach, vec, wide_vec, weights, keep, outs, first_done):
@@ -809,13 +983,11 @@
 
     rows = tok.shape[1]
     per = o_in.shape[3]
-    row = lax.broadcasted_iota(jnp.int32, (rows, 1), 0)
     for s in range(seqs):
         for d in range(GROUPS):
             coming[s, d].wait()
         att = jnp.concatenate([o_in[s, g] for g in range(GROUPS)], 1)
-        first, later = (jnp.where(row < sc[2 * s], 1.0, 0.0), jnp.where(row - BLK < sc[2 * s + 1], 1.0, 0.0))
-        mask = jnp.where(row < BLK, first, later)
+        mask = valid_rows(sc, s, rows)
         waits = (lambda: loaded([0]), lambda: loaded([1, 2])) if s == 0 else (lambda: None,) * 2
         found = middle_stage(
             s,
@@ -938,35 +1110,10 @@
     )(sc, tok, teach, vec, wide_vec, *attended, *weights)
 
 
-def halve_kernel(a_own, a_in, b_own, b_in, a_keep, a_give, b_keep, b_give):
-    _, y, _, x = position()
-    half = a_keep.shape[0]
-    for target, which in ((a_keep, y), (a_give, 1 - y)):
-        part = pl.ds(pl.multiple_of(which * half, 16), half)
-        target[...] = add_low(a_own[part, :], a_in[part, :])
-    for target, which in ((b_keep, x), (b_give, 1 - x)):
-        target[...] = add_low(b_own[which], b_in[which])
-
-
-def halve(a_own, a_in, b_own, b_in):
-    a = jax.ShapeDtypeStruct((a_own.shape[0] // 2, a_own.shape[1]), BF16)
-    b = jax.ShapeDtypeStruct(b_own.shape[1:], BF16)
-    return pl.pallas_call(
-        halve_kernel,
-        out_shape=[a, a, b, b],
-        in_specs=[VMEM] * 4,
-        out_specs=[VMEM] * 4,
-        compiler_params=ROOM,
-        cost_estimate=cost(3),
-        name="halve",
-    )(a_own, a_in, b_own, b_in)
-
-
 def sum_kernel(grads, small, *rest):
-    ready, rest = rest[:4], rest[4:]
-    out, dense_out, small_out, *rest = rest
-    acc, from_core, from_x, from_y, from_z, res, vec, vec_in = rest[:8]
-    two, a_in, b_in, dense_res, sems, small_sems, d_sems, last_sem = rest[8:]
+    ready, out, dense_out, small_out, *rest = rest
+    acc, from_core, from_x, from_y, from_z, res, vec, vec_in, dense_res = rest[:9]
+    sems, small_sems, d_sems, last_sem = rest[9:]
     z, y, c, x = position()
     sibling, beside, over = device(z, y, 1 - c, x), device(z, 1 - y, c, x), device(z, y, c, 1 - x)
     line = [None] + [device(z ^ d, y, c, x) for d in range(1, GROUPS)]
@@ -989,23 +1136,14 @@
     core = [
         send(grads.at[p, 1 - c], from_core.at[p], pair(0, p), sibling) for p in range(parts)
     ]
-    a_cut = 2 * ready[0].shape[0]
-    parts_of = []
-    for i, landing in enumerate((a_in, b_in)):
-        keep, other = ready[2 * i], ready[2 * i + 1]
-        n = keep.shape[0]
-        own = two.at[i, 0:n]
-        own[...] = add_low(keep[...], other[...])
-        parts_of.append((own, landing, n, n // GROUPS, i * a_cut + y * n))
-
-    def d_pair(k, i):
-        return d_sems.at[0, k, i], d_sems.at[1, k, i]
-
-    dense_lines = {}
-    for i, (own, landing, n, size, _) in enumerate(parts_of):
-        for d in range(1, GROUPS):
-            src = own.at[pl.ds(pl.multiple_of((z ^ d) * size, 16), size)]
-            dense_lines[i, d] = send(src, landing.at[d], d_pair(d, i), line[d])
+    a_half = cut_of(dense_res.shape[1]) // 2
+    b_half = ready.shape[0] - a_half
+    dense_flows = []
+    for i, (start, n, base) in enumerate(((0, a_half, 0), (a_half, b_half, 2 * a_half))):
+        place = dense_res.at[c, pl.ds(pl.multiple_of(base + y * n, 16), n)]
+        src = ready.at[pl.ds(start, n)]
+        dense_flows.append(send(src, place, (d_sems.at[0, 0, i], d_sems.at[1, 0, i]), beside))
+        place[...] = src[...]
     short = send(small, vec_in.at[0], small_pair(0), sibling)
     flows = []
     for p in range(parts):
@@ -1047,16 +1185,6 @@
     shorts = [
         send(vec, vec_in.at[4 + z], small_pair(2 + d), line[d]) for d in range(1, GROUPS)
     ]
-    dense_spread = {}
-    for i, (own, landing, n, size, base) in enumerate(parts_of):
-        total = own[pl.ds(pl.multiple_of(z * size, 16), size), :].astype(F32)
-        for d in range(1, GROUPS):
-            dense_lines[i, d].wait()
-            total += landing[d].astype(F32)
-        place = dense_res.at[c, pl.ds(pl.multiple_of(base + z * size, 16), size)]
-        place[...] = total.astype(BF16)
-        for d in range(1, GROUPS):
-            dense_spread[i, d] = send(place, place, d_pair(3 + d, i), line[d])
     spread = {}
     for p in (1, 0, 2):
         total = acc[p, x, piece_of(z)].astype(F32)
@@ -1077,22 +1205,16 @@
         flows[p] = send(
             res.at[c, p, own_half], res.at[c, p, own_half], pair(9, p), beside
         )
-    dense_flows = []
-    for i, (own, landing, n, size, base) in enumerate(parts_of):
-        for d in range(1, GROUPS):
-            dense_spread[i, d].wait()
-        place = dense_res.at[c, pl.ds(pl.multiple_of(base, 16), n)]
-        dense_flows.append(send(place, place, d_pair(7, i), beside))
+    for i, (base, n) in enumerate(((0, 2 * a_half), (2 * a_half, 2 * b_half))):
+        dense_flows[i].wait()
+        place = dense_res.at[c, pl.ds(base, n)]
+        dense_flows[i] = send(place, place, (d_sems.at[0, 1, i], d_sems.at[1, 1, i]), sibling)
     for copy in shorts:
         copy.wait()
     small_out[...] = vec_in[4] + vec_in[5] + (vec_in[6] + vec_in[7])
     for p in (1, 0, 2):
         flows[p].wait()
         flows[p] = send(res.at[c, p], res.at[c, p], pair(10, p), sibling)
-    for i, (own, landing, n, size, base) in enumerate(parts_of):
-        dense_flows[i].wait()
-        place = dense_res.at[c, pl.ds(i * a_cut, 2 * n)]
-        dense_flows[i] = send(place, place, d_pair(8, i), sibling)
     for p in (1, 0, 2):
         flows[p].wait()
     for copy in dense_flows:
@@ -1109,18 +1231,16 @@
 
 def sum_grads(grads, small, ready):
     parts, _, _, rows, lanes = grads.shape
-    a, b = ready[0].shape, ready[2].shape
-    total = 2 * (a[0] + b[0])
-    most = max(a[0], b[0])
+    total, half = 2 * ready.shape[0], ready.shape[1]
     dma = pltpu.SemaphoreType.DMA
     return pl.pallas_call(
         sum_kernel,
         out_shape=[
             jax.ShapeDtypeStruct((2, parts, rows, lanes), BF16),
-            jax.ShapeDtypeStruct((2, total, a[1]), BF16),
+            jax.ShapeDtypeStruct((2, total, half), BF16),
             jax.ShapeDtypeStruct(small.shape, F32),
         ],
-        in_specs=[VMEM] * 6,
+        in_specs=[VMEM] * 3,
         out_specs=[ANY, ANY, VMEM],
         scratch_shapes=[
             pltpu.VMEM((parts, 2, rows, lanes), BF16),
@@ -1131,13 +1251,10 @@
             pltpu.VMEM((2, parts, rows, lanes), BF16),
             pltpu.VMEM(small.shape, F32),
             pltpu.VMEM((8, *small.shape), F32),
-            pltpu.VMEM((2, most, a[1]), BF16),
-            pltpu.VMEM((GROUPS, a[0] // GROUPS, a[1]), BF16),
-            pltpu.VMEM((GROUPS, b[0] // GROUPS, b[1]), BF16),
-            pltpu.VMEM((2, total, a[1]), BF16),
+            pltpu.VMEM((2, total, half), BF16),
             dma((2, 11, parts)),
             dma((2, 6)),
-            dma((2, 9, 2)),
+            dma((2, 2, 2)),
             dma((2,)),
         ],
         compiler_params=pltpu.CompilerParams(
@@ -1145,7 +1262,64 @@
         ),
         cost_estimate=cost(50),
         name="sum_grads",
-    )(grads, small, *ready)
+    )(grads, small, ready)
+
+
+def unpack_kernel(qkv, total, *refs):
+    outs, (narrow, inner, outer, sems) = refs[:6], refs[6:]
+    half = qkv.shape[2] // 3
+    blocks = inner.shape[1] // (2 * half)
+    copies = []
+
+    def leave(src, i):
+        copy = pltpu.make_async_copy(src, outs[i], sems.at[i])
+        copy.start()
+        copies.append(copy)
+
+    for k in range(2):
+        cols = slice(k * half, (k + 1) * half)
+        outer[:, cols] = total[k, (1 + blocks) * half :].astype(F32)
+    leave(outer, 5)
+    for k in range(2):
+        for t in range(blocks):
+            cols = slice((2 * t + k) * half, (2 * t + k + 1) * half)
+            inner[:, cols] = total[k, (1 + t) * half : (2 + t) * half].astype(F32)
+    leave(inner, 4)
+    for i in range(3):
+        for k in range(2):
+            for p in range(3):
+                cols = slice((3 * k + p) * 128, (3 * k + p + 1) * 128)
+                narrow[i, :, cols] = qkv[k, p, i * half : (i + 1) * half].astype(F32)
+        leave(narrow.at[i], i)
+    for k in range(2):
+        narrow[3, :, k * half : (k + 1) * half] = total[k, 0:half].astype(F32)
+    leave(narrow.at[3], 3)
+    for copy in copies:
+        copy.wait()
+
+
+def unpack(qkv, total, hidden):
+    half = total.shape[2]
+    narrow = jax.ShapeDtypeStruct((half, 2 * half), F32)
+    return pl.pallas_call(
+        unpack_kernel,
+        out_shape=[narrow] * 4
+        + [
+            jax.ShapeDtypeStruct((half, hidden), F32),
+            jax.ShapeDtypeStruct((hidden // 2, 2 * half), F32),
+        ],
+        in_specs=[VMEM] * 2,
+        out_specs=[ANY] * 6,
+        scratch_shapes=[
+            pltpu.VMEM((4, half, 2 * half), F32),
+            pltpu.VMEM((half, hidden), F32),
+            pltpu.VMEM((hidden // 2, 2 * half), F32),
+            pltpu.SemaphoreType.DMA((6,)),
+        ],
+        compiler_params=ROOM,
+        cost_estimate=cost(10),
+        name="unpack",
+    )(qkv, total)
 
 
 def pick(table, index):
@@ -1276,8 +1450,9 @@
         scalars.append(jnp.concatenate([head, query_order, key_order]))
         row_counts.append(jnp.clip(lengths[s] - own_pos * BLK, 0, BLK))
 
+    counts = jnp.concatenate(row_counts)
     projected = project(
-        tokens, narrow, query_weight, key_weight, value_weight, first_qkv, second_qkv
+        counts, tokens, narrow, query_weight, key_weight, value_weight, first_qkv, second_qkv
     )
     queries, pieces = [], []
     for s in range(seqs):
@@ -1297,12 +1472,11 @@
     if fused:
         fours = [a.reshape(GROUPS, rows, -1) for a in attended]
         found = middle(
-            jnp.concatenate(row_counts), tokens, teacher, narrow[2:], wide_vec, fours, dense_weights
+            counts, tokens, teacher, narrow[2:], wide_vec, fours, dense_weights
         )
         output, firsts, sums, wide_sums, a_own, a_give, b_own, b_give = found[:8]
         heads_grad = [g.reshape(queries[0].shape) for g in found[8:]]
-        first_grads = [firsts[s] for s in range(seqs)]
-        a_in, b_in = across(a_give), flip(b_give, 2)
+        ready = (a_own, a_give, b_own, b_give)
     else:
         dense_out = []
         for s in range(seqs):
@@ -1319,39 +1493,44 @@
         wide_sums = sum(d[10] for d in dense_out)
         dense_sums = [reduced_dense(g) for g in dense_grads([d[3:9] for d in dense_out])]
 
-    dqs, dkvs = [], []
-    for s in range(seqs):
-        found = attend_back(
-            scalars[s], queries[s], heads_grad[s], attended[s], lses[s], pieces[s]
+    if fused:
+        flat_rows = (GROUPS * rows, width // GROUPS)
+        rq, rkv, ready = attend_back_all(
+            [
+                [
+                    *(a.reshape(flat_rows) for a in (queries[s], heads_grad[s], attended[s])),
+                    lses[s],
+                    *(piece.reshape(-1, piece.shape[2]) for piece in pieces[s]),
+                ]
+                for s in range(seqs)
+            ],
+            ready,
         )
-        if fused and s == 0:
-            a_in, b_in, *found = lax.optimization_barrier((a_in, b_in, *found))
-            a_keep, a_give, b_keep, b_give = halve(a_own, a_in, b_own, b_in)
-            a_more, b_more = flip(a_give, 2), across(b_give)
-            scalars[1], a_keep, b_keep = lax.optimization_barrier((scalars[1], a_keep, b_keep))
-        dqs.append(found[0].reshape(GROUPS, rows, -1))
-        dkvs.append([piece.reshape(GROUPS, rows, -1) for piece in found[1:]])
-    if fused:
-        returned = return_grads(dqs, dkvs)
-        dqs, dkvs = returned[0::2], returned[1::2]
+        first_grads, grads = [firsts], [rq, rkv]
     else:
+        dqs, dkvs = [], []
         for s in range(seqs):
-            dqs[s] = turn(dqs[s])
-            held = dkvs[s]
+            found = attend_back(
+                scalars[s], queries[s], heads_grad[s], attended[s], lses[s], pieces[s]
+            )
+            dqs.append(turn(found[0].reshape(GROUPS, rows, -1)))
+            held = [piece.reshape(GROUPS, rows, -1) for piece in found[1:]]
             for m in reversed(masks):
                 n = len(held) // 2
                 held = [add_low(mine, flip(theirs, m)) for mine, theirs in zip(held[:n], held[n:])]
-            dkvs[s] = turn(held[0])
+            dkvs.append(turn(held[0]))
+        grads = dqs + dkvs
     tokens_grad, g_qkv, sums_qkv = project_grads(
+        counts,
         tokens,
         first_grads,
-        dqs,
-        dkvs,
+        grads,
         query_weight,
         key_weight,
         value_weight,
         first_qkv,
         second_qkv,
+        fused,
     )
 
     loss_part = jnp.sum(sums[6])
@@ -1367,22 +1546,21 @@
     small = jnp.pad(small, (0, -small.shape[0] % 1024)).reshape(-1, 128)
     hidden = wide_vec.shape[1]
     if fused:
-        qkv, total, small = sum_grads(g_qkv, small, (a_keep, a_more, b_keep, b_more))
-        out_grad = total[:, :half].swapaxes(0, 1).reshape(half, width)
-        inner_grad = total[:, half : half + hidden // 2].reshape(2, hidden // width, half, half)
-        inner_grad = inner_grad.transpose(2, 1, 0, 3).reshape(half, hidden)
-        outer_grad = total[:, half + hidden // 2 :].swapaxes(0, 1).reshape(hidden // 2, width)
-        dense_sums = (out_grad, inner_grad, outer_grad)
+        qkv, total, small = sum_grads(g_qkv, small, ready)
+        query_grad, key_grad, value_grad, out_grad, inner_grad, outer_grad = unpack(
+            qkv, total, hidden
+        )
     else:
         small = lax.psum(small, ("ctx", "wa"))
         qkv = reduced(jnp.moveaxis(g_qkv, (2, 1), (0, 1)).reshape(4, 3, -1, 128))
-        dense_sums = [paired(g).reshape(-1, g.shape[-1]) for g in dense_sums]
+        out_grad, inner_grad, outer_grad = (
+            paired(g).reshape(-1, g.shape[-1]).astype(F32) for g in dense_sums
+        )
+        qkv = qkv.reshape(6, 3, half, 128).astype(F32)
+        query_grad, key_grad, value_grad = (
+            qkv[:, i].swapaxes(0, 1).reshape(half, width) for i in range(3)
+        )
     small = small.reshape(-1)
-    qkv = qkv.reshape(6, 3, half, 128).astype(F32)
-    query_grad, key_grad, value_grad = (
-        qkv[:, i].swapaxes(0, 1).reshape(half, width) for i in range(3)
-    )
-    out_grad, inner_grad, outer_grad = (g.astype(F32) for g in dense_sums)
 
     def vector(start, length):
         return lax.dynamic_slice_in_dim(small, start + x * (length // 2), length // 2, 0)

time: 583 us -> 500 us (0.86)
  local copies, waits for them, and re-layouts: 80.6 us -> 28.9 us
  starting transfers between devices: 42.1 us -> 29.3 us
  waiting for transfers between devices: 72.6 us -> 63 us
  other arithmetic: 13.7 us -> 6.08 us
    pallas_call x6 -> x4, Pallas kernels: 132 us -> 194 us  [the longest x1 168 us: attend_back_all(): pl.pallas_call(functools.partial(back_kernel, seqs), out_shape=[jax.Shape...]
    pallas_call x1, Pallas kernels: 139 us -> 77.8 us  [sum_grads(): pl.pallas_call(sum_kernel, out_shape=[jax.ShapeDtypeStruct((2, parts, row...]
    unnamed x112 -> x68, local copies, waits for them, and re-layouts: 39 us -> 10.2 us
    convert_element_type x4 -> x0, local copies, waits for them, and re-layouts: 19.3 us -> none  [shards(): out_grad, inner_grad, outer_grad = (g.astype(F32) for g in dense_sums)]
    ppermute x7 -> x5, waiting for transfers between devices: 36.1 us -> 22.6 us  [across(): return lax.ppermute(value, 'wa', [(0, 1), (1, 0)])]
    ppermute x7 -> x5, starting transfers between devices: 19.4 us -> 7.76 us  [across(): return lax.ppermute(value, 'wa', [(0, 1), (1, 0)])]
    convert_element_type x3 -> x0, other arithmetic: 7.57 us -> none  [shards(): out_grad, inner_grad, outer_grad = (g.astype(F32) for g in dense_sums)]
  transfers between devices with their start and end apart: 23 -> 19, of which waited for: 7 -> 5; matrix products, arithmetic and copies ran while one was open for 5% -> 5% of each run, Pallas kernels for 27% -> 7%
where the time goes in v4:
time: 500 us; the launch traced here: 493 us
  Pallas kernels  361 us (72%)
  waiting for transfers between devices  63 us (13%)
  starting transfers between devices  29.3 us (6%)
  local copies, waits for them, and re-layouts  28.9 us (6%)
  other arithmetic  6.08 us (1%)
  between operations  5.09 us (1%)
    pallas_call x1, Pallas kernels, attend_back_all(): pl.pallas_call(functools.partial(back_kernel, seqs), out_shape=[jax.Shape...  168 us
    pallas_call x1, Pallas kernels, sum_grads(): pl.pallas_call(sum_kernel, out_shape=[jax.ShapeDtypeStruct((2, parts, row...  77.8 us
    pallas_call x1, Pallas kernels, middle(): pl.pallas_call(functools.partial(middle_kernel, seqs), out_shape=[jax.Sha...  54.5 us
    all_to_all x4, waiting for transfers between devices, turn(): return lax.all_to_all(value, 'ctx', 0, 0, axis_index_groups=lines)  40.4 us
    pallas_call x2, Pallas kernels, attend(): pl.pallas_call(functools.partial(forward_kernel, 8, 2, len(pieces)), out_...  34.8 us
    ppermute x5, waiting for transfers between devices, across(): return lax.ppermute(value, 'wa', [(0, 1), (1, 0)])  22.6 us
    all_to_all x4, starting transfers between devices, turn(): return lax.all_to_all(value, 'ctx', 0, 0, axis_index_groups=lines)  17 us
    pallas_call x1, Pallas kernels, project_grads(): pl.pallas_call(functools.partial(project_grads_kernel, seqs, paired), out...  10.7 us
  transfers between devices with their start and end apart: 19, of which 5 were waited for; matrix products, arithmetic and copies ran while one was open for 5% of the time, Pallas kernels for 7%

profile of v4, /device:TPU:0, one launch (start us, length us, event | category | flops | bytes accessed | tf_op | source)
XLA Modules:
  0.0 492.9 jit_solution(11348505947970402909)
XLA Ops:
  0.7 1.0 constant_dynamic-slice_fusion.5
  1.8 1.1 constant_dynamic-slice_fusion.3
  3.0 3.0 collective-permute-start.1
  8.7 17.1 %collective-permute-done.1.first.refs_6_ = bf16[576,768]{1,0:T(8,128)(2,1)S(1)} collective-permute-done((bf16[576,768]{1,0:T(8,128)(2,1)S(1)}, bf16[576,768]{1,0:T(8,128)(2,1)S(1)}, u32[]{:S(2)}, u32[]{:S(2)}) %collective-permute-start.1) | collective-permute-done | bytes 884768 | tf_op jit(solution)/shard_map/ppermute | solution.py:1363
  25.8 1.9 fusion.11
  29.1 0.6 copy.55
  29.7 0.9 copy-done.22
  30.6 6.6 %project.1 = (bf16[4,256,192]{2,1,0:T(8,128)(2,1)}, bf16[4,256,384]{2,1,0:T(8,128)(2,1)}, bf16[4,256,192]{2,1,0:T(8,128)(2,1)}, bf16[4,256,384]{2,1,0:T(8,128)(2,1)}) custom-call(s32[4]{0:T(128)} %pad_add_fusion.sc, bf16[2,256,768]{2,1,0:T(8,128)(2,1)} %tok.5, f32[8,768]{1,0:T(8,128)} %bitcast.57, bf16[384,768]{1,0:T(8,128)(2,1)} %refs_3_.1, ...), custom_call_target="tpu_custom_call" | custom-call | flops 5750000128 | bytes 1048576 | tf_op jit(solution)/shard_map/project/pallas_call | solution.py:105
  37.3 5.3 %all-to-all-start.3 = ((bf16[4,256,384]{2,1,0:T(8,128)(2,1)}), bf16[4,256,384]{2,1,0:T(8,128)(2,1)}, u32[]{:S(2)}, u32[]{:S(2)}) async-start(bf16[4,256,384]{2,1,0:T(8,128)(2,1)} %get-tuple-element.58), calls=%async_computation.3 | async-start | bytes 1572864 | tf_op jit(solution)/shard_map/all_to_all | solution.py:1371
  42.6 1.6 collective-permute-start.9
  44.2 19.3 %all-to-all-done.3 = bf16[4,256,384]{2,1,0:T(8,128)(2,1)} async-done(((bf16[4,256,384]{2,1,0:T(8,128)(2,1)}), bf16[4,256,384]{2,1,0:T(8,128)(2,1)}, u32[]{:S(2)}, u32[]{:S(2)}) %all-to-all-start.3) | async-done | bytes 786464 | tf_op jit(solution)/shard_map/all_to_all | solution.py:1371
  63.5 3.5 all-to-all-start.1
  67.0 1.4 constant_dynamic-slice_fusion.1
  68.3 1.6 collective-permute-start.11
  70.0 1.3 constant_dynamic-slice_fusion
  71.3 1.6 collective-permute-start.6
  72.9 2.0 copy.49
  74.9 11.9 %all-to-all-done.1 = bf16[4,256,384]{2,1,0:T(8,128)(2,1)S(1)} async-done(((bf16[4,256,384]{2,1,0:T(8,128)(2,1)}), bf16[4,256,384]{2,1,0:T(8,128)(2,1)S(1)}, u32[]{:S(2)}, u32[]{:S(2)}) %all-to-all-start.1) | async-done | bytes 786464 | tf_op jit(solution)/shard_map/all_to_all | solution.py:1371
  86.9 3.5 all-to-all-start.2
  90.4 5.4 %collective-permute-done.11.refs_6_ = bf16[192,3072]{1,0:T(8,128)(2,1)} collective-permute-done((bf16[192,3072]{1,0:T(8,128)(2,1)S(1)}, bf16[192,3072]{1,0:T(8,128)(2,1)}, u32[]{:S(2)}, u32[]{:S(2)}) %collective-permute-start.11) | collective-permute-done | bytes 1179680 | tf_op jit(solution)/shard_map/ppermute | solution.py:1363
  95.8 1.5 collective-permute-start.13
  97.5 1.9 fusion.9
  99.8 1.6 collective-permute-start.3
  101.7 1.9 concatenate.38.sc
  103.5 1.9 concatenate.36.sc
  106.7 2.0 copy.47
  108.7 4.8 all-to-all-start
  113.5 0.6 copy.53
  114.1 0.7 slice_bitcast_fusion.1
  114.9 0.6 copy.54
  115.5 1.0 copy.50
  116.6 9.1 %all-to-all-done = bf16[4,256,192]{1,2,0:T(8,128)(2,1)S(1)} async-done(((bf16[4,256,192]{1,2,0:T(8,128)(2,1)}), bf16[4,256,192]{1,2,0:T(8,128)(2,1)S(1)}, u32[]{:S(2)}, u32[]{:S(2)}) %all-to-all-start) | async-done | bytes 393248 | tf_op jit(solution)/shard_map/all_to_all | solution.py:1371
  125.7 1.0 copy.48
  127.7 21.3 %attend.3 = (bf16[1024,192]{1,0:T(8,128)(2,1)}, f32[3,8,1024]{2,1,0:T(8,128)}) custom-call(s32[48]{0:T(128)} %concatenate.38.sc, bf16[8,128,192]{2,1,0:T(8,128)(2,1)} %bitcast.50, bf16[8,128,384]{2,1,0:T(8,128)(2,1)} %bitcast.12.rest_0_, bf16[8,128,384]{2,1,0:T(8,128)(2,1)} %collective-permute-done.6.rest_1_, ...), custom_call_target="tpu_custom_call" | custom-call | flops 23000000512 | bytes 1048576 | tf_op jit(solution)/shard_map/attend/pallas_call | solution.py:225
  149.2 0.8 copy-done.23
  150.3 13.4 %attend.2 = (bf16[1024,192]{1,0:T(8,128)(2,1)}, f32[3,8,1024]{2,1,0:T(8,128)}) custom-call(s32[48]{0:T(128)} %concatenate.36.sc, bf16[8,128,192]{2,1,0:T(8,128)(2,1)} %bitcast.52, bf16[8,128,384]{2,1,0:T(8,128)(2,1)} %bitcast.48, bf16[8,128,384]{2,1,0:T(8,128)(2,1)} %collective-permute-done.3.rest_1_, bf16[8,128,384]{2,1,0:T(8,128)(2,1)} %copy-done.23, ...), custom_call_target="tpu_custom_call" | custom-call | flops 23000000512 | bytes 1048576 | tf_op jit(solution)/shard_map/attend/pallas_call | solution.py:225
  163.7 1.0 copy-done.20
  164.7 54.5 %middle.1 = (bf16[2,256,768]{2,1,0:T(8,128)(2,1)}, f32[2,256,768]{2,1,0:T(8,128)}, f32[8,768]{1,0:T(8,128)}, f32[1,3072]{1,0:T(1,128)}, bf16[1664,384]{1,0:T(8,1...) custom-call(s32[4]{0:T(128)} %pad_add_fusion.sc, ...), custom_call_target="tpu_custom_call" | custom-call | flops 69000003584 | bytes 1048576 | tf_op jit(solution)/shard_map/middle/pallas_call | solution.py:1069
  219.2 167.7 %attend_back_all.1 = (bf16[3,4,256,128]{3,2,1,0:T(8,128)(2,1)}, bf16[6,4,256,128]{3,2,1,0:T(8,128)(2,1)}, bf16[1728,384]{1,0:T(8,128)(2,1)}) custom-call(bf16[1024,192]{1,0:T(8,128)(2,1)} %bitcast.53, bf16[1024,192]{1,0:T(8,128)(2,1)} %bitcast.66, bf16[1024,192]{1,0:T(8,128)(2,1)} %get-tuple-element.56.refs_2_, f32[3,8,1024]{2,1,0:T(8,128)} %get-tuple-element.66.refs_3_, ...), custom_call_target="tpu_custom_call" | custom-call | flops 138000007168 | bytes 1048576 | tf_op jit(solution)/shard_map/attend_back_all/pallas_call | solution.py:839
  387.0 10.7 %project_grads.1 = (f32[2,256,768]{2,1,0:T(8,128)}, bf16[3,2,2,1152,128]{4,3,2,1,0:T(8,128)(2,1)}, f32[8,768]{1,0:T(8,128)}) custom-call(s32[4]{0:T(128)} %pad_add_fusion.sc, bf16[2,256,768]{2,1,0:T(8,128)(2,1)} %tok.5, f32[2,256,768]{2,1,0:T(8,128)} %get-tuple-element.64.refs_0_, bf16[3,4,256,128]{3,2,1,0:T(8,128)(2,1)} %get-tuple-element.73.refs_1_, ...), custom_call_target="tpu_custom_call" | custom-call | flops 11500000256 | bytes 1048576 | tf_op jit(solution)/shard_map/project_grads/pallas_call | solution.py:590
  397.7 0.7 slice.44
  399.0 0.7 concatenate.39
  399.8 77.8 %sum_grads.1 = (bf16[2,3,1152,128]{3,2,1,0:T(8,128)(2,1)S(1)}, bf16[2,3456,384]{2,1,0:T(8,128)(2,1)}, f32[80,128]{1,0:T(8,128)S(1)}) custom-call(bf16[3,2,2,1152,128]{4,3,2,1,0:T(8,128)(2,1)} %get-tuple-element.76.grads, f32[80,128]{1,0:T(8,128)S(1)} %pad_bitcast_fusion.small, bf16[1728,384]{1,0:T(8,128)(2,1)S(1)} %copy-done.1), custom_call_target="tpu_custom_call" | custom-call | flops 57500000256 | bytes 1048576 | tf_op jit(solution)/shard_map/sum_grads/pallas_call | solution.py:1236
  477.5 1.3 copy-done
  479.4 0.7 dynamic_slice.56
  481.4 8.5 %unpack.1 = (f32[384,768]{1,0:T(8,128)}, f32[384,768]{1,0:T(8,128)}, f32[384,768]{1,0:T(8,128)}, f32[384,768]{1,0:T(8,128)}, f32[384,3072]{1,0:T(8,128)}, /*index=5*/f32[1536,768]{1,0:T(8,128)}) custom-call(bf16[2,3,1152,128]{3,2,1,0:T(8,128)(2,1)} %copy-done, bf16[2,3456,384]{2,1,0:T(8,128)(2,1)} %get-tuple-element.82.total), custom_call_target="tpu_custom_call" | custom-call | flops 11500000256 | bytes 1048576 | tf_op jit(solution)/shard_map/unpack/pallas_call | solution.py:1304
  489.9 0.7 fusion.13
  490.6 0.9 copy.66
  (108 shorter events, 7.7 us)
Async XLA Ops:
  1.7 4.3 copy-start.12
  1.7 4.5 copy-start.13
  1.7 4.7 copy-start.14
  1.7 4.9 %copy-start.15 = (bf16[384]{0:T(512)(128)(2,1)S(1)}, bf16[384]{0:T(512)(128)(2,1)}, u32[]{:S(2)}) copy-start(bf16[384]{0:T(512)(128)(2,1)} %param.31) | copy-start | bytes 2308
  1.7 5.1 %copy-start.16 = (bf16[384]{0:T(512)(128)(2,1)S(1)}, bf16[384]{0:T(512)(128)(2,1)}, u32[]{:S(2)}) copy-start(bf16[384]{0:T(512)(128)(2,1)} %param.32) | copy-start | bytes 2308
  1.7 5.4 %copy-start.17 = (bf16[384]{0:T(512)(128)(2,1)S(1)}, bf16[384]{0:T(512)(128)(2,1)}, u32[]{:S(2)}) copy-start(bf16[384]{0:T(512)(128)(2,1)} %param.36) | copy-start | bytes 2308
  1.7 5.6 %copy-start.18 = (bf16[384]{0:T(512)(128)(2,1)S(1)}, bf16[384]{0:T(512)(128)(2,1)}, u32[]{:S(2)}) copy-start(bf16[384]{0:T(512)(128)(2,1)} %param.37) | copy-start | bytes 2308
  1.7 5.8 %copy-start.19 = (bf16[384]{0:T(512)(128)(2,1)S(1)}, bf16[384]{0:T(512)(128)(2,1)}, u32[]{:S(2)}) copy-start(bf16[384]{0:T(512)(128)(2,1)} %param.38) | copy-start | bytes 2308
  1.8 6.0 %copy-start.10 = (bf16[1536]{0:T(1024)(128)(2,1)S(1)}, bf16[1536]{0:T(1024)(128)(2,1)}, u32[]{:S(2)}) copy-start(bf16[1536]{0:T(1024)(128)(2,1)} %param.34) | copy-start | bytes 9220
  1.8 6.2 %copy-start.11 = (s32[2]{0:T(128)S(1)}, s32[2]{0:T(128)}, u32[]{:S(2)}) copy-start(s32[2]{0:T(128)} %param.22) | copy-start | bytes 28
  1.8 6.7 %copy-start.25 = (s32[32]{0:T(128)S(1)}, s32[32]{0:T(128)}, u32[]{:S(2)}) copy-start(s32[32]{0:T(128)} %param.23) | copy-start | bytes 388
  3.0 22.8 %collective-permute-start.1 = (bf16[576,768]{1,0:T(8,128)(2,1)S(1)}, bf16[576,768]{1,0:T(8,128)(2,1)S(1)}, u32[]{:S(2)}, u32[]{:S(2)}) collective-permute-start(bf16[576,768]{1,0:T(8,128)(2,1)S(1)} %pad_maximum_fusion), channel_id=1, source_target_pairs={{0,1},{1,0},{2,3},{3,2},{4,5},{5,4},{6,7},{7,6},{8,9},{9,8},{10,11... | collective-permute-start | bytes 2654216 | tf_op jit(solution)/shard_map/ppermute | solution.py:1363
  7.8 20.6 %collective-permute-start = (bf16[1,4608]{1,0:T(2,128)(2,1)S(1)}, bf16[1,4608]{1,0:T(2,128)(2,1)S(1)}, u32[]{:S(2)}, u32[]{:S(2)}) collective-permute-start(bf16[1,4608]{1,0:T(2,128)(2,1)S(1)} %broadcast_in_dim.73), channel_id=1, source_target_pairs={{0,1},{1,0},{2,3},{3,2},{4,5},{5,4},{6,7},{7,6},{8,9},{9,8},{10,11... | collective-permute-start | bytes 27656 | tf_op jit(solution)/shard_map/ppermute | solution.py:1363
  25.8 3.9 copy-start.21
  25.8 3.9 collective-permute-start.2
  28.5 1.2 copy-start.6
  28.5 0.6 copy-start.4
  29.7 0.9 copy-start.22
  37.3 5.3 %copy-start.7 = (bf16[384,768]{1,0:T(8,128)(2,1)S(1)}, bf16[384,768]{1,0:T(8,128)(2,1)}, u32[]{:S(2)}) copy-start(bf16[384,768]{1,0:T(8,128)(2,1)} %refs_2_.1) | copy-start | bytes 1769476
  37.3 26.2 %all-to-all-start.3 = ((bf16[4,256,384]{2,1,0:T(8,128)(2,1)}), bf16[4,256,384]{2,1,0:T(8,128)(2,1)}, u32[]{:S(2)}, u32[]{:S(2)}) async-start(bf16[4,256,384]{2,1,0:T(8,128)(2,1)} %get-tuple-element.58), calls=%async_computation.3 | async-start | bytes 1572864 | tf_op jit(solution)/shard_map/all_to_all | solution.py:1371
  42.6 25.7 %collective-permute-start.9 = (bf16[192,768]{1,0:T(8,128)(2,1)S(1)}, bf16[192,768]{1,0:T(8,128)(2,1)}, u32[]{:S(2)}, u32[]{:S(2)}) collective-permute-start(bf16[192,768]{1,0:T(8,128)(2,1)S(1)} %constant_dynamic-slice_fusion.2), channel_id=1, source_target_pairs={{0,1},{1,0},{2,3},{3,2},{4,5},{5,4},{6,7},{7,6},{8,9},{9,8},{10,11... | collective-permute-start | bytes 884744 | tf_op jit(solution)/shard_map/ppermute | solution.py:1363
  63.5 23.4 %all-to-all-start.1 = ((bf16[4,256,384]{2,1,0:T(8,128)(2,1)}), bf16[4,256,384]{2,1,0:T(8,128)(2,1)S(1)}, u32[]{:S(2)}, u32[]{:S(2)}) async-start(bf16[4,256,384]{2,1,0:T(8,128)(2,1)} %get-tuple-element.55), calls=%async_computation.1 | async-start | bytes 1572864 | tf_op jit(solution)/shard_map/all_to_all | solution.py:1371
  67.0 2.9 copy-start.26
  68.3 27.5 %collective-permute-start.11 = (bf16[192,3072]{1,0:T(8,128)(2,1)S(1)}, bf16[192,3072]{1,0:T(8,128)(2,1)}, u32[]{:S(2)}, u32[]{:S(2)}) collective-permute-start(bf16[192,3072]{1,0:T(8,128)(2,1)S(1)} %constant_dynamic-slice_fusion.1), channel_id=1, source_target_pairs={{0,1},{1,0},{2,3},{3,2},{4,5},{5,4},{6,7},{7,6},{8,9},{9,8},{10,11... | collective-permute-start | bytes 3538952 | tf_op jit(solution)/shard_map/ppermute | solution.py:1363
  71.3 30.0 %collective-permute-start.6 = (bf16[8,128,384]{2,1,0:T(8,128)(2,1)}, bf16[8,128,384]{2,1,0:T(8,128)(2,1)}, u32[]{:S(2)}, u32[]{:S(2)}) collective-permute-start(bf16[8,128,384]{2,1,0:T(8,128)(2,1)} %bitcast.12.rest_0_), channel_id=1, source_target_pairs={{0,4},{2,6},{4,0},{6,2},{8,12},{10,14},{12,8},{14,10},{16,20},{18,... | collective-permute-start | bytes 2359304 | tf_op jit(solution)/shard_map/ppermute | solution.py:1366
  86.9 62.2 %copy-start.2 = (bf16[4,256,384]{2,1,0:T(8,128)(2,1)}, bf16[4,256,384]{2,1,0:T(8,128)(2,1)S(1)}, u32[]{:S(2)}) copy-start(bf16[4,256,384]{2,1,0:T(8,128)(2,1)S(1)} %all-to-all-done.1) | copy-start | bytes 2359300
  86.9 21.9 %all-to-all-start.2 = ((bf16[4,256,192]{1,2,0:T(8,128)(2,1)}), bf16[4,256,192]{1,2,0:T(8,128)(2,1)S(1)}, u32[]{:S(2)}, u32[]{:S(2)}) async-start(bf16[4,256,192]{1,2,0:T(8,128)(2,1)} %copy.49), calls=%async_computation.2 | async-start | bytes 786432 | tf_op jit(solution)/shard_map/all_to_all | solution.py:1371
  95.8 17.7 %copy-start.5 = (f32[2,1,3072]{2,0,1:T(2,128)S(1)}, f32[2,1,3072]{2,0,1:T(2,128)}, u32[]{:S(2)}) copy-start(f32[2,1,3072]{2,0,1:T(2,128)} %copy-done.4) | copy-start | bytes 73732
  95.8 30.9 %collective-permute-start.13 = (bf16[768,768]{1,0:T(8,128)(2,1)S(1)}, bf16[768,768]{1,0:T(8,128)(2,1)}, u32[]{:S(2)}, u32[]{:S(2)}) collective-permute-start(bf16[768,768]{1,0:T(8,128)(2,1)S(1)} %constant_dynamic-slice_fusion), channel_id=1, source_target_pairs={{0,1},{1,0},{2,3},{3,2},{4,5},{5,4},{6,7},{7,6},{8,9},{9,8},{10,11... | collective-permute-start | bytes 3538952 | tf_op jit(solution)/shard_map/ppermute | solution.py:1363
  99.7 27.0 %collective-permute-start.7 = (bf16[8,128,384]{2,1,0:T(8,128)(2,1)}, bf16[8,128,384]{2,1,0:T(8,128)(2,1)}, u32[]{:S(2)}, u32[]{:S(2)}) collective-permute-start(bf16[8,128,384]{2,1,0:T(8,128)(2,1)} %bitcast.12.rest_0_), channel_id=1, source_target_pairs={{0,2},{2,0},{4,6},{6,4},{8,10},{10,8},{12,14},{14,12},{16,18},{18,... | collective-permute-start | bytes 2359304 | tf_op jit(solution)/shard_map/ppermute | solution.py:1366
  99.8 27.5 %collective-permute-start.3 = (bf16[8,128,384]{2,1,0:T(8,128)(2,1)S(1)}, bf16[8,128,384]{2,1,0:T(8,128)(2,1)}, u32[]{:S(2)}, u32[]{:S(2)}) collective-permute-start(bf16[8,128,384]{2,1,0:T(8,128)(2,1)S(1)} %bitcast.46), channel_id=1, source_target_pairs={{0,4},{2,6},{4,0},{6,2},{8,12},{10,14},{12,8},{14,10},{16,20},{18,... | collective-permute-start | bytes 2359304 | tf_op jit(solution)/shard_map/ppermute | solution.py:1366
  101.4 25.9 %collective-permute-start.8 = (bf16[8,128,384]{2,1,0:T(8,128)(2,1)}, bf16[8,128,384]{2,1,0:T(8,128)(2,1)}, u32[]{:S(2)}, u32[]{:S(2)}) collective-permute-start(bf16[8,128,384]{2,1,0:T(8,128)(2,1)} %collective-permute-done.6.rest_1_), channel_id=1, source_target_pairs={{0,2},{2,0},{4,6},{6,4},{8,10},{10,8},{12,14},{14,12},{16,18},{18,... | collective-permute-start | bytes 2359304 | tf_op jit(solution)/shard_map/ppermute | solution.py:1366
  108.7 17.0 %all-to-all-start = ((bf16[4,256,192]{1,2,0:T(8,128)(2,1)}), bf16[4,256,192]{1,2,0:T(8,128)(2,1)S(1)}, u32[]{:S(2)}, u32[]{:S(2)}) async-start(bf16[4,256,192]{1,2,0:T(8,128)(2,1)} %copy.47), calls=%async_computation | async-start | bytes 786432 | tf_op jit(solution)/shard_map/all_to_all | solution.py:1371
  115.5 48.2 %collective-permute-start.10 = (bf16[192,768]{1,0:T(8,128)(2,1)}, bf16[192,768]{1,0:T(8,128)(2,1)}, u32[]{:S(2)}, u32[]{:S(2)}) collective-permute-start(bf16[192,768]{1,0:T(8,128)(2,1)} %collective-permute-done.9.refs_3_), channel_id=1, source_target_pairs={{0,2},{2,0},{4,6},{6,4},{8,10},{10,8},{12,14},{14,12},{16,18},{18,... | collective-permute-start | bytes 884744 | tf_op jit(solution)/shard_map/ppermute | solution.py:1366
  126.7 37.0 %collective-permute-start.12 = (bf16[192,3072]{1,0:T(8,128)(2,1)}, bf16[192,3072]{1,0:T(8,128)(2,1)S(1)}, u32[]{:S(2)}, u32[]{:S(2)}) collective-permute-start(bf16[192,3072]{1,0:T(8,128)(2,1)} %collective-permute-done.11.refs_6_), channel_id=1, source_target_pairs={{0,2},{2,0},{4,6},{6,4},{8,10},{10,8},{12,14},{14,12},{16,18},{18,... | collective-permute-start | bytes 3538952 | tf_op jit(solution)/shard_map/ppermute | solution.py:1366
  126.7 22.4 %collective-permute-start.4 = (bf16[8,128,384]{2,1,0:T(8,128)(2,1)S(1)}, bf16[8,128,384]{2,1,0:T(8,128)(2,1)S(1)}, u32[]{:S(2)}, u32[]{:S(2)}) collective-permute-start(bf16[8,128,384]{2,1,0:T(8,128)(2,1)S(1)} %bitcast.47), channel_id=1, source_target_pairs={{0,2},{2,0},{4,6},{6,4},{8,10},{10,8},{12,14},{14,12},{16,18},{18,... | collective-permute-start | bytes 2359304 | tf_op jit(solution)/shard_map/ppermute | solution.py:1366
  127.2 36.5 %collective-permute-start.14 = (bf16[768,768]{1,0:T(8,128)(2,1)}, bf16[768,768]{1,0:T(8,128)(2,1)}, u32[]{:S(2)}, u32[]{:S(2)}) collective-permute-start(bf16[768,768]{1,0:T(8,128)(2,1)} %collective-permute-done.13.refs_9_), channel_id=1, source_target_pairs={{0,2},{2,0},{4,6},{6,4},{8,10},{10,8},{12,14},{14,12},{16,18},{18,... | collective-permute-start | bytes 3538952 | tf_op jit(solution)/shard_map/ppermute | solution.py:1366
  127.3 21.8 %collective-permute-start.5 = (bf16[8,128,384]{2,1,0:T(8,128)(2,1)}, bf16[8,128,384]{2,1,0:T(8,128)(2,1)S(1)}, u32[]{:S(2)}, u32[]{:S(2)}) collective-permute-start(bf16[8,128,384]{2,1,0:T(8,128)(2,1)} %collective-permute-done.3.rest_1_), channel_id=1, source_target_pairs={{0,2},{2,0},{4,6},{6,4},{8,10},{10,8},{12,14},{14,12},{16,18},{18,... | collective-permute-start | bytes 2359304 | tf_op jit(solution)/shard_map/ppermute | solution.py:1366
  149.1 0.9 copy-start.23
  149.1 1.1 copy-start.24
  163.7 1.0 copy-start.20
  386.9 11.5 %copy-start.8 = (f32[8,768]{1,0:T(8,128)S(1)}, f32[8,768]{1,0:T(8,128)}, u32[]{:S(2)}) copy-start(f32[8,768]{1,0:T(8,128)} %get-tuple-element.77) | copy-start | bytes 73732
  387.0 12.1 %copy-start.9 = (f32[1,3072]{1,0:T(1,128)S(1)}, f32[1,3072]{1,0:T(1,128)}, u32[]{:S(2)}) copy-start(f32[1,3072]{1,0:T(1,128)} %get-tuple-element.79) | copy-start | bytes 36868
  387.0 12.8 %copy-start.1 = (bf16[1728,384]{1,0:T(8,128)(2,1)S(1)}, bf16[1728,384]{1,0:T(8,128)(2,1)}, u32[]{:S(2)}) copy-start(bf16[1728,384]{1,0:T(8,128)(2,1)} %get-tuple-element.80.rest_0_) | copy-start | bytes 3981316
  477.5 1.3 copy-start
  481.4 9.2 %copy-start.3 = (bf16[2,256,768]{2,1,0:T(8,128)(2,1)S(1)}, bf16[2,256,768]{2,1,0:T(8,128)(2,1)}, u32[]{:S(2)}) copy-start(bf16[2,256,768]{2,1,0:T(8,128)(2,1)} %get-tuple-element.130) | copy-start | bytes 2359300
